TPU v7x, 512 devices: a whole 4x8x8 slice. The times are simulated.
512 devices in a mesh: vocab: 16 (over y_lo, x, core), dp: 32 (over z, y_hi).
Axes of the slice: x: 4, y: 8 (y_hi: 4, y_lo: 2; y = y_hi * 2 + y_lo), z: 8, core: 2. Of those that a mesh axis runs over, the one named last changes fastest.
Arguments:
- ids: int32 [4096], P('dp'), may hold values from 0 to 65535, as said below
- hidden: bfloat16 [4096, 3584], P('dp', 'vocab'), may hold values from -700 to 700
- table: bfloat16 [3584, 65536], P('dp', 'vocab'), may hold values from -700 to 700
- gain_embed: float32 [3584], P('vocab'), may hold values from 0.1 to 1.9
- gain_hidden: float32 [3584], P('vocab'), may hold values from 0.1 to 1.9
- proj_embed: bfloat16 [3584, 3584], P('vocab', 'dp'), may hold values from -0.125 to 0.125
- proj_hidden: bfloat16 [3584, 3584], P('vocab', 'dp'), may hold values from -0.125 to 0.125
- grad_out: bfloat16 [4096, 3584], P('dp', 'vocab'), may hold values from -6 to 6
Outputs:
- projected: bfloat16 [4096, 3584], P('dp', 'vocab')
- grad_hidden: bfloat16 [4096, 3584], P('dp', 'vocab')
- grad_table: float32 [3584, 65536], P('dp', 'vocab')
- grad_proj_embed: float32 [3584, 3584], P('vocab', 'dp')
- grad_proj_hidden: float32 [3584, 3584], P('vocab', 'dp')
- grad_gains: float32 [2, 3584], P(None, 'vocab')
Inputs may be any that keep to these rules, and one draw needn't show every extreme that they name: Within a block of 128 tokens of one index of dp, any number of tokens, up to all of them, may take ids from one vocabulary shard of 4096 entries; in some block all of them do.
All inputs are finite; a program needn't handle non-finite values.
Results may differ from a plain program's by a relative error of at most 0.022.
Values may be sent and summed in bfloat16 or wider, within the bound.
No kernel may reach another device: no remote copies, remote signals or barrier semaphores. Data moves between devices by JAX's collectives and lax.ppermute only.
A program may use at most 64 MiB of HBM per device.

v0:
```python
import math

import jax
import jax.numpy as jnp
from jax import lax
from jax.sharding import PartitionSpec as P

EPS = 1e-06


def per_device(ids, hidden, table, gain_embed, gain_hidden, proj_embed, proj_hidden, grad_out):
    vocab_index = lax.axis_index("vocab")
    vocab_count = lax.axis_size("vocab")
    tok_rows, feat_width = hidden.shape
    col_width, table_rows = table.shape
    full_width = feat_width * vocab_count
    all_ids = lax.all_gather(ids, "dp", axis=0, tiled=True)
    local_ids = all_ids - vocab_index * table_rows
    token_count = all_ids.shape[0]
    block_rows = math.gcd(token_count, 512)
    row_numbers = jnp.arange(table_rows, dtype=jnp.int32)[None, :]
    contract_last = (((1,), (1,)), ((), ()))

    def lookup(id_block):
        one_hot = (id_block[:, None] == row_numbers).astype(jnp.bfloat16)
        return lax.dot_general(
            one_hot, table, contract_last, preferred_element_type=jnp.float32
        ).astype(jnp.bfloat16)

    pieces = lax.map(lookup, local_ids.reshape(token_count // block_rows, block_rows)).reshape(
        token_count, col_width
    )
    partial_rows = lax.all_to_all(pieces, "dp", split_axis=0, concat_axis=1, tiled=True)
    hidden_f = hidden.astype(jnp.float32)
    hidden_sq = jnp.sum(hidden_f * hidden_f, axis=1)
    whole_rows = lax.psum(partial_rows.astype(jnp.float32).astype(jnp.bfloat16), "vocab").astype(
        jnp.float32
    )
    embed_total = jnp.sum(whole_rows * whole_rows, axis=1)
    embed_f = lax.dynamic_slice_in_dim(whole_rows, vocab_index * feat_width, feat_width, 1)
    hidden_total = lax.psum(hidden_sq, "vocab")
    inv_embed = lax.rsqrt(embed_total / full_width + EPS)[:, None]
    inv_hidden = lax.rsqrt(hidden_total / full_width + EPS)[:, None]
    norm_embed = embed_f * inv_embed
    norm_hidden = hidden_f * inv_hidden
    left = (norm_embed * gain_embed).astype(jnp.bfloat16)
    right = (norm_hidden * gain_hidden).astype(jnp.bfloat16)
    embed_weights, hidden_weights = (
        lax.all_gather(proj_embed, "dp", axis=1, tiled=True),
        lax.all_gather(proj_hidden, "dp", axis=1, tiled=True),
    )
    out_terms = jnp.dot(left, embed_weights, preferred_element_type=jnp.float32) + jnp.dot(
        right, hidden_weights, preferred_element_type=jnp.float32
    )
    projected = lax.psum_scatter(
        out_terms.astype(jnp.bfloat16), "vocab", scatter_dimension=1, tiled=True
    )
    grad_full = lax.all_gather(grad_out, "vocab", axis=1, tiled=True)
    grad_left = lax.dot_general(
        grad_full, embed_weights, contract_last, preferred_element_type=jnp.float32
    )
    grad_right = lax.dot_general(
        grad_full, hidden_weights, contract_last, preferred_element_type=jnp.float32
    )
    normed_rows = jnp.concatenate([left, right], axis=1)
    weight_shares = lax.psum_scatter(
        lax.dot_general(
            grad_full, normed_rows, (((0,), (0,)), ((), ())), preferred_element_type=jnp.float32
        ).astype(jnp.bfloat16),
        "dp",
        scatter_dimension=0,
        tiled=True,
    ).astype(jnp.float32)
    grad_proj_embed = weight_shares[:, :feat_width].T
    grad_proj_hidden = weight_shares[:, feat_width:].T
    gain_left, gain_right = lax.psum(
        (jnp.sum(grad_left * norm_embed, axis=0), jnp.sum(grad_right * norm_hidden, axis=0)), "dp"
    )
    grad_gains = jnp.stack([gain_left, gain_right])
    dn_embed = grad_left * gain_embed
    dn_hidden = grad_right * gain_hidden
    coef_embed, coef_hidden = lax.psum(
        (jnp.sum(dn_embed * norm_embed, axis=1), jnp.sum(dn_hidden * norm_hidden, axis=1)), "vocab"
    )
    grad_embedded = (
        inv_embed * (dn_embed - norm_embed * (coef_embed / full_width)[:, None])
    ).astype(jnp.bfloat16)
    grad_hidden = (
        inv_hidden * (dn_hidden - norm_hidden * (coef_hidden / full_width)[:, None])
    ).astype(jnp.bfloat16)
    embed_grad_full = lax.all_gather(grad_embedded, "vocab", axis=1, tiled=True)
    embed_grad_cols = lax.all_to_all(embed_grad_full, "dp", split_axis=1, concat_axis=0, tiled=True)
    inside = (local_ids >= 0) & (local_ids < table_rows)
    target_cols = jnp.where(inside, local_ids, table_rows)
    grad_table = (
        jnp.zeros((col_width, table_rows), jnp.float32)
        .at[:, target_cols]
        .add(embed_grad_cols.astype(jnp.float32).T, mode="drop")
    )
    return (projected, grad_hidden, grad_table, grad_proj_embed, grad_proj_hidden, grad_gains)


def solution(mesh):
    placed = (
        P("dp"),
        P("dp", "vocab"),
        P("dp", "vocab"),
        P("vocab"),
        P("vocab"),
        P("vocab", "dp"),
        P("vocab", "dp"),
        P("dp", "vocab"),
    )
    return jax.shard_map(
        per_device,
        mesh=mesh,
        in_specs=placed,
        out_specs=(
            P("dp", "vocab"),
            P("dp", "vocab"),
            P("dp", "vocab"),
            P("vocab", "dp"),
            P("vocab", "dp"),
            P(None, "vocab"),
        ),
        check_vma=False,
    )
```

profile of v0, /device:TPU:1, one launch (start us, length us, event | category | flops | bytes accessed | tf_op | source)
XLA Modules:
  0.0 665.1 jit_solution(15059466786413972272)
XLA Ops:
  8.1 74.4 %all-gather = s32[32,1,128]{2,1,0:T(1,128)S(1)} all-gather(s32[1,1,128]{2,1,0:T(1,128)} %bitcast.47), channel_id=1, replica_groups=mesh['vocab'=16,'dp'=32] {'dp'}, dimensions={0}, use_global_device_ids=true | all-gather | bytes 16896 | tf_op jit(solution)/shard_map/all_gather | solution.py:17
  82.4 0.5 broadcast.47
  83.0 0.7 fusion.26
  83.7 24.4 %while.11 = (s32[]{:T(128)}, bf16[8,512,112]{1,2,0:T(8,128)(2,1)S(1)}, s32[8,512]{1,0:T(8,128)S(1)}, bf16[112,4096]{1,0:T(8,128)(2,1)}, s32[]{:T(128)}) while((s32[]{:T(128)}, bf16[8,512,112]{1,2,0:T(8,128)(2,1)S(1)}, s32[8,512]{1,0:T(8,128)S(1)}, bf16[112,4096]{1,0:T(8,128)(2,1)}, s32[]{:T(128)}) %tuple.37), condition=%wide.region_1.2_spmd.clone, body=%wide.region_0.1_spmd.clone.sunk | while | flops 471916544 | bytes 1038413 | solution.py:30
  83.7 3.0 fusion.41
  86.7 3.0 fusion.41
  89.8 3.0 fusion.41
  92.8 3.0 fusion.41
  95.9 3.0 fusion.41
  98.9 3.0 fusion.41
  102.0 3.0 fusion.41
  105.1 3.0 fusion.41
  108.1 0.5 copy.20
  108.6 0.5 all_to_all.24
  109.2 0.4 copy.21
  109.6 22.7 %all_to_all.32 = bf16[32,128,112]{1,2,0:T(8,128)(2,1)} all-to-all(bf16[32,128,112]{1,2,0:T(8,128)(2,1)S(1)} %copy.21), channel_id=1, replica_groups=mesh['vocab'=16,'dp'=32] {'dp'}, dimensions={0} | all-to-all | bytes 1835008 | tf_op jit(solution)/shard_map/all_to_all | solution.py:33
  132.4 0.7 copy.23
  133.1 0.0 all-gather.4.cloned.1.call-start
  133.2 0.7 copy.22
  134.1 42.5 %psum.43 = f32[128]{0:T(128)S(1)} all-reduce(f32[128]{0:T(128)S(1)} %fusion.21), channel_id=1, replica_groups=mesh['vocab'=16,'dp'=32] {'vocab'}, use_global_device_ids=true, to_apply=%region_5.6 | all-reduce | flops 128 | bytes 1024 | tf_op jit(solution)/shard_map/psum | solution.py:41
  176.6 19.9 %all_gather.18 = bf16[128,3584]{0,1:T(8,128)(2,1)S(1)} all-gather(bf16[128,224]{0,1:T(8,128)(2,1)S(1)} %copy-done.7), channel_id=1, replica_groups=mesh['vocab'=16,'dp'=32] {'vocab'}, dimensions={1}, use_global_device_ids=true | all-gather | bytes 974848 | tf_op jit(solution)/shard_map/all_gather | solution.py:58
  196.5 82.4 %all-reduce.4.cloned.1.call-done = bf16[128,3584]{0,1:T(8,128)(2,1)} async-done(((bf16[128,3584]{0,1:T(8,128)(2,1)}), bf16[128,3584]{0,1:T(8,128)(2,1)}) %all-reduce.4.cloned.1.call-update) | async-done | bytes 917520 | tf_op jit(solution)/shard_map/psum | solution.py:36
  278.9 1.4 convert_element_type.43
  280.3 0.1 copy-done.3
  280.4 0.5 multiply_reduce_fusion
  280.9 2.4 fusion.20
  283.3 28.6 %all-gather.4.cloned.1.call-done = bf16[224,3584]{0,1:T(8,128)(2,1)} async-done(((bf16[224,112]{0,1:T(8,128)(2,1)}), bf16[224,3584]{0,1:T(8,128)(2,1)}) %all-gather.4.cloned.1.call-update) | async-done | bytes 1605648 | tf_op jit(solution)/shard_map/all_gather | solution.py:49
  312.0 2.4 multiply_reduce_fusion.1
  314.4 31.5 %all-reduce.1 = (f32[128]{0:T(128)S(1)}, f32[128]{0:T(128)S(1)}) all-reduce(f32[128]{0:T(128)S(1)} %get-tuple-element.65, f32[128]{0:T(128)S(1)} %get-tuple-element.63), channel_id=1, replica_groups=mesh['vocab'=16,'dp'=32] {'vocab'}, use_global_device_ids=true, to_apply=%region_8.9 | all-reduce | flops 256 | bytes 2048 | tf_op jit(solution)/shard_map/psum | solution.py:82
  345.9 0.7 fusion.19
  346.6 0.1 multiply_convert_fusion
  346.7 2.2 fusion.7
  348.9 3.6 copy.26
  352.6 21.4 %all_gather.19 = bf16[128,3584]{0,1:T(8,128)(2,1)} all-gather(bf16[128,224]{0,1:T(8,128)(2,1)S(1)} %get-tuple-element.80), channel_id=1, replica_groups=mesh['vocab'=16,'dp'=32] {'vocab'}, dimensions={1}, use_global_device_ids=true | all-gather | bytes 974848 | tf_op jit(solution)/shard_map/all_gather | solution.py:91
  374.0 8.0 %all-to-all-start.1 = ((bf16[128,32,112]{0,2,1:T(8,128)(2,1)}), bf16[128,32,112]{0,2,1:T(8,128)(2,1)S(1)}, u32[]{:S(2)}, u32[]{:S(2)}) async-start(bf16[128,32,112]{0,2,1:T(8,128)(2,1)} %bitcast.4), calls=%async_computation.2 | async-start | bytes 1835008 | tf_op jit(solution)/shard_map/all_to_all | solution.py:92
  382.1 0.6 fusion.27
  382.7 0.9 copy-done.2
  383.6 1.6 fusion.8
  385.2 79.1 %all-reduce = (f32[1,224]{1,0:T(1,128)S(1)}, f32[1,224]{1,0:T(1,128)S(1)}) all-reduce(f32[1,224]{1,0:T(1,128)S(1)} %bitcast.45, f32[1,224]{1,0:T(1,128)S(1)} %bitcast.46), channel_id=1, replica_groups=mesh['vocab'=16,'dp'=32] {'dp'}, use_global_device_ids=true, to_apply=%region_16.17 | all-reduce | flops 448 | bytes 3584 | tf_op jit(solution)/shard_map/psum | solution.py:76
  464.2 0.6 pad_maximum_fusion
  464.8 0.1 convert_bitcast_fusion
  464.9 1.9 copy.24
  466.8 23.2 %scatter_custom_fusion = f32[112,4096]{0,1:T(8,128)S(1)} fusion(s32[4096]{0:T(1024)S(1)} %compare_select_fusion, f32[4096,112]{1,0:T(8,128)} %bitcast.42, f32[]{:T(128)} %constant.35.clone.1), kind=kCustom, calls=%fused_computation.15 | custom fusion | flops 458752 | bytes 1835520 | tf_op jit(solution)/shard_map/scatter-add | solution.py:98
  490.0 1.8 copy.25
  491.7 97.7 %reduce-scatter.7.cloned.1.call-done = bf16[112,448]{1,0:T(8,128)(2,1)} async-done(((bf16[3584,448]{1,0:T(8,128)(2,1)}), bf16[112,448]{1,0:T(8,128)(2,1)}) %reduce-scatter.7.cloned.1.call-update) | async-done | bytes 100368
  589.4 1.0 copy.27
  590.5 0.7 slice_bitcast_fusion
  591.2 66.3 %reduce-scatter.5.cloned.1.call-done = bf16[128,224]{0,1:T(8,128)(2,1)} async-done(((bf16[128,3584]{0,1:T(8,128)(2,1)}), bf16[128,224]{0,1:T(8,128)(2,1)}) %reduce-scatter.5.cloned.1.call-update) | async-done | bytes 57360 | tf_op jit(solution)/shard_map/reduce_scatter | solution.py:55
  (45 shorter events, 0.5 us)
Async XLA Ops:
  8.0 270.9 %all-reduce.4.cloned.1.call-start = ((), (), s32[]{:S(2)}) async-start(), calls=%async_computation.4 | async-start | bytes 1835008 | tf_op jit(solution)/shard_map/psum | solution.py:36
  109.5 22.8 %copy-start.5 = (bf16[224,112]{1,0:T(8,128)(2,1)S(1)}, bf16[224,112]{1,0:T(8,128)(2,1)}, u32[]{:S(2)}) copy-start(bf16[224,112]{1,0:T(8,128)(2,1)} %param.16) | copy-start | bytes 150532
  109.5 23.6 %copy-start.6 = (bf16[224,112]{1,0:T(8,128)(2,1)S(1)}, bf16[224,112]{1,0:T(8,128)(2,1)}, u32[]{:S(2)}) copy-start(bf16[224,112]{1,0:T(8,128)(2,1)} %param.15) | copy-start | bytes 150532
  109.5 24.5 %copy-start.4 = (bf16[128,224]{0,1:T(8,128)(2,1)S(1)}, bf16[128,224]{0,1:T(8,128)(2,1)}, u32[]{:S(2)}) copy-start(bf16[128,224]{0,1:T(8,128)(2,1)} %param.11) | copy-start | bytes 172036
  109.6 67.0 %copy-start.7 = (bf16[128,224]{0,1:T(8,128)(2,1)S(1)}, bf16[128,224]{0,1:T(8,128)(2,1)}, u32[]{:S(2)}) copy-start(bf16[128,224]{0,1:T(8,128)(2,1)} %param.17) | copy-start | bytes 172036
  132.3 148.6 %all-gather.6.cloned.1.call-start = ((), (), s32[]{:S(2)}) async-start(), calls=%async_computation.6 | async-start | bytes 1892352 | tf_op jit(solution)/shard_map/all_gather | solution.py:50
  133.1 178.9 %all-gather.4.cloned.1.call-start = ((), (), s32[]{:S(2)}) async-start(), calls=%async_computation.5 | async-start | bytes 1892352 | tf_op jit(solution)/shard_map/all_gather | solution.py:49
  133.9 455.5 %reduce-scatter.7.cloned.1.call-start = ((), (), s32[]{:S(2)}) async-start(), calls=%async_computation.8 | async-start | bytes 3784704
  196.5 115.4 %copy-start = (bf16[128,3584]{0,1:T(8,128)(2,1)}, bf16[128,3584]{0,1:T(8,128)(2,1)S(1)}, u32[]{:S(2)}) copy-start(bf16[128,3584]{0,1:T(8,128)(2,1)S(1)} %all_gather.18) | copy-start | bytes 2752516
  196.5 84.4 %copy-start.8 = (f32[224]{0:T(256)S(1)}, f32[224]{0:T(256)}, u32[]{:S(2)}) copy-start(f32[224]{0:T(256)} %param.14) | copy-start | bytes 2692
  278.9 1.5 copy-start.3
  280.4 31.6 %copy-start.9 = (f32[224]{0:T(256)S(1)}, f32[224]{0:T(256)}, u32[]{:S(2)}) copy-start(f32[224]{0:T(256)} %param.13) | copy-start | bytes 2692
  352.6 29.5 %copy-start.1 = (bf16[224,3584]{0,1:T(8,128)(2,1)S(1)}, bf16[224,3584]{0,1:T(8,128)(2,1)}, u32[]{:S(2)}) copy-start(bf16[224,3584]{0,1:T(8,128)(2,1)} %all-gather.4.cloned.1.call-done) | copy-start | bytes 4816900
  374.0 90.8 %all-to-all-start.1 = ((bf16[128,32,112]{0,2,1:T(8,128)(2,1)}), bf16[128,32,112]{0,2,1:T(8,128)(2,1)S(1)}, u32[]{:S(2)}, u32[]{:S(2)}) async-start(bf16[128,32,112]{0,2,1:T(8,128)(2,1)} %bitcast.4), calls=%async_computation.2 | async-start | bytes 1835008 | tf_op jit(solution)/shard_map/all_to_all | solution.py:92
  382.0 275.5 %reduce-scatter.5.cloned.1.call-start = ((), (), s32[]{:S(2)}) async-start(), calls=%async_computation.7 | async-start | bytes 974848 | tf_op jit(solution)/shard_map/reduce_scatter | solution.py:55
  382.0 1.5 copy-start.2
Sparse Core Ops, SparseCore 0:
  132.4 146.4 all-reduce.3
Sparse Core Ops, SparseCore 1:
  136.5 89.6 all-gather.5
  229.8 82.1 all-gather.3
  352.6 236.7 reduce-scatter.6
  592.8 64.6 reduce-scatter.4
where the time goes:
time: 667 us; the launch traced here: 665 us
  blocking collectives  292 us (44%)
  waiting for transfers between devices  275 us (41%)
  matrix products  33.4 us (5%)
  other arithmetic  27.3 us (4%)
  between operations  15.9 us (2%)
  local copies, waits for them, and re-layouts  13.4 us (2%)
  starting transfers between devices  8.19 us (1%)
    unnamed x6, waiting for transfers between devices  97.8 us
    psum x1, waiting for transfers between devices, per_device(): lax.psum(partial_rows.astype(jnp.float32).astype(jnp.bfloat16), 'vocab')  82.4 us
    psum x1, blocking collectives, per_device(): lax.psum((jnp.sum(grad_left * norm_embed, axis=0), jnp.sum(grad_right * n...  79.1 us
    all_gather x1, blocking collectives, per_device(): all_ids = lax.all_gather(ids, 'dp', axis=0, tiled=True)  74.4 us
    reduce_scatter x1, waiting for transfers between devices, per_device(): lax.psum_scatter(out_terms.astype(jnp.bfloat16), 'vocab', scatter_dimensi...  66.3 us
    psum x1, blocking collectives, per_device(): hidden_total = lax.psum(hidden_sq, 'vocab')  42.5 us
    psum x1, blocking collectives, per_device(): lax.psum((jnp.sum(dn_embed * norm_embed, axis=1), jnp.sum(dn_hidden * nor...  31.5 us
    all_gather x1, waiting for transfers between devices, per_device(): lax.all_gather(proj_embed, 'dp', axis=1, tiled=True)  28.6 us
  transfers between devices with their start and end apart: 6, of which 4 were waited for; matrix products, arithmetic and copies ran while one was open for 6% of the time, Pallas kernels for 0%

commit v1 on v0

v1 whole, which is shorter than its diff:
```python
import jax
import jax.numpy as jnp
from jax import lax
from jax.experimental import pallas as pl
from jax.sharding import Mesh
from jax.sharding import PartitionSpec as P

EPS = 1e-06
GROUPS = 8
BF16 = jnp.bfloat16
F32 = jnp.float32
DP = ("z", "yhi")
ALL = ("vocab", "z", "yhi")


def gather(x, axes, count):
    return lax.all_to_all(
        jnp.broadcast_to(x[None], (count,) + x.shape), axes, 0, 0, tiled=True
    )


def one_hot_of(ids, width):
    rows = lax.broadcasted_iota(jnp.int32, (width, ids.shape[1]), 0)
    return jnp.where(rows == ids % width, 1.0, 0.0).astype(BF16)


def lookup_kernel(ids_ref, table_ref, out_ref):
    ids = ids_ref[0]
    width = table_ref.shape[1] // GROUPS
    one_hot = one_hot_of(ids, width)
    group = lax.div(jnp.where(ids < 0, -width, ids), width)
    total = jnp.zeros(out_ref.shape[1:], F32)
    for k in range(GROUPS):
        picked = jnp.dot(
            table_ref[:, k * width : (k + 1) * width], one_hot, preferred_element_type=F32
        )
        total = jnp.where(group == k, picked, total)
    out_ref[0] = total.astype(BF16)


def lookup(ids, table):
    blocks, _, rows = ids.shape
    cols, entries = table.shape
    return pl.pallas_call(
        lookup_kernel,
        grid=(blocks,),
        in_specs=[
            pl.BlockSpec((1, 1, rows), lambda i: (i, 0, 0)),
            pl.BlockSpec((cols, entries), lambda i: (0, 0)),
        ],
        out_specs=pl.BlockSpec((1, cols, rows), lambda i: (i, 0, 0)),
        out_shape=jax.ShapeDtypeStruct((blocks, cols, rows), BF16),
        cost_estimate=pl.CostEstimate(
            flops=2 * blocks * rows * cols * entries,
            bytes_accessed=2 * cols * (entries + blocks * rows),
            transcendentals=0,
        ),
    )(ids, table)


def scatter_kernel(ids_ref, rows_ref, out_ref):
    ids = ids_ref[0]
    width = out_ref.shape[1] // GROUPS
    one_hot = one_hot_of(ids, width)
    group = lax.div(jnp.where(ids < 0, -width, ids), width)
    values = rows_ref[0]

    @pl.when(pl.program_id(0) == 0)
    def _():
        out_ref[...] = jnp.zeros_like(out_ref)

    for k in range(GROUPS):
        inside = jnp.where(group == k, 1.0, 0.0).astype(BF16)
        out_ref[:, k * width : (k + 1) * width] += lax.dot_general(
            values * inside, one_hot, (((1,), (1,)), ((), ())), preferred_element_type=F32
        )


def scatter(ids, values, entries):
    blocks, cols, rows = values.shape
    return pl.pallas_call(
        scatter_kernel,
        grid=(blocks,),
        in_specs=[
            pl.BlockSpec((1, 1, rows), lambda i: (i, 0, 0)),
            pl.BlockSpec((1, cols, rows), lambda i: (i, 0, 0)),
        ],
        out_specs=pl.BlockSpec((cols, entries), lambda i: (0, 0)),
        out_shape=jax.ShapeDtypeStruct((cols, entries), F32),
        cost_estimate=pl.CostEstimate(
            flops=2 * blocks * rows * cols * entries,
            bytes_accessed=cols * (4 * entries + 2 * blocks * rows),
            transcendentals=0,
        ),
    )(ids, values)


def per_device(ids, hidden, table, gain_embed, gain_hidden, proj_embed, proj_hidden, grad_out):
    v = lax.axis_index("vocab")
    nv = lax.axis_size("vocab")
    na, nb = lax.axis_size("z"), lax.axis_size("yhi")
    nd = na * nb
    d = lax.axis_index("z") * nb + lax.axis_index("yhi")
    odd = d % 2 == 1
    toks, fw = hidden.shape
    cw, entries = table.shape
    full = fw * nv

    def swap_route(c):
        return [
            (i * nd + j, (j // 2) * nd + 2 * i + (j % 2 + c) % 2)
            for i in range(nv)
            for j in range(nd)
        ]

    def swap_back(c):
        return [(b, a) for a, b in swap_route(c)]

    turn = [
        (i * nd + a * nb + b, (2 * a + i % 2) * nd + (i // 2) * nb + b)
        for i in range(nv)
        for a in range(na)
        for b in range(nb)
    ]
    turn_back = [(b, a) for a, b in turn]

    all_ids = gather(ids, DP, nd)
    local_ids = (all_ids - v * entries).reshape(nv, 1, 2 * toks)
    weights = jnp.concatenate([proj_embed, proj_hidden], axis=0).T
    weights = gather(weights, "yhi", nb).reshape(nb * cw, 2 * fw)
    cot = gather(lax.ppermute(grad_out.T, ALL, turn), "vocab", nv)
    cot = cot.reshape(na, 2 * fw, toks)

    pieces = lax.all_to_all(lookup(local_ids, table), "vocab", 0, 0, tiled=True)
    cols = jnp.sum(pieces.astype(F32), axis=0).astype(BF16)
    first, second = cols[:, :toks], cols[:, toks:]
    got0 = lax.ppermute(jnp.where(odd, second, first), ALL, swap_route(0))
    got1 = lax.ppermute(jnp.where(odd, first, second), ALL, swap_route(1))
    embed = jnp.concatenate(
        [jnp.where(odd, got1, got0), jnp.where(odd, got0, got1)], axis=0
    ).astype(F32)

    hid = hidden.T.astype(F32)
    gain_e, gain_h = gain_embed[:, None], gain_hidden[:, None]
    hid_total = jnp.sum(gather(jnp.sum(hid * hid, axis=0), "vocab", nv), axis=0)
    inv_hidden = lax.rsqrt(hid_total / full + EPS)[None]
    norm_hidden = hid * inv_hidden
    right = gather((norm_hidden * gain_h).astype(BF16), "z", na)

    shares = jnp.stack(
        [
            lax.dot_general(
                weights, cot[a], (((0,), (0,)), ((), ())), preferred_element_type=F32
            ).astype(BF16)
            for a in range(na)
        ]
    )
    grads = jnp.sum(lax.all_to_all(shares, "z", 0, 0, tiled=True).astype(F32), axis=0)
    grad_left, grad_right = grads[:fw], grads[fw:]
    dn_embed, dn_hidden = grad_left * gain_e, grad_right * gain_h

    stats = jnp.stack(
        [
            jnp.sum(embed * embed, axis=0),
            jnp.sum(dn_embed * embed, axis=0),
            jnp.sum(dn_hidden * norm_hidden, axis=0),
        ]
    )
    stats = jnp.sum(gather(stats, "vocab", nv), axis=0)
    inv_embed = lax.rsqrt(stats[0] / full + EPS)[None]
    norm_embed = embed * inv_embed
    coef_embed = stats[1][None] * inv_embed / full
    coef_hidden = stats[2][None] / full
    grad_embedded = (inv_embed * (dn_embed - norm_embed * coef_embed)).astype(BF16)
    grad_hidden = (inv_hidden * (dn_hidden - norm_hidden * coef_hidden)).astype(BF16)

    low, high = grad_embedded[:cw], grad_embedded[cw:]
    got0 = lax.ppermute(jnp.where(odd, high, low), ALL, swap_back(0))
    got1 = lax.ppermute(jnp.where(odd, low, high), ALL, swap_back(1))
    mine = jnp.concatenate(
        [jnp.where(odd, got1, got0), jnp.where(odd, got0, got1)], axis=1
    )
    grad_table = scatter(local_ids, gather(mine, "vocab", nv), entries)

    left = gather((norm_embed * gain_e).astype(BF16), "z", na)
    both = jnp.concatenate([left, right], axis=1)
    terms = jnp.stack(
        [jnp.dot(weights, both[a], preferred_element_type=F32).astype(BF16) for a in range(na)]
    ).reshape(nv, fw, toks)
    terms = lax.all_to_all(terms, "vocab", 0, 0, tiled=True)
    projected = jnp.sum(terms.astype(F32), axis=0).astype(BF16)
    projected = lax.ppermute(projected, ALL, turn_back).T
    weight_terms = lax.dot_general(
        cot, both, (((0, 2), (0, 2)), ((), ())), preferred_element_type=F32
    ).astype(BF16)
    weight_terms = lax.all_to_all(weight_terms.reshape(nb, cw, 2 * fw), "yhi", 0, 0, tiled=True)
    weight_grads = jnp.sum(weight_terms.astype(F32), axis=0).T

    gains = jnp.concatenate(
        [jnp.sum(grad_left * norm_embed, axis=1), jnp.sum(grad_right * norm_hidden, axis=1)]
    )
    grad_gains = jnp.sum(gather(gains, DP, nd), axis=0).reshape(2, fw)
    return (projected, grad_hidden.T, grad_table, weight_grads[:fw], weight_grads[fw:], grad_gains)


def solution(mesh):
    nv, nd = mesh.shape["vocab"], mesh.shape["dp"]
    nb = min(4, nd)
    split = Mesh(mesh.devices.reshape(nv, nd // nb, nb), ALL)
    rows = P(DP, "vocab")
    return jax.shard_map(
        per_device,
        mesh=split,
        in_specs=(
            P(DP),
            rows,
            rows,
            P("vocab"),
            P("vocab"),
            P("vocab", DP),
            P("vocab", DP),
            rows,
        ),
        out_specs=(rows, rows, rows, P("vocab", DP), P("vocab", DP), P(None, "vocab")),
        check_vma=False,
    )
```

time: 667 us -> 284 us (0.43)
  blocking collectives: 292 us -> 76.2 us
  waiting for transfers between devices: 275 us -> 78.1 us
  starting transfers between devices: 8.19 us -> 70 us
  Pallas kernels: 0 us -> 27.7 us
  other arithmetic: 27.3 us -> 3.21 us
  matrix products: 33.4 us -> 14.6 us
  between operations: 15.9 us -> 1 us
    psum x3 -> x0, blocking collectives: 153 us -> none  [the longest x1 79.1 us: per_device(): lax.psum((jnp.sum(grad_left * norm_embed, axis=0), jnp.sum(grad_right * n...]
    all_gather x3 -> x0, blocking collectives: 116 us -> none  [the longest x1 74.4 us: per_device(): all_ids = lax.all_gather(ids, 'dp', axis=0, tiled=True)]
    unnamed x6 -> x0, waiting for transfers between devices: 97.8 us -> none
    psum x1 -> x0, waiting for transfers between devices: 82.4 us -> none  [per_device(): lax.psum(partial_rows.astype(jnp.float32).astype(jnp.bfloat16), 'vocab')]
    all_to_all x1 -> x9, waiting for transfers between devices: 0.01 us -> 70.3 us  [the longest x5 45 us: gather(): lax.all_to_all(jnp.broadcast_to(x[None], (count,) + x.shape), axes, 0, 0,...]
    reduce_scatter x1 -> x0, waiting for transfers between devices: 66.3 us -> none  [per_device(): lax.psum_scatter(out_terms.astype(jnp.bfloat16), 'vocab', scatter_dimensi...]
    all_to_all x1 -> x4, blocking collectives: 22.7 us -> 76.2 us  [gather(): lax.all_to_all(jnp.broadcast_to(x[None], (count,) + x.shape), axes, 0, 0,...]
    all_to_all x1 -> x9, starting transfers between devices: 7.97 us -> 48.8 us  [the longest x5 27.6 us: gather(): lax.all_to_all(jnp.broadcast_to(x[None], (count,) + x.shape), axes, 0, 0,...]
  transfers between devices with their start and end apart: 6 -> 15, of which waited for: 4 -> 11; matrix products, arithmetic and copies ran while one was open for 6% -> 7% of each run, Pallas kernels for 0% -> 10%
where the time goes in v1:
time: 284 us; the launch traced here: 282 us
  waiting for transfers between devices  78.1 us (27%)
  blocking collectives  76.2 us (27%)
  starting transfers between devices  70 us (25%)
  Pallas kernels  27.7 us (10%)
  matrix products  14.6 us (5%)
  local copies, waits for them, and re-layouts  10.8 us (4%)
  other arithmetic  3.21 us (1%)
    all_to_all x4, blocking collectives, gather(): lax.all_to_all(jnp.broadcast_to(x[None], (count,) + x.shape), axes, 0, 0,...  76.2 us
    all_to_all x5, waiting for transfers between devices, gather(): lax.all_to_all(jnp.broadcast_to(x[None], (count,) + x.shape), axes, 0, 0,...  45 us
    all_to_all x5, starting transfers between devices, gather(): lax.all_to_all(jnp.broadcast_to(x[None], (count,) + x.shape), axes, 0, 0,...  27.6 us
    pallas_call x1, Pallas kernels, scatter(): pl.pallas_call(scatter_kernel, grid=(blocks,), in_specs=[pl.BlockSpec((1,...  16.3 us
    pallas_call x1, Pallas kernels, lookup(): pl.pallas_call(lookup_kernel, grid=(blocks,), in_specs=[pl.BlockSpec((1,...  11.4 us
    all_to_all x1, waiting for transfers between devices, per_device(): lax.all_to_all(shares, 'z', 0, 0, tiled=True).astype(F32)  9.15 us
    all_to_all x1, starting transfers between devices, per_device(): terms = lax.all_to_all(terms, 'vocab', 0, 0, tiled=True)  8.47 us
    all_to_all x1, waiting for transfers between devices, per_device(): pieces = lax.all_to_all(lookup(local_ids, table), 'vocab', 0, 0, tiled=True)  7.61 us
  transfers between devices with their start and end apart: 15, of which 11 were waited for; matrix products, arithmetic and copies ran while one was open for 7% of the time, Pallas kernels for 10%

profile of v1, /device:TPU:1, one launch (start us, length us, event | category | flops | bytes accessed | tf_op | source)
XLA Modules:
  0.0 281.6 jit_solution(1780219753406726595)
XLA Ops:
  0.7 1.6 collective-permute-start.2
  2.3 0.9 fusion.36
  3.1 21.5 %all_to_all.68 = f32[16,1,128]{2,1,0:T(1,128)} all-to-all(f32[16,1,128]{2,1,0:T(1,128)S(1)} %broadcast_in_dim.21), channel_id=1, replica_groups=mesh['vocab'=16,'z'=8,'yhi'=4] {'vocab'}, dimensions={0} | all-to-all | bytes 16384 | tf_op jit(solution)/shard_map/all_to_all | solution.py:17
  25.3 20.5 %all_to_all.69 = s32[32,1,128]{2,1,0:T(1,128)S(1)} all-to-all(s32[32,1,128]{2,1,0:T(1,128)S(1)} %broadcast_in_dim.19), channel_id=1, replica_groups=mesh['vocab'=16,'z'=8,'yhi'=4] {'z','yhi'}, dimensions={0} | all-to-all | bytes 32768 | tf_op jit(solution)/shard_map/all_to_all | solution.py:17
  45.8 1.0 broadcast_in_dim.20
  46.9 5.4 %all-to-all-start.3 = ((bf16[16,224,128]{2,1,0:T(8,128)(2,1)}), bf16[16,224,128]{2,1,0:T(8,128)(2,1)S(1)}, u32[]{:S(2)}, u32[]{:S(2)}) async-start(bf16[16,224,128]{2,1,0:T(8,128)(2,1)} %broadcast_in_dim.20), calls=%async_computation.3 | async-start | bytes 1835008 | tf_op jit(solution)/shard_map/all_to_all | solution.py:17
  53.0 13.7 %all-to-all-done.3 = bf16[16,224,128]{2,1,0:T(8,128)(2,1)S(1)} async-done(((bf16[16,224,128]{2,1,0:T(8,128)(2,1)}), bf16[16,224,128]{2,1,0:T(8,128)(2,1)S(1)}, u32[]{:S(2)}, u32[]{:S(2)}) %all-to-all-start.3) | async-done | bytes 917536 | tf_op jit(solution)/shard_map/all_to_all | solution.py:17
  67.5 3.5 %all-to-all-start = ((bf16[4,112,448]{2,1,0:T(8,128)(2,1)}), bf16[4,112,448]{2,1,0:T(8,128)(2,1)S(1)}, u32[]{:S(2)}, u32[]{:S(2)}) async-start(bf16[4,112,448]{2,1,0:T(8,128)(2,1)} %broadcast_in_dim.18), calls=%async_computation | async-start | bytes 917504 | tf_op jit(solution)/shard_map/all_to_all | solution.py:17
  71.0 11.4 %shard_map.127 = bf16[16,112,256]{2,1,0:T(8,128)(2,1)} custom-call(s32[16,1,256]{2,1,0:T(1,128)} %bitcast.205, bf16[112,4096]{1,0:T(8,128)(2,1)} %table_ref.1), custom_call_target="tpu_custom_call" | custom-call | flops 3758096384 | bytes 1835008 | tf_op jit(solution)/shard_map/pallas_call | solution.py:44
  83.2 0.9 all-to-all-done
  84.1 5.8 %all-to-all-start.2 = ((bf16[16,112,256]{2,1,0:T(8,128)(2,1)}), bf16[16,112,256]{2,1,0:T(8,128)(2,1)S(1)}, u32[]{:S(2)}, u32[]{:S(2)}) async-start(bf16[16,112,256]{2,1,0:T(8,128)(2,1)} %shard_map.127), calls=%async_computation.2 | async-start | bytes 1835008 | tf_op jit(solution)/shard_map/all_to_all | solution.py:134
  89.9 1.3 fusion.2
  91.2 1.3 fusion.4
  92.5 1.3 fusion.6
  95.8 0.9 copy-done
  96.7 7.6 %all-to-all-done.2 = bf16[16,112,256]{2,1,0:T(8,128)(2,1)S(1)} async-done(((bf16[16,112,256]{2,1,0:T(8,128)(2,1)}), bf16[16,112,256]{2,1,0:T(8,128)(2,1)S(1)}, u32[]{:S(2)}, u32[]{:S(2)}) %all-to-all-start.2) | async-done | bytes 917536 | tf_op jit(solution)/shard_map/all_to_all | solution.py:134
  104.3 3.6 %all-to-all-start.4 = ((bf16[8,448,128]{2,1,0:T(8,128)(2,1)}), bf16[8,448,128]{2,1,0:T(8,128)(2,1)S(1)}, u32[]{:S(2)}, u32[]{:S(2)}) async-start(bf16[8,448,128]{2,1,0:T(8,128)(2,1)} %copy-done), calls=%async_computation.4 | async-start | bytes 1835008 | tf_op jit(solution)/shard_map/all_to_all | solution.py:158
  108.0 4.2 %collective-permute-start = (bf16[112,128]{1,0:T(8,128)(2,1)S(1)}, bf16[112,128]{1,0:T(8,128)(2,1)S(1)}, u32[]{:S(2)}, u32[]{:S(2)}) collective-permute-start(bf16[112,128]{1,0:T(8,128)(2,1)S(1)} %get-tuple-element.49), channel_id=1, source_target_pairs={{0,1},{1,0},{2,33},{3,32},{4,65},{5,64},{6,97},{7,96},{8,129},{9,1... | collective-permute-start | bytes 86024 | tf_op jit(solution)/shard_map/ppermute | solution.py:138
  112.2 5.0 %collective-permute-start.1 = (bf16[112,128]{1,0:T(8,128)(2,1)S(1)}, bf16[112,128]{1,0:T(8,128)(2,1)S(1)}, u32[]{:S(2)}, u32[]{:S(2)}) collective-permute-start(bf16[112,128]{1,0:T(8,128)(2,1)S(1)} %get-tuple-element.50), channel_id=1, source_target_pairs={{0,0},{1,1},{2,32},{3,33},{4,64},{5,65},{6,96},{7,97},{8,128},{9,1... | collective-permute-start | bytes 86024 | tf_op jit(solution)/shard_map/ppermute | solution.py:137
  117.3 4.1 %collective-permute-done.1 = bf16[112,128]{1,0:T(8,128)(2,1)S(1)} collective-permute-done((bf16[112,128]{1,0:T(8,128)(2,1)S(1)}, bf16[112,128]{1,0:T(8,128)(2,1)S(1)}, u32[]{:S(2)}, u32[]{:S(2)}) %collective-permute-start.1) | collective-permute-done | bytes 28704 | tf_op jit(solution)/shard_map/ppermute | solution.py:137
  121.4 9.1 %all-to-all-done.4 = bf16[8,448,128]{2,1,0:T(8,128)(2,1)S(1)} async-done(((bf16[8,448,128]{2,1,0:T(8,128)(2,1)}), bf16[8,448,128]{2,1,0:T(8,128)(2,1)S(1)}, u32[]{:S(2)}, u32[]{:S(2)}) %all-to-all-start.4) | async-done | bytes 917536 | tf_op jit(solution)/shard_map/all_to_all | solution.py:158
  131.0 14.0 %all_to_all.70 = f32[16,3,128]{2,1,0:T(4,128)S(1)} all-to-all(f32[16,3,128]{2,1,0:T(4,128)S(1)} %broadcast_in_dim.22), channel_id=1, replica_groups=mesh['vocab'=16,'z'=8,'yhi'=4] {'vocab'}, dimensions={0} | all-to-all | bytes 49152 | tf_op jit(solution)/shard_map/all_to_all | solution.py:17
  145.9 20.1 %all_to_all.71 = bf16[8,224,128]{2,1,0:T(8,128)(2,1)S(1)} all-to-all(bf16[8,224,128]{2,1,0:T(8,128)(2,1)S(1)} %broadcast_in_dim.23), channel_id=1, replica_groups=mesh['vocab'=16,'z'=8,'yhi'=4] {'z'}, dimensions={0} | all-to-all | bytes 917504 | tf_op jit(solution)/shard_map/all_to_all | solution.py:17
  166.9 3.5 %all-to-all-start.8 = ((bf16[8,224,128]{2,1,0:T(8,128)(2,1)}), bf16[8,224,128]{2,1,0:T(8,128)(2,1)S(1)}, u32[]{:S(2)}, u32[]{:S(2)}) async-start(bf16[8,224,128]{2,1,0:T(8,128)(2,1)} %broadcast_in_dim.24), calls=%async_computation.8 | async-start | bytes 917504 | tf_op jit(solution)/shard_map/all_to_all | solution.py:17
  170.5 14.2 %all-to-all-done.8 = bf16[8,224,128]{2,1,0:T(8,128)(2,1)S(1)} async-done(((bf16[8,224,128]{2,1,0:T(8,128)(2,1)}), bf16[8,224,128]{2,1,0:T(8,128)(2,1)S(1)}, u32[]{:S(2)}, u32[]{:S(2)}) %all-to-all-start.8) | async-done | bytes 458784 | tf_op jit(solution)/shard_map/all_to_all | solution.py:17
  185.3 5.9 %all-to-all-start.12 = ((f32[32,1,448]{2,1,0:T(1,128)}), f32[32,1,448]{2,1,0:T(1,128)S(1)}, u32[]{:S(2)}, u32[]{:S(2)}) async-start(f32[32,1,448]{2,1,0:T(1,128)} %broadcast_in_dim.26), calls=%async_computation.12 | async-start | bytes 131072 | tf_op jit(solution)/shard_map/all_to_all | solution.py:17
  191.4 0.9 fusion.18
  192.3 0.9 fusion.20
  193.2 0.9 fusion.22
  194.1 0.9 fusion.24
  195.1 1.4 fusion
  196.5 0.9 fusion.26
  197.4 5.0 %all-to-all-done.12 = f32[32,1,448]{2,1,0:T(1,128)S(1)} async-done(((f32[32,1,448]{2,1,0:T(1,128)}), f32[32,1,448]{2,1,0:T(1,128)S(1)}, u32[]{:S(2)}, u32[]{:S(2)}) %all-to-all-start.12) | async-done | bytes 57376 | tf_op jit(solution)/shard_map/all_to_all | solution.py:17
  202.4 3.5 %all-to-all-start.11 = ((bf16[4,112,448]{2,1,0:T(8,128)(2,1)}), bf16[4,112,448]{2,1,0:T(8,128)(2,1)S(1)}, u32[]{:S(2)}, u32[]{:S(2)}) async-start(bf16[4,112,448]{2,1,0:T(8,128)(2,1)} %bitcast.50), calls=%async_computation.11 | async-start | bytes 917504 | tf_op jit(solution)/shard_map/all_to_all | solution.py:196
  205.9 0.9 fusion.28
  206.8 0.9 fusion.30
  207.7 0.9 fusion.32
  208.6 7.2 %all-to-all-done.11 = bf16[4,112,448]{2,1,0:T(8,128)(2,1)S(1)} async-done(((bf16[4,112,448]{2,1,0:T(8,128)(2,1)}), bf16[4,112,448]{2,1,0:T(8,128)(2,1)S(1)}, u32[]{:S(2)}, u32[]{:S(2)}) %all-to-all-start.11) | async-done | bytes 401440 | tf_op jit(solution)/shard_map/all_to_all | solution.py:196
  215.8 8.5 %all-to-all-start.9 = ((bf16[16,224,128]{2,1,0:T(8,128)(2,1)}), bf16[16,224,128]{2,1,0:T(8,128)(2,1)S(1)}, u32[]{:S(2)}, u32[]{:S(2)}) async-start(bf16[16,224,128]{2,1,0:T(8,128)(2,1)} %bitcast.42), calls=%async_computation.9 | async-start | bytes 1835008 | tf_op jit(solution)/shard_map/all_to_all | solution.py:190
  224.3 3.5 %collective-permute-start.4 = (bf16[112,128]{1,0:T(8,128)(2,1)S(1)}, bf16[112,128]{1,0:T(8,128)(2,1)S(1)}, u32[]{:S(2)}, u32[]{:S(2)}) collective-permute-start(bf16[112,128]{1,0:T(8,128)(2,1)S(1)} %get-tuple-element.45), channel_id=1, source_target_pairs={{1,0},{0,1},{33,2},{32,3},{65,4},{64,5},{97,6},{96,7},{129,8},{128... | collective-permute-start | bytes 86024 | tf_op jit(solution)/shard_map/ppermute | solution.py:179
  227.8 6.1 %collective-permute-start.5 = (bf16[112,128]{1,0:T(8,128)(2,1)S(1)}, bf16[112,128]{1,0:T(8,128)(2,1)S(1)}, u32[]{:S(2)}, u32[]{:S(2)}) collective-permute-start(bf16[112,128]{1,0:T(8,128)(2,1)S(1)} %get-tuple-element.46), channel_id=1, source_target_pairs={{0,0},{1,1},{32,2},{33,3},{64,4},{65,5},{96,6},{97,7},{128,8},{129... | collective-permute-start | bytes 86024 | tf_op jit(solution)/shard_map/ppermute | solution.py:178
  233.9 3.7 %collective-permute-done.4 = bf16[112,128]{1,0:T(8,128)(2,1)S(1)} collective-permute-done((bf16[112,128]{1,0:T(8,128)(2,1)S(1)}, bf16[112,128]{1,0:T(8,128)(2,1)S(1)}, u32[]{:S(2)}, u32[]{:S(2)}) %collective-permute-start.4) | collective-permute-done | bytes 28704 | tf_op jit(solution)/shard_map/ppermute | solution.py:179
  237.7 1.4 all-to-all-done.9
  239.1 1.0 broadcast_in_dim.25
  240.0 9.3 %all-to-all-start.10 = ((bf16[16,112,256]{2,1,0:T(8,128)(2,1)}), bf16[16,112,256]{2,1,0:T(8,128)(2,1)S(1)}, u32[]{:S(2)}, u32[]{:S(2)}) async-start(bf16[16,112,256]{2,1,0:T(8,128)(2,1)} %broadcast_in_dim.25), calls=%async_computation.10 | async-start | bytes 1835008 | tf_op jit(solution)/shard_map/all_to_all | solution.py:17
  252.6 11.2 %all-to-all-done.10.rows_ref = bf16[16,112,256]{2,1,0:T(8,128)(2,1)S(1)} async-done(((bf16[16,112,256]{2,1,0:T(8,128)(2,1)}), bf16[16,112,256]{2,1,0:T(8,128)(2,1)S(1)}, u32[]{:S(2)}, u32[]{:S(2)}) %all-to-all-start.10) | async-done | bytes 917536 | tf_op jit(solution)/shard_map/all_to_all | solution.py:17
  263.8 0.9 copy-done.1
  264.7 16.3 %shard_map.128 = f32[112,4096]{1,0:T(8,128)} custom-call(s32[16,1,256]{2,1,0:T(1,128)} %bitcast.206, bf16[16,112,256]{2,1,0:T(8,128)(2,1)} %copy-done.1), custom_call_target="tpu_custom_call" | custom-call | flops 3758096384 | bytes 2752512 | tf_op jit(solution)/shard_map/pallas_call | solution.py:81
  (64 shorter events, 11.9 us)
Async XLA Ops:
  0.6 51.6 %copy-start.5 = (bf16[224,112]{1,0:T(8,128)(2,1)S(1)}, bf16[224,112]{1,0:T(8,128)(2,1)}, u32[]{:S(2)}) copy-start(bf16[224,112]{1,0:T(8,128)(2,1)} %param.14) | copy-start | bytes 150532
  0.6 51.6 %copy-start.6 = (bf16[224,112]{1,0:T(8,128)(2,1)S(1)}, bf16[224,112]{1,0:T(8,128)(2,1)}, u32[]{:S(2)}) copy-start(bf16[224,112]{1,0:T(8,128)(2,1)} %param.13) | copy-start | bytes 150532
  0.7 45.2 %collective-permute-start.2 = (bf16[224,128]{1,0:T(8,128)(2,1)}, bf16[224,128]{1,0:T(8,128)(2,1)S(1)}, u32[]{:S(2)}, u32[]{:S(2)}) collective-permute-start(bf16[224,128]{1,0:T(8,128)(2,1)} %bitcast.210), channel_id=1, source_target_pairs={{0,0},{1,1},{2,2},{3,3},{4,64},{5,65},{6,66},{7,67},{8,128},{9,129... | collective-permute-start | bytes 172040 | tf_op jit(solution)/shard_map/ppermute | solution.py:131
  46.9 19.8 %all-to-all-start.3 = ((bf16[16,224,128]{2,1,0:T(8,128)(2,1)}), bf16[16,224,128]{2,1,0:T(8,128)(2,1)S(1)}, u32[]{:S(2)}, u32[]{:S(2)}) async-start(bf16[16,224,128]{2,1,0:T(8,128)(2,1)} %broadcast_in_dim.20), calls=%async_computation.3 | async-start | bytes 1835008 | tf_op jit(solution)/shard_map/all_to_all | solution.py:17
  67.5 16.6 %all-to-all-start = ((bf16[4,112,448]{2,1,0:T(8,128)(2,1)}), bf16[4,112,448]{2,1,0:T(8,128)(2,1)S(1)}, u32[]{:S(2)}, u32[]{:S(2)}) async-start(bf16[4,112,448]{2,1,0:T(8,128)(2,1)} %broadcast_in_dim.18), calls=%async_computation | async-start | bytes 917504 | tf_op jit(solution)/shard_map/all_to_all | solution.py:17
  84.1 20.1 %all-to-all-start.2 = ((bf16[16,112,256]{2,1,0:T(8,128)(2,1)}), bf16[16,112,256]{2,1,0:T(8,128)(2,1)S(1)}, u32[]{:S(2)}, u32[]{:S(2)}) async-start(bf16[16,112,256]{2,1,0:T(8,128)(2,1)} %shard_map.127), calls=%async_computation.2 | async-start | bytes 1835008 | tf_op jit(solution)/shard_map/all_to_all | solution.py:134
  89.9 3.9 %copy-start.4 = (bf16[2,224,128]{2,1,0:T(8,128)(2,1)S(1)}, bf16[2,224,128]{2,1,0:T(8,128)(2,1)}, u32[]{:S(2)}) copy-start(bf16[2,224,128]{2,1,0:T(8,128)(2,1)} %get-tuple-element.32) | copy-start | bytes 344068
  89.9 4.3 %copy-start.3 = (bf16[2,224,128]{2,1,0:T(8,128)(2,1)S(1)}, bf16[2,224,128]{2,1,0:T(8,128)(2,1)}, u32[]{:S(2)}) copy-start(bf16[2,224,128]{2,1,0:T(8,128)(2,1)} %get-tuple-element.31) | copy-start | bytes 344068
  95.0 12.9 %copy-start.7 = (f32[16,1,128]{2,1,0:T(1,128)S(1)}, f32[16,1,128]{2,1,0:T(1,128)}, u32[]{:S(2)}) copy-start(f32[16,1,128]{2,1,0:T(1,128)} %all_to_all.68) | copy-start | bytes 24580
  95.7 0.9 copy-start
  96.7 34.0 %copy-start.2 = (bf16[128,224]{0,1:T(8,128)(2,1)S(1)}, bf16[128,224]{0,1:T(8,128)(2,1)}, u32[]{:S(2)}) copy-start(bf16[128,224]{0,1:T(8,128)(2,1)} %param.9) | copy-start | bytes 172036
  96.7 34.1 %copy-start.8 = (f32[224]{0:T(256)S(1)}, f32[224]{0:T(256)}, u32[]{:S(2)}) copy-start(f32[224]{0:T(256)} %param.12) | copy-start | bytes 2692
  96.7 34.1 %copy-start.9 = (f32[224]{0:T(256)S(1)}, f32[224]{0:T(256)}, u32[]{:S(2)}) copy-start(f32[224]{0:T(256)} %param.11) | copy-start | bytes 2692
  104.3 26.3 %all-to-all-start.4 = ((bf16[8,448,128]{2,1,0:T(8,128)(2,1)}), bf16[8,448,128]{2,1,0:T(8,128)(2,1)S(1)}, u32[]{:S(2)}, u32[]{:S(2)}) async-start(bf16[8,448,128]{2,1,0:T(8,128)(2,1)} %copy-done), calls=%async_computation.4 | async-start | bytes 1835008 | tf_op jit(solution)/shard_map/all_to_all | solution.py:158
  108.0 9.3 %collective-permute-start = (bf16[112,128]{1,0:T(8,128)(2,1)S(1)}, bf16[112,128]{1,0:T(8,128)(2,1)S(1)}, u32[]{:S(2)}, u32[]{:S(2)}) collective-permute-start(bf16[112,128]{1,0:T(8,128)(2,1)S(1)} %get-tuple-element.49), channel_id=1, source_target_pairs={{0,1},{1,0},{2,33},{3,32},{4,65},{5,64},{6,97},{7,96},{8,129},{9,1... | collective-permute-start | bytes 86024 | tf_op jit(solution)/shard_map/ppermute | solution.py:138
  112.2 9.2 %collective-permute-start.1 = (bf16[112,128]{1,0:T(8,128)(2,1)S(1)}, bf16[112,128]{1,0:T(8,128)(2,1)S(1)}, u32[]{:S(2)}, u32[]{:S(2)}) collective-permute-start(bf16[112,128]{1,0:T(8,128)(2,1)S(1)} %get-tuple-element.50), channel_id=1, source_target_pairs={{0,0},{1,1},{2,32},{3,33},{4,64},{5,65},{6,96},{7,97},{8,128},{9,1... | collective-permute-start | bytes 86024 | tf_op jit(solution)/shard_map/ppermute | solution.py:137
  166.9 17.8 %all-to-all-start.8 = ((bf16[8,224,128]{2,1,0:T(8,128)(2,1)}), bf16[8,224,128]{2,1,0:T(8,128)(2,1)S(1)}, u32[]{:S(2)}, u32[]{:S(2)}) async-start(bf16[8,224,128]{2,1,0:T(8,128)(2,1)} %broadcast_in_dim.24), calls=%async_computation.8 | async-start | bytes 917504 | tf_op jit(solution)/shard_map/all_to_all | solution.py:17
  185.3 17.0 %all-to-all-start.12 = ((f32[32,1,448]{2,1,0:T(1,128)}), f32[32,1,448]{2,1,0:T(1,128)S(1)}, u32[]{:S(2)}, u32[]{:S(2)}) async-start(f32[32,1,448]{2,1,0:T(1,128)} %broadcast_in_dim.26), calls=%async_computation.12 | async-start | bytes 131072 | tf_op jit(solution)/shard_map/all_to_all | solution.py:17
  202.4 13.4 %all-to-all-start.11 = ((bf16[4,112,448]{2,1,0:T(8,128)(2,1)}), bf16[4,112,448]{2,1,0:T(8,128)(2,1)S(1)}, u32[]{:S(2)}, u32[]{:S(2)}) async-start(bf16[4,112,448]{2,1,0:T(8,128)(2,1)} %bitcast.50), calls=%async_computation.11 | async-start | bytes 917504 | tf_op jit(solution)/shard_map/all_to_all | solution.py:196
  215.8 23.2 %all-to-all-start.9 = ((bf16[16,224,128]{2,1,0:T(8,128)(2,1)}), bf16[16,224,128]{2,1,0:T(8,128)(2,1)S(1)}, u32[]{:S(2)}, u32[]{:S(2)}) async-start(bf16[16,224,128]{2,1,0:T(8,128)(2,1)} %bitcast.42), calls=%async_computation.9 | async-start | bytes 1835008 | tf_op jit(solution)/shard_map/all_to_all | solution.py:190
  224.3 13.4 %collective-permute-start.4 = (bf16[112,128]{1,0:T(8,128)(2,1)S(1)}, bf16[112,128]{1,0:T(8,128)(2,1)S(1)}, u32[]{:S(2)}, u32[]{:S(2)}) collective-permute-start(bf16[112,128]{1,0:T(8,128)(2,1)S(1)} %get-tuple-element.45), channel_id=1, source_target_pairs={{1,0},{0,1},{33,2},{32,3},{65,4},{64,5},{97,6},{96,7},{129,8},{128... | collective-permute-start | bytes 86024 | tf_op jit(solution)/shard_map/ppermute | solution.py:179
  227.8 9.8 %collective-permute-start.5 = (bf16[112,128]{1,0:T(8,128)(2,1)S(1)}, bf16[112,128]{1,0:T(8,128)(2,1)S(1)}, u32[]{:S(2)}, u32[]{:S(2)}) collective-permute-start(bf16[112,128]{1,0:T(8,128)(2,1)S(1)} %get-tuple-element.46), channel_id=1, source_target_pairs={{0,0},{1,1},{32,2},{33,3},{64,4},{65,5},{96,6},{97,7},{128,8},{129... | collective-permute-start | bytes 86024 | tf_op jit(solution)/shard_map/ppermute | solution.py:178
  240.0 23.7 %all-to-all-start.10 = ((bf16[16,112,256]{2,1,0:T(8,128)(2,1)}), bf16[16,112,256]{2,1,0:T(8,128)(2,1)S(1)}, u32[]{:S(2)}, u32[]{:S(2)}) async-start(bf16[16,112,256]{2,1,0:T(8,128)(2,1)} %broadcast_in_dim.25), calls=%async_computation.10 | async-start | bytes 1835008 | tf_op jit(solution)/shard_map/all_to_all | solution.py:17
  251.9 29.1 %collective-permute-start.3 = (bf16[224,128]{1,0:T(8,128)(2,1)S(1)}, bf16[224,128]{1,0:T(8,128)(2,1)S(1)}, u32[]{:S(2)}, u32[]{:S(2)}) collective-permute-start(bf16[224,128]{1,0:T(8,128)(2,1)S(1)} %reduce_sum.131), channel_id=1, source_target_pairs={{0,0},{1,1},{2,2},{3,3},{64,4},{65,5},{66,6},{67,7},{128,8},{129,9... | collective-permute-start | bytes 172040 | tf_op jit(solution)/shard_map/ppermute | solution.py:192
  263.8 0.9 copy-start.1

commit v2 on v1

v2 whole, which is shorter than its diff:
```python
import jax
import jax.numpy as jnp
from jax import lax
from jax.experimental import pallas as pl
from jax.experimental.pallas import tpu as pltpu
from jax.sharding import Mesh
from jax.sharding import PartitionSpec as P

EPS = 1e-06
GROUPS = 8
BF16 = jnp.bfloat16
F32 = jnp.float32
DP = ("z", "yhi")
ALL = ("vocab", "z", "yhi")


def gather(x, axes, count):
    return lax.all_to_all(
        jnp.broadcast_to(x[None], (count,) + x.shape), axes, 0, 0, tiled=True
    )


def one_hot_of(ids, width):
    rows = lax.broadcasted_iota(jnp.int32, (width, ids.shape[1]), 0)
    return jnp.where(rows == ids % width, 1.0, 0.0).astype(BF16)


def group_of(ids, width):
    return lax.div(jnp.where(ids < 0, -width, ids), width)


def lookup_kernel(ids_ref, table_ref, out_ref):
    ids = ids_ref[0]
    width = table_ref.shape[1]
    cols = table_ref.shape[0] // GROUPS
    picked = jnp.dot(
        table_ref[...], one_hot_of(ids, width), preferred_element_type=F32
    )
    group = group_of(ids, width)
    total = jnp.zeros((cols, ids.shape[1]), F32)
    for k in range(GROUPS):
        total = jnp.where(group == k, picked[k * cols : (k + 1) * cols], total)
    out_ref[0] = total.astype(BF16)


def lookup(ids, table):
    blocks, _, rows = ids.shape
    cols, entries = table.shape
    width = entries // GROUPS
    stacked = table.reshape(cols, GROUPS, width).transpose(1, 0, 2).reshape(cols * GROUPS, width)
    return pl.pallas_call(
        lookup_kernel,
        grid=(blocks,),
        in_specs=[
            pl.BlockSpec((1, 1, rows), lambda i: (i, 0, 0)),
            pl.BlockSpec((cols * GROUPS, width), lambda i: (0, 0)),
        ],
        out_specs=pl.BlockSpec((1, cols, rows), lambda i: (i, 0, 0)),
        out_shape=jax.ShapeDtypeStruct((blocks, cols, rows), BF16),
        cost_estimate=pl.CostEstimate(
            flops=2 * blocks * rows * cols * entries,
            bytes_accessed=2 * cols * (entries + blocks * rows),
            transcendentals=0,
        ),
    )(ids, stacked)


def scatter_kernel(ids_ref, rows_ref, out_ref):
    width = out_ref.shape[1] // GROUPS
    cols = out_ref.shape[0]
    parts = ids_ref.shape[0]
    ids = jnp.concatenate([ids_ref[i] for i in range(parts)], axis=1)
    values = jnp.concatenate([rows_ref[i] for i in range(parts)], axis=1)
    group = group_of(ids, width)
    spread = jnp.concatenate(
        [values * jnp.where(group == k, 1.0, 0.0).astype(BF16) for k in range(GROUPS)], axis=0
    )
    sums = lax.dot_general(
        spread, one_hot_of(ids, width), (((1,), (1,)), ((), ())), preferred_element_type=F32
    )

    @pl.when(pl.program_id(0) == 0)
    def _():
        for k in range(GROUPS):
            out_ref[:, k * width : (k + 1) * width] = sums[k * cols : (k + 1) * cols]

    @pl.when(pl.program_id(0) > 0)
    def _():
        for k in range(GROUPS):
            out_ref[:, k * width : (k + 1) * width] += sums[k * cols : (k + 1) * cols]


def scatter(ids, values, entries):
    blocks, cols, rows = values.shape
    parts = 4
    return pl.pallas_call(
        scatter_kernel,
        grid=(blocks // parts,),
        in_specs=[
            pl.BlockSpec((parts, 1, rows), lambda i: (i, 0, 0)),
            pl.BlockSpec((parts, cols, rows), lambda i: (i, 0, 0)),
        ],
        out_specs=pl.BlockSpec((cols, entries), lambda i: (0, 0)),
        out_shape=jax.ShapeDtypeStruct((cols, entries), F32),
        cost_estimate=pl.CostEstimate(
            flops=2 * blocks * rows * cols * entries,
            bytes_accessed=cols * (4 * entries + 2 * blocks * rows),
            transcendentals=0,
        ),
        compiler_params=pltpu.CompilerParams(vmem_limit_bytes=32 * 1024 * 1024),
    )(ids, values)


def grad_kernel(weights_ref, cot_ref, out_ref):
    weights = weights_ref[...].T
    for a in range(cot_ref.shape[0]):
        out_ref[a] = jnp.dot(weights, cot_ref[a], preferred_element_type=F32).astype(BF16)


def grad_products(weights, cot):
    na, outs, toks = cot.shape
    feats = weights.shape[1]
    return pl.pallas_call(
        grad_kernel,
        out_shape=jax.ShapeDtypeStruct((na, feats, toks), BF16),
        cost_estimate=pl.CostEstimate(
            flops=2 * na * outs * feats * toks,
            bytes_accessed=2 * (outs * feats + na * (outs + feats) * toks),
            transcendentals=0,
        ),
        compiler_params=pltpu.CompilerParams(vmem_limit_bytes=16 * 1024 * 1024),
    )(weights, cot)


def out_kernel(weights_ref, cot_ref, normed_ref, out_ref, sums_ref):
    weights = weights_ref[...]
    feats = weights.shape[1]
    for a in range(cot_ref.shape[0]):
        out_ref[a] = jnp.dot(
            weights, normed_ref[a, :feats], preferred_element_type=F32
        ).astype(BF16)
    cot = jnp.concatenate([cot_ref[a] for a in range(cot_ref.shape[0])], axis=1)
    normed = jnp.concatenate([normed_ref[a, :feats] for a in range(cot_ref.shape[0])], axis=1)
    sums_ref[...] = lax.dot_general(
        cot, normed, (((1,), (1,)), ((), ())), preferred_element_type=F32
    ).astype(BF16)


def out_products(weights, cot, normed):
    na, outs, toks = cot.shape
    feats = weights.shape[1]
    return pl.pallas_call(
        out_kernel,
        out_shape=(
            jax.ShapeDtypeStruct((na, outs, toks), BF16),
            jax.ShapeDtypeStruct((outs, feats), BF16),
        ),
        cost_estimate=pl.CostEstimate(
            flops=4 * na * outs * feats * toks,
            bytes_accessed=2 * (2 * outs * feats + na * (2 * outs + feats) * toks),
            transcendentals=0,
        ),
        compiler_params=pltpu.CompilerParams(vmem_limit_bytes=16 * 1024 * 1024),
    )(weights, cot, normed)


def per_device(ids, hidden, table, gain_embed, gain_hidden, proj_embed, proj_hidden, grad_out):
    v = lax.axis_index("vocab")
    nv = lax.axis_size("vocab")
    na, nb = lax.axis_size("z"), lax.axis_size("yhi")
    nd = na * nb
    d = lax.axis_index("z") * nb + lax.axis_index("yhi")
    odd = d % 2 == 1
    toks, fw = hidden.shape
    cw, entries = table.shape
    full = fw * nv

    def swap_route(c):
        return [
            (i * nd + j, (j // 2) * nd + 2 * i + (j % 2 + c) % 2)
            for i in range(nv)
            for j in range(nd)
        ]

    def swap_back(c):
        return [(b, a) for a, b in swap_route(c)]

    def in_order(got0, got1, axis):
        return jnp.concatenate(
            [jnp.where(odd, got1, got0), jnp.where(odd, got0, got1)], axis=axis
        )

    turn = [
        (i * nd + a * nb + b, (2 * a + i % 2) * nd + (i // 2) * nb + b)
        for i in range(nv)
        for a in range(na)
        for b in range(nb)
    ]
    turn_back = [(b, a) for a, b in turn]

    weights = jnp.concatenate([proj_embed, proj_hidden], axis=0).T
    weights = gather(weights, "yhi", nb).reshape(nb * cw, 2 * fw)

    digits = jnp.stack([ids // 256, ids % 256]).astype(BF16)
    digits = in_order(
        lax.ppermute(digits, ALL, swap_route(0)), lax.ppermute(digits, ALL, swap_route(1)), 0
    )
    cot = lax.ppermute(grad_out.T, ALL, turn)
    cot = jnp.concatenate([cot, jnp.pad(digits, ((0, 12), (0, 0)))], axis=0)
    cot = gather(cot, "vocab", nv)
    digits = cot[:, fw : fw + 4].astype(jnp.int32)
    cot = cot[:, :fw].reshape(na, 2 * fw, toks)
    all_ids = 256 * digits[:, 0::2] + digits[:, 1::2]
    local_ids = (all_ids - v * entries).reshape(nv, 1, 2 * toks)

    grads = lax.psum_scatter(
        grad_products(weights, cot).reshape(na * 2 * fw, toks), "z", scatter_dimension=0, tiled=True
    ).astype(F32)

    pieces = lax.all_to_all(lookup(local_ids, table), "vocab", 0, 0, tiled=True)
    cols = jnp.sum(pieces.astype(F32), axis=0).astype(BF16)
    first, second = cols[:, :toks], cols[:, toks:]
    embed = in_order(
        lax.ppermute(jnp.where(odd, second, first), ALL, swap_route(0)),
        lax.ppermute(jnp.where(odd, first, second), ALL, swap_route(1)),
        0,
    ).astype(F32)

    hid = hidden.T.astype(F32)
    gain_e, gain_h = gain_embed[:, None], gain_hidden[:, None]
    grad_left, grad_right = grads[:fw], grads[fw:]
    dn_embed, dn_hidden = grad_left * gain_e, grad_right * gain_h
    stats = jnp.stack(
        [
            jnp.sum(embed * embed, axis=0),
            jnp.sum(hid * hid, axis=0),
            jnp.sum(dn_embed * embed, axis=0),
            jnp.sum(dn_hidden * hid, axis=0),
        ]
    )
    stats = jnp.sum(gather(stats, "vocab", nv), axis=0)
    inv_embed = lax.rsqrt(stats[0] / full + EPS)[None]
    inv_hidden = lax.rsqrt(stats[1] / full + EPS)[None]
    norm_embed, norm_hidden = embed * inv_embed, hid * inv_hidden
    coef_embed = stats[2][None] * inv_embed / full
    coef_hidden = stats[3][None] * inv_hidden / full
    grad_embedded = (inv_embed * (dn_embed - norm_embed * coef_embed)).astype(BF16)
    grad_hidden = (inv_hidden * (dn_hidden - norm_hidden * coef_hidden)).astype(BF16)

    gains = jnp.concatenate(
        [jnp.sum(grad_left * norm_embed, axis=1), jnp.sum(grad_right * norm_hidden, axis=1)]
    )
    gains_high = gains.astype(BF16)
    gains_low = (gains - gains_high.astype(F32)).astype(BF16)
    lines = 2 * fw // toks + 1
    extra = jnp.pad(
        jnp.stack([gains_high, gains_low]), ((0, 0), (0, lines * toks - 2 * fw))
    ).reshape(2 * lines, toks)
    extra = jnp.pad(extra, ((0, -2 * lines % 16), (0, 0)))
    normed = gather(
        jnp.concatenate(
            [(norm_embed * gain_e).astype(BF16), (norm_hidden * gain_h).astype(BF16), extra], axis=0
        ),
        "z",
        na,
    )
    gains = jnp.sum(
        normed[:, 2 * fw : 2 * fw + 2 * lines].reshape(na, 2, lines * toks).astype(F32), axis=(0, 1)
    )[: 2 * fw]

    low, high = grad_embedded[:cw], grad_embedded[cw:]
    mine = in_order(
        lax.ppermute(jnp.where(odd, high, low), ALL, swap_back(0)),
        lax.ppermute(jnp.where(odd, low, high), ALL, swap_back(1)),
        1,
    )
    grad_table = scatter(local_ids, gather(mine, "vocab", nv), entries)

    terms, weight_terms = out_products(weights, cot, normed)
    terms = lax.all_to_all(terms.reshape(nv, fw, toks), "vocab", 0, 0, tiled=True)
    projected = jnp.sum(terms.astype(F32), axis=0).astype(BF16)
    projected = lax.ppermute(projected, ALL, turn_back).T
    gains = jnp.pad(gains.astype(BF16)[None], ((0, 15), (0, 0)))
    weight_terms = jnp.concatenate(
        [
            weight_terms.reshape(nb, cw, 2 * fw),
            jnp.broadcast_to(gains[None], (nb,) + gains.shape),
        ],
        axis=1,
    )
    weight_terms = lax.psum_scatter(
        weight_terms.reshape(nb * (cw + 16), 2 * fw), "yhi", scatter_dimension=0, tiled=True
    ).astype(F32)
    weight_grads = weight_terms[:cw].T
    grad_gains = weight_terms[cw].reshape(2, fw)
    return (projected, grad_hidden.T, grad_table, weight_grads[:fw], weight_grads[fw:], grad_gains)


def solution(mesh):
    nv, nd = mesh.shape["vocab"], mesh.shape["dp"]
    nb = min(4, nd)
    split = Mesh(mesh.devices.reshape(nv, nd // nb, nb), ALL)
    rows = P(DP, "vocab")
    return jax.shard_map(
        per_device,
        mesh=split,
        in_specs=(
            P(DP),
            rows,
            rows,
            P("vocab"),
            P("vocab"),
            P("vocab", DP),
            P("vocab", DP),
            rows,
        ),
        out_specs=(rows, rows, rows, P("vocab", DP), P("vocab", DP), P(None, "vocab")),
        check_vma=False,
    )
```

time: 284 us -> 257 us (0.905)
  the two profiles are of different devices: /device:TPU:1 before, /device:TPU:56 now
where the time goes in v2:
time: 257 us; the launch traced here: 256 us
  waiting for transfers between devices  103 us (40%)
  starting transfers between devices  92.2 us (36%)
  Pallas kernels  21.6 us (8%)
  between operations  14.4 us (6%)
  local copies, waits for them, and re-layouts  9.37 us (4%)
  blocking collectives  8.97 us (3%)
  other arithmetic  5.92 us (2%)
    all_to_all x4, waiting for transfers between devices, gather(): lax.all_to_all(jnp.broadcast_to(x[None], (count,) + x.shape), axes, 0, 0,...  32.6 us
    unnamed x3, waiting for transfers between devices  22.7 us
    all_to_all x4, starting transfers between devices, gather(): lax.all_to_all(jnp.broadcast_to(x[None], (count,) + x.shape), axes, 0, 0,...  19.6 us
    reduce_scatter x1, waiting for transfers between devices, per_device(): lax.psum_scatter(grad_products(weights, cot).reshape(na * 2 * fw, toks),...  13.5 us
    ppermute x1, starting transfers between devices, per_device(): cot = lax.ppermute(grad_out.T, ALL, turn)  12.2 us
    ppermute x1, starting transfers between devices, per_device(): lax.ppermute(digits, ALL, swap_route(0))  11.6 us
    all_to_all x1, waiting for transfers between devices, per_device(): pieces = lax.all_to_all(lookup(local_ids, table), 'vocab', 0, 0, tiled=True)  11.5 us
    pallas_call x1, Pallas kernels, lookup(): pl.pallas_call(lookup_kernel, grid=(blocks,), in_specs=[pl.BlockSpec((1,...  10.8 us
  transfers between devices with their start and end apart: 16, of which 11 were waited for; matrix products, arithmetic and copies ran while one was open for 2% of the time, Pallas kernels for 8%

profile of v2, /device:TPU:56, one launch (start us, length us, event | category | flops | bytes accessed | tf_op | source)
XLA Modules:
  0.0 255.7 jit_solution(1445369517157110377)
XLA Ops:
  7.2 0.7 convert_bitcast_fusion
  8.0 11.6 %collective-permute-start.2 = (bf16[2,128]{1,0:T(2,128)(2,1)S(1)}, bf16[2,128]{1,0:T(2,128)(2,1)S(1)}, u32[]{:S(2)}, u32[]{:S(2)}) collective-permute-start(bf16[2,128]{1,0:T(2,128)(2,1)S(1)} %pad_maximum_fusion.6), channel_id=1, source_target_pairs={{0,0},{1,1},{2,32},{3,33},{4,64},{5,65},{6,96},{7,97},{8,128},{9,1... | collective-permute-start | bytes 1544 | tf_op jit(solution)/shard_map/ppermute | solution.py:206
  19.5 1.9 collective-permute-start.1
  21.5 12.2 %collective-permute-start = (bf16[224,128]{1,0:T(8,128)(2,1)}, bf16[224,128]{1,0:T(8,128)(2,1)S(1)}, u32[]{:S(2)}, u32[]{:S(2)}) collective-permute-start(bf16[224,128]{1,0:T(8,128)(2,1)} %bitcast.88), channel_id=1, source_target_pairs={{0,0},{1,1},{2,2},{3,3},{4,64},{5,65},{6,66},{7,67},{8,128},{9,129... | collective-permute-start | bytes 172040 | tf_op jit(solution)/shard_map/ppermute | solution.py:208
  33.8 3.2 %collective-permute-done = bf16[224,128]{1,0:T(8,128)(2,1)S(1)} collective-permute-done((bf16[224,128]{1,0:T(8,128)(2,1)}, bf16[224,128]{1,0:T(8,128)(2,1)S(1)}, u32[]{:S(2)}, u32[]{:S(2)}) %collective-permute-start) | collective-permute-done | bytes 57376 | tf_op jit(solution)/shard_map/ppermute | solution.py:208
  37.0 1.1 broadcast_in_dim.15
  38.1 6.1 %all-to-all-start.1 = ((bf16[16,240,128]{2,1,0:T(8,128)(2,1)}), bf16[16,240,128]{2,1,0:T(8,128)(2,1)S(1)}, u32[]{:S(2)}, u32[]{:S(2)}) async-start(bf16[16,240,128]{2,1,0:T(8,128)(2,1)} %broadcast_in_dim.15), calls=%async_computation.1 | async-start | bytes 1966080 | tf_op jit(solution)/shard_map/all_to_all | solution.py:18
  44.3 1.0 copy.40
  45.4 13.3 %all-to-all-done.1 = bf16[16,240,128]{2,1,0:T(8,128)(2,1)S(1)} async-done(((bf16[16,240,128]{2,1,0:T(8,128)(2,1)}), bf16[16,240,128]{2,1,0:T(8,128)(2,1)S(1)}, u32[]{:S(2)}, u32[]{:S(2)}) %all-to-all-start.1) | async-done | bytes 983072 | tf_op jit(solution)/shard_map/all_to_all | solution.py:18
  58.7 0.8 broadcast_in_dim.14
  59.5 5.4 %all-to-all-start = ((bf16[4,112,448]{2,1,0:T(8,128)(2,1)}), bf16[4,112,448]{2,1,0:T(8,128)(2,1)S(1)}, u32[]{:S(2)}, u32[]{:S(2)}) async-start(bf16[4,112,448]{2,1,0:T(8,128)(2,1)} %broadcast_in_dim.14), calls=%async_computation | async-start | bytes 917504 | tf_op jit(solution)/shard_map/all_to_all | solution.py:18
  65.0 0.6 add_subtract_fusion
  65.6 10.8 %shard_map.127 = bf16[16,112,256]{2,1,0:T(8,128)(2,1)} custom-call(s32[16,1,256]{2,1,0:T(1,128)} %bitcast.73, bf16[896,512]{1,0:T(8,128)(2,1)} %bitcast.77), custom_call_target="tpu_custom_call" | custom-call | flops 3758096384 | bytes 1835008 | tf_op jit(solution)/shard_map/pallas_call | solution.py:51
  76.3 0.9 all-to-all-done
  77.2 4.1 %all-to-all-start.2 = ((bf16[16,112,256]{2,1,0:T(8,128)(2,1)}), bf16[16,112,256]{2,1,0:T(8,128)(2,1)S(1)}, u32[]{:S(2)}, u32[]{:S(2)}) async-start(bf16[16,112,256]{2,1,0:T(8,128)(2,1)} %shard_map.127), calls=%async_computation.2 | async-start | bytes 1835008 | tf_op jit(solution)/shard_map/all_to_all | solution.py:220
  81.4 2.1 shard_map.128
  83.5 11.5 %all-to-all-done.2 = bf16[16,112,256]{2,1,0:T(8,128)(2,1)S(1)} async-done(((bf16[16,112,256]{2,1,0:T(8,128)(2,1)}), bf16[16,112,256]{2,1,0:T(8,128)(2,1)S(1)}, u32[]{:S(2)}, u32[]{:S(2)}) %all-to-all-start.2) | async-done | bytes 917536 | tf_op jit(solution)/shard_map/all_to_all | solution.py:220
  95.2 9.1 %collective-permute-start.3 = (bf16[112,128]{1,0:T(8,128)(2,1)S(1)}, bf16[112,128]{1,0:T(8,128)(2,1)S(1)}, u32[]{:S(2)}, u32[]{:S(2)}) collective-permute-start(bf16[112,128]{1,0:T(8,128)(2,1)S(1)} %get-tuple-element.28), channel_id=1, source_target_pairs={{0,1},{1,0},{2,33},{3,32},{4,65},{5,64},{6,97},{7,96},{8,129},{9,1... | collective-permute-start | bytes 86024 | tf_op jit(solution)/shard_map/ppermute | solution.py:225
  104.3 5.2 %collective-permute-start.4 = (bf16[112,128]{1,0:T(8,128)(2,1)S(1)}, bf16[112,128]{1,0:T(8,128)(2,1)S(1)}, u32[]{:S(2)}, u32[]{:S(2)}) collective-permute-start(bf16[112,128]{1,0:T(8,128)(2,1)S(1)} %get-tuple-element.29), channel_id=1, source_target_pairs={{0,0},{1,1},{2,32},{3,33},{4,64},{5,65},{6,96},{7,97},{8,128},{9,1... | collective-permute-start | bytes 86024 | tf_op jit(solution)/shard_map/ppermute | solution.py:224
  109.5 8.3 %collective-permute-done.4 = bf16[112,128]{1,0:T(8,128)(2,1)S(1)} collective-permute-done((bf16[112,128]{1,0:T(8,128)(2,1)S(1)}, bf16[112,128]{1,0:T(8,128)(2,1)S(1)}, u32[]{:S(2)}, u32[]{:S(2)}) %collective-permute-start.4) | collective-permute-done | bytes 28704 | tf_op jit(solution)/shard_map/ppermute | solution.py:224
  117.8 13.5 %reduce-scatter.5.cloned.1.call-done = bf16[448,128]{1,0:T(8,128)(2,1)} async-done(((bf16[3584,128]{1,0:T(8,128)(2,1)}), bf16[448,128]{1,0:T(8,128)(2,1)}) %reduce-scatter.5.cloned.1.call-update) | async-done | bytes 114704 | tf_op jit(solution)/shard_map/reduce_scatter | solution.py:216
  131.4 0.9 convert_element_type.86
  132.3 0.1 fusion.11
  132.5 9.0 %all_to_all.35 = f32[16,4,128]{2,1,0:T(4,128)S(1)} all-to-all(f32[16,4,128]{2,1,0:T(4,128)S(1)} %broadcast_in_dim.16), channel_id=1, replica_groups=mesh['vocab'=16,'z'=8,'yhi'=4] {'vocab'}, dimensions={0} | all-to-all | bytes 65536 | tf_op jit(solution)/shard_map/all_to_all | solution.py:18
  141.5 0.8 fusion.6
  142.5 1.1 broadcast_in_dim.17
  143.5 3.6 %all-to-all-start.4 = ((bf16[8,464,128]{2,1,0:T(8,128)(2,1)}), bf16[8,464,128]{2,1,0:T(8,128)(2,1)S(1)}, u32[]{:S(2)}, u32[]{:S(2)}) async-start(bf16[8,464,128]{2,1,0:T(8,128)(2,1)} %broadcast_in_dim.17), calls=%async_computation.5 | async-start | bytes 1900544 | tf_op jit(solution)/shard_map/all_to_all | solution.py:18
  147.1 8.0 %collective-permute-start.6 = (bf16[112,128]{1,0:T(8,128)(2,1)S(1)}, bf16[112,128]{1,0:T(8,128)(2,1)S(1)}, u32[]{:S(2)}, u32[]{:S(2)}) collective-permute-start(bf16[112,128]{1,0:T(8,128)(2,1)S(1)} %get-tuple-element.24), channel_id=1, source_target_pairs={{1,0},{0,1},{33,2},{32,3},{65,4},{64,5},{97,6},{96,7},{129,8},{128... | collective-permute-start | bytes 86024 | tf_op jit(solution)/shard_map/ppermute | solution.py:274
  155.1 5.3 %collective-permute-start.7 = (bf16[112,128]{1,0:T(8,128)(2,1)S(1)}, bf16[112,128]{1,0:T(8,128)(2,1)S(1)}, u32[]{:S(2)}, u32[]{:S(2)}) collective-permute-start(bf16[112,128]{1,0:T(8,128)(2,1)S(1)} %get-tuple-element.25), channel_id=1, source_target_pairs={{0,0},{1,1},{32,2},{33,3},{64,4},{65,5},{96,6},{97,7},{128,8},{129... | collective-permute-start | bytes 86024 | tf_op jit(solution)/shard_map/ppermute | solution.py:273
  160.4 7.7 %collective-permute-done.7 = bf16[112,128]{1,0:T(8,128)(2,1)S(1)} collective-permute-done((bf16[112,128]{1,0:T(8,128)(2,1)S(1)}, bf16[112,128]{1,0:T(8,128)(2,1)S(1)}, u32[]{:S(2)}, u32[]{:S(2)}) %collective-permute-start.7) | collective-permute-done | bytes 28704 | tf_op jit(solution)/shard_map/ppermute | solution.py:273
  168.2 7.7 %all-to-all-done.4.normed_ref = bf16[8,464,128]{2,1,0:T(8,128)(2,1)S(1)} async-done(((bf16[8,464,128]{2,1,0:T(8,128)(2,1)}), bf16[8,464,128]{2,1,0:T(8,128)(2,1)S(1)}, u32[]{:S(2)}, u32[]{:S(2)}) %all-to-all-start.4) | async-done | bytes 950304 | tf_op jit(solution)/shard_map/all_to_all | solution.py:18
  175.9 1.0 broadcast_in_dim.18
  176.9 4.6 %all-to-all-start.6 = ((bf16[16,112,256]{2,1,0:T(8,128)(2,1)}), bf16[16,112,256]{2,1,0:T(8,128)(2,1)S(1)}, u32[]{:S(2)}, u32[]{:S(2)}) async-start(bf16[16,112,256]{2,1,0:T(8,128)(2,1)} %broadcast_in_dim.18), calls=%async_computation.7 | async-start | bytes 1835008 | tf_op jit(solution)/shard_map/all_to_all | solution.py:18
  181.5 2.3 shard_map.129
  183.8 0.8 copy-done
  184.6 10.7 %all-to-all-done.6.rows_ref = bf16[16,112,256]{2,1,0:T(8,128)(2,1)S(1)} async-done(((bf16[16,112,256]{2,1,0:T(8,128)(2,1)}), bf16[16,112,256]{2,1,0:T(8,128)(2,1)S(1)}, u32[]{:S(2)}, u32[]{:S(2)}) %all-to-all-start.6) | async-done | bytes 917536 | tf_op jit(solution)/shard_map/all_to_all | solution.py:18
  195.3 5.7 %all-to-all-start.5 = ((bf16[16,224,128]{2,1,0:T(8,128)(2,1)}), bf16[16,224,128]{2,1,0:T(8,128)(2,1)}, u32[]{:S(2)}, u32[]{:S(2)}) async-start(bf16[16,224,128]{2,1,0:T(8,128)(2,1)} %bitcast.20), calls=%async_computation.6 | async-start | bytes 1835008 | tf_op jit(solution)/shard_map/all_to_all | solution.py:280
  201.2 0.9 pad_maximum_fusion
  202.1 6.5 %shard_map.130 = f32[112,4096]{1,0:T(8,128)} custom-call(s32[16,1,256]{2,1,0:T(1,128)S(1)} %bitcast.74, bf16[16,112,256]{2,1,0:T(8,128)(2,1)S(1)} %all-to-all-done.6.rows_ref), custom_call_target="tpu_custom_call" | custom-call | flops 3758096384 | bytes 2752512 | tf_op jit(solution)/shard_map/pallas_call | solution.py:96
  208.6 22.7 %reduce-scatter.7.cloned.1.call-done = bf16[128,448]{1,0:T(8,128)(2,1)} async-done(((bf16[512,448]{1,0:T(8,128)(2,1)}), bf16[128,448]{1,0:T(8,128)(2,1)}) %reduce-scatter.7.cloned.1.call-update) | async-done | bytes 114704
  231.3 1.0 copy.31
  232.4 0.7 fusion.34
  233.1 1.3 reduce_sum.111
  234.4 9.4 %collective-permute-start.5 = (bf16[224,128]{1,0:T(8,128)(2,1)S(1)}, bf16[224,128]{1,0:T(8,128)(2,1)S(1)}, u32[]{:S(2)}, u32[]{:S(2)}) collective-permute-start(bf16[224,128]{1,0:T(8,128)(2,1)S(1)} %reduce_sum.111), channel_id=1, source_target_pairs={{0,0},{1,1},{2,2},{3,3},{64,4},{65,5},{66,6},{67,7},{128,8},{129,9... | collective-permute-start | bytes 172040 | tf_op jit(solution)/shard_map/ppermute | solution.py:282
  243.8 0.2 slice_reduce_fusion
  244.0 0.7 reshape_squeeze.3
  244.7 3.6 %collective-permute-done.5 = bf16[224,128]{1,0:T(8,128)(2,1)S(1)} collective-permute-done((bf16[224,128]{1,0:T(8,128)(2,1)S(1)}, bf16[224,128]{1,0:T(8,128)(2,1)S(1)}, u32[]{:S(2)}, u32[]{:S(2)}) %collective-permute-start.5) | collective-permute-done | bytes 57376 | tf_op jit(solution)/shard_map/ppermute | solution.py:282
  248.3 0.6 copy.42
  (59 shorter events, 1.0 us)
Async XLA Ops:
  7.2 37.0 %copy-start.5 = (bf16[224,112]{1,0:T(8,128)(2,1)S(1)}, bf16[224,112]{1,0:T(8,128)(2,1)}, u32[]{:S(2)}) copy-start(bf16[224,112]{1,0:T(8,128)(2,1)} %param.14) | copy-start | bytes 150532
  7.2 37.0 %copy-start.6 = (bf16[224,112]{1,0:T(8,128)(2,1)S(1)}, bf16[224,112]{1,0:T(8,128)(2,1)}, u32[]{:S(2)}) copy-start(bf16[224,112]{1,0:T(8,128)(2,1)} %param.13) | copy-start | bytes 150532
  7.2 37.2 %copy-start.3 = (bf16[112,4096]{1,0:T(8,128)(2,1)S(1)}, bf16[112,4096]{1,0:T(8,128)(2,1)}, u32[]{:S(2)}) copy-start(bf16[112,4096]{1,0:T(8,128)(2,1)} %param.10) | copy-start | bytes 2752516
  8.0 25.8 %collective-permute-start.2 = (bf16[2,128]{1,0:T(2,128)(2,1)S(1)}, bf16[2,128]{1,0:T(2,128)(2,1)S(1)}, u32[]{:S(2)}, u32[]{:S(2)}) collective-permute-start(bf16[2,128]{1,0:T(2,128)(2,1)S(1)} %pad_maximum_fusion.6), channel_id=1, source_target_pairs={{0,0},{1,1},{2,32},{3,33},{4,64},{5,65},{6,96},{7,97},{8,128},{9,1... | collective-permute-start | bytes 1544 | tf_op jit(solution)/shard_map/ppermute | solution.py:206
  19.5 14.2 %collective-permute-start.1 = (bf16[2,128]{1,0:T(2,128)(2,1)S(1)}, bf16[2,128]{1,0:T(2,128)(2,1)S(1)}, u32[]{:S(2)}, u32[]{:S(2)}) collective-permute-start(bf16[2,128]{1,0:T(2,128)(2,1)S(1)} %pad_maximum_fusion.6), channel_id=1, source_target_pairs={{0,1},{1,0},{2,33},{3,32},{4,65},{5,64},{6,97},{7,96},{8,129},{9,1... | collective-permute-start | bytes 1544 | tf_op jit(solution)/shard_map/ppermute | solution.py:206
  21.5 15.6 %collective-permute-start = (bf16[224,128]{1,0:T(8,128)(2,1)}, bf16[224,128]{1,0:T(8,128)(2,1)S(1)}, u32[]{:S(2)}, u32[]{:S(2)}) collective-permute-start(bf16[224,128]{1,0:T(8,128)(2,1)} %bitcast.88), channel_id=1, source_target_pairs={{0,0},{1,1},{2,2},{3,3},{4,64},{5,65},{6,66},{7,67},{8,128},{9,129... | collective-permute-start | bytes 172040 | tf_op jit(solution)/shard_map/ppermute | solution.py:208
  38.1 20.6 %all-to-all-start.1 = ((bf16[16,240,128]{2,1,0:T(8,128)(2,1)}), bf16[16,240,128]{2,1,0:T(8,128)(2,1)S(1)}, u32[]{:S(2)}, u32[]{:S(2)}) async-start(bf16[16,240,128]{2,1,0:T(8,128)(2,1)} %broadcast_in_dim.15), calls=%async_computation.1 | async-start | bytes 1966080 | tf_op jit(solution)/shard_map/all_to_all | solution.py:18
  59.5 17.7 %all-to-all-start = ((bf16[4,112,448]{2,1,0:T(8,128)(2,1)}), bf16[4,112,448]{2,1,0:T(8,128)(2,1)S(1)}, u32[]{:S(2)}, u32[]{:S(2)}) async-start(bf16[4,112,448]{2,1,0:T(8,128)(2,1)} %broadcast_in_dim.14), calls=%async_computation | async-start | bytes 917504 | tf_op jit(solution)/shard_map/all_to_all | solution.py:18
  77.2 17.8 %all-to-all-start.2 = ((bf16[16,112,256]{2,1,0:T(8,128)(2,1)}), bf16[16,112,256]{2,1,0:T(8,128)(2,1)S(1)}, u32[]{:S(2)}, u32[]{:S(2)}) async-start(bf16[16,112,256]{2,1,0:T(8,128)(2,1)} %shard_map.127), calls=%async_computation.2 | async-start | bytes 1835008 | tf_op jit(solution)/shard_map/all_to_all | solution.py:220
  81.3 50.1 %reduce-scatter.5.cloned.1.call-start = ((), (), s32[]{:S(2)}) async-start(), calls=%async_computation.9 | async-start | bytes 1032192 | tf_op jit(solution)/shard_map/reduce_scatter | solution.py:216
  81.4 50.9 %copy-start.4 = (bf16[128,224]{0,1:T(8,128)(2,1)S(1)}, bf16[128,224]{0,1:T(8,128)(2,1)}, u32[]{:S(2)}) copy-start(bf16[128,224]{0,1:T(8,128)(2,1)} %param.9) | copy-start | bytes 172036
  81.4 50.9 %copy-start.7 = (f32[224]{0:T(256)S(1)}, f32[224]{0:T(256)}, u32[]{:S(2)}) copy-start(f32[224]{0:T(256)} %param.11) | copy-start | bytes 2692
  81.4 50.9 %copy-start.8 = (f32[224]{0:T(256)S(1)}, f32[224]{0:T(256)}, u32[]{:S(2)}) copy-start(f32[224]{0:T(256)} %param.12) | copy-start | bytes 2692
  95.2 14.3 %collective-permute-start.3 = (bf16[112,128]{1,0:T(8,128)(2,1)S(1)}, bf16[112,128]{1,0:T(8,128)(2,1)S(1)}, u32[]{:S(2)}, u32[]{:S(2)}) collective-permute-start(bf16[112,128]{1,0:T(8,128)(2,1)S(1)} %get-tuple-element.28), channel_id=1, source_target_pairs={{0,1},{1,0},{2,33},{3,32},{4,65},{5,64},{6,97},{7,96},{8,129},{9,1... | collective-permute-start | bytes 86024 | tf_op jit(solution)/shard_map/ppermute | solution.py:225
  104.3 13.5 %collective-permute-start.4 = (bf16[112,128]{1,0:T(8,128)(2,1)S(1)}, bf16[112,128]{1,0:T(8,128)(2,1)S(1)}, u32[]{:S(2)}, u32[]{:S(2)}) collective-permute-start(bf16[112,128]{1,0:T(8,128)(2,1)S(1)} %get-tuple-element.29), channel_id=1, source_target_pairs={{0,0},{1,1},{2,32},{3,33},{4,64},{5,65},{6,96},{7,97},{8,128},{9,1... | collective-permute-start | bytes 86024 | tf_op jit(solution)/shard_map/ppermute | solution.py:224
  143.5 32.4 %all-to-all-start.4 = ((bf16[8,464,128]{2,1,0:T(8,128)(2,1)}), bf16[8,464,128]{2,1,0:T(8,128)(2,1)S(1)}, u32[]{:S(2)}, u32[]{:S(2)}) async-start(bf16[8,464,128]{2,1,0:T(8,128)(2,1)} %broadcast_in_dim.17), calls=%async_computation.5 | async-start | bytes 1900544 | tf_op jit(solution)/shard_map/all_to_all | solution.py:18
  147.1 13.3 %collective-permute-start.6 = (bf16[112,128]{1,0:T(8,128)(2,1)S(1)}, bf16[112,128]{1,0:T(8,128)(2,1)S(1)}, u32[]{:S(2)}, u32[]{:S(2)}) collective-permute-start(bf16[112,128]{1,0:T(8,128)(2,1)S(1)} %get-tuple-element.24), channel_id=1, source_target_pairs={{1,0},{0,1},{33,2},{32,3},{65,4},{64,5},{97,6},{96,7},{129,8},{128... | collective-permute-start | bytes 86024 | tf_op jit(solution)/shard_map/ppermute | solution.py:274
  155.1 13.0 %collective-permute-start.7 = (bf16[112,128]{1,0:T(8,128)(2,1)S(1)}, bf16[112,128]{1,0:T(8,128)(2,1)S(1)}, u32[]{:S(2)}, u32[]{:S(2)}) collective-permute-start(bf16[112,128]{1,0:T(8,128)(2,1)S(1)} %get-tuple-element.25), channel_id=1, source_target_pairs={{0,0},{1,1},{32,2},{33,3},{64,4},{65,5},{96,6},{97,7},{128,8},{129... | collective-permute-start | bytes 86024 | tf_op jit(solution)/shard_map/ppermute | solution.py:273
  176.9 18.4 %all-to-all-start.6 = ((bf16[16,112,256]{2,1,0:T(8,128)(2,1)}), bf16[16,112,256]{2,1,0:T(8,128)(2,1)S(1)}, u32[]{:S(2)}, u32[]{:S(2)}) async-start(bf16[16,112,256]{2,1,0:T(8,128)(2,1)} %broadcast_in_dim.18), calls=%async_computation.7 | async-start | bytes 1835008 | tf_op jit(solution)/shard_map/all_to_all | solution.py:18
  183.8 0.8 copy-start
  184.6 17.5 %copy-start.2 = (s32[16,2,128]{2,1,0:T(2,128)S(1)}, s32[16,2,128]{2,1,0:T(2,128)}, u32[]{:S(2)}) copy-start(s32[16,2,128]{2,1,0:T(2,128)} %add_subtract_fusion) | copy-start | bytes 49156
  195.3 5.8 %copy-start.1 = (bf16[448,448]{1,0:T(8,128)(2,1)S(1)}, bf16[448,448]{1,0:T(8,128)(2,1)}, u32[]{:S(2)}) copy-start(bf16[448,448]{1,0:T(8,128)(2,1)} %copy-done) | copy-start | bytes 1204228
  195.3 37.7 %all-to-all-start.5 = ((bf16[16,224,128]{2,1,0:T(8,128)(2,1)}), bf16[16,224,128]{2,1,0:T(8,128)(2,1)}, u32[]{:S(2)}, u32[]{:S(2)}) async-start(bf16[16,224,128]{2,1,0:T(8,128)(2,1)} %bitcast.20), calls=%async_computation.6 | async-start | bytes 1835008 | tf_op jit(solution)/shard_map/all_to_all | solution.py:280
  201.0 30.2 %reduce-scatter.7.cloned.1.call-start = ((), (), s32[]{:S(2)}) async-start(), calls=%async_computation.10 | async-start | bytes 655360
  234.4 13.9 %collective-permute-start.5 = (bf16[224,128]{1,0:T(8,128)(2,1)S(1)}, bf16[224,128]{1,0:T(8,128)(2,1)S(1)}, u32[]{:S(2)}, u32[]{:S(2)}) collective-permute-start(bf16[224,128]{1,0:T(8,128)(2,1)S(1)} %reduce_sum.111), channel_id=1, source_target_pairs={{0,0},{1,1},{2,2},{3,3},{64,4},{65,5},{66,6},{67,7},{128,8},{129,9... | collective-permute-start | bytes 172040 | tf_op jit(solution)/shard_map/ppermute | solution.py:282
Sparse Core Ops, SparseCore 0:
  85.5 45.7 reduce-scatter.4
  204.9 26.2 reduce-scatter.6

commit v3 on v2

v3 whole, which is shorter than its diff:
```python
import functools

import jax
import jax.numpy as jnp
from jax import lax
from jax.experimental import pallas as pl
from jax.experimental.pallas import tpu as pltpu
from jax.sharding import Mesh
from jax.sharding import PartitionSpec as P

EPS = 1e-06
GROUPS = 8
BF16 = jnp.bfloat16
F32 = jnp.float32
DP = ("z", "yhi")
ALL = ("vocab", "z", "yhi")


def gather(x, axes, count):
    return lax.all_to_all(
        jnp.broadcast_to(x[None], (count,) + x.shape), axes, 0, 0, tiled=True
    )


def one_hot_of(ids, width):
    rows = lax.broadcasted_iota(jnp.int32, (width, ids.shape[1]), 0)
    return jnp.where(rows == ids % width, 1.0, 0.0).astype(BF16)


def group_of(ids, width):
    return lax.div(jnp.where(ids < 0, -width, ids), width)


def lookup_kernel(ids_ref, table_ref, out_ref):
    parts, _, rows = ids_ref.shape
    width = table_ref.shape[1]
    cols = table_ref.shape[0] // GROUPS
    ids = jnp.concatenate([ids_ref[i] for i in range(parts)], axis=1)
    picked = jnp.dot(
        table_ref[...], one_hot_of(ids, width), preferred_element_type=F32
    )
    group = group_of(ids, width)
    total = jnp.zeros((cols, ids.shape[1]), F32)
    for k in range(GROUPS):
        total = jnp.where(group == k, picked[k * cols : (k + 1) * cols], total)
    for i in range(parts):
        out_ref[i] = total[:, i * rows : (i + 1) * rows].astype(BF16)


def lookup(ids, table):
    blocks, _, rows = ids.shape
    cols, entries = table.shape
    width = entries // GROUPS
    parts = 4
    stacked = table.reshape(cols, GROUPS, width).transpose(1, 0, 2).reshape(cols * GROUPS, width)
    return pl.pallas_call(
        lookup_kernel,
        grid=(blocks // parts,),
        in_specs=[
            pl.BlockSpec((parts, 1, rows), lambda i: (i, 0, 0)),
            pl.BlockSpec((cols * GROUPS, width), lambda i: (0, 0)),
        ],
        out_specs=pl.BlockSpec((parts, cols, rows), lambda i: (i, 0, 0)),
        out_shape=jax.ShapeDtypeStruct((blocks, cols, rows), BF16),
        cost_estimate=pl.CostEstimate(
            flops=2 * blocks * rows * cols * entries,
            bytes_accessed=2 * cols * (entries + blocks * rows),
            transcendentals=0,
        ),
        compiler_params=pltpu.CompilerParams(vmem_limit_bytes=32 * 1024 * 1024),
    )(ids, stacked)


def scatter_kernel(ids_ref, rows_ref, out_ref):
    width = out_ref.shape[1] // GROUPS
    cols = out_ref.shape[0]
    parts = ids_ref.shape[0]
    ids = jnp.concatenate([ids_ref[i] for i in range(parts)], axis=1)
    values = jnp.concatenate(
        [rows_ref[i, j * cols : (j + 1) * cols] for i in range(parts) for j in range(2)], axis=1
    )
    group = group_of(ids, width)
    spread = jnp.concatenate(
        [values * jnp.where(group == k, 1.0, 0.0).astype(BF16) for k in range(GROUPS)], axis=0
    )
    sums = lax.dot_general(
        spread, one_hot_of(ids, width), (((1,), (1,)), ((), ())), preferred_element_type=F32
    )

    @pl.when(pl.program_id(0) == 0)
    def _():
        for k in range(GROUPS):
            out_ref[:, k * width : (k + 1) * width] = sums[k * cols : (k + 1) * cols]

    @pl.when(pl.program_id(0) > 0)
    def _():
        for k in range(GROUPS):
            out_ref[:, k * width : (k + 1) * width] += sums[k * cols : (k + 1) * cols]


def scatter(ids, values, entries):
    blocks, rows, toks = values.shape
    cols = rows // 4
    parts = 4
    return pl.pallas_call(
        scatter_kernel,
        grid=(blocks // parts,),
        in_specs=[
            pl.BlockSpec((parts, 1, 2 * toks), lambda i: (i, 0, 0)),
            pl.BlockSpec((parts, 2 * cols, toks), lambda i: (i, 1, 0)),
        ],
        out_specs=pl.BlockSpec((cols, entries), lambda i: (0, 0)),
        out_shape=jax.ShapeDtypeStruct((cols, entries), F32),
        cost_estimate=pl.CostEstimate(
            flops=4 * blocks * toks * cols * entries,
            bytes_accessed=cols * (4 * entries + 4 * blocks * toks),
            transcendentals=0,
        ),
        compiler_params=pltpu.CompilerParams(vmem_limit_bytes=32 * 1024 * 1024),
    )(ids, values)


def cot_columns(cot_ref, b, cw):
    half = b % 2 * cw
    return jnp.concatenate(
        [cot_ref[i, half : half + cw] for i in range(b // 2, cot_ref.shape[0], 2)], axis=0
    )


def grad_kernel(cw, weights_ref, cot_ref, out_ref):
    nb, feats, _ = out_ref.shape
    weights = jnp.concatenate(
        [weights_ref[a, :cw, :feats] for a in range(weights_ref.shape[0])], axis=0
    ).T
    for b in range(nb):
        out_ref[b] = jnp.dot(
            weights, cot_columns(cot_ref, b, cw), preferred_element_type=F32
        ).astype(BF16)


def grad_products(weights, cot, nb, cw, feats):
    na, toks = weights.shape[0], cot.shape[2]
    return pl.pallas_call(
        functools.partial(grad_kernel, cw),
        out_shape=jax.ShapeDtypeStruct((nb, feats, toks), BF16),
        cost_estimate=pl.CostEstimate(
            flops=2 * na * cw * feats * nb * toks,
            bytes_accessed=2 * (weights.size + cot.size + nb * feats * toks),
            transcendentals=0,
        ),
        compiler_params=pltpu.CompilerParams(vmem_limit_bytes=16 * 1024 * 1024),
    )(weights, cot)


def out_kernel(cw, feats, weights_ref, cot_ref, normed_ref, mine_ref, out_ref, sums_ref):
    na, nb = weights_ref.shape[0], normed_ref.shape[0]
    toks = normed_ref.shape[2]
    weights = jnp.concatenate([weights_ref[a, :cw, :feats] for a in range(na)], axis=0)
    for b in range(nb):
        terms = jnp.dot(weights, normed_ref[b, :feats], preferred_element_type=F32).astype(BF16)
        for a in range(na):
            half = b % 2 * cw
            out_ref[2 * a + b // 2, half : half + cw] = terms[a * cw : (a + 1) * cw]
    mine = mine_ref[...]
    for i in range(out_ref.shape[0]):
        out_ref[i, 2 * cw :] = mine
    cot = jnp.concatenate([cot_columns(cot_ref, b, cw) for b in range(nb)], axis=1)
    normed = jnp.concatenate([normed_ref[b, :feats] for b in range(nb)], axis=1)
    sums = lax.dot_general(
        cot, normed, (((1,), (1,)), ((), ())), preferred_element_type=F32
    ).astype(BF16)
    gains = jnp.zeros((16, toks), F32)
    for b in range(nb):
        gains += normed_ref[b, feats : feats + 16].astype(F32)
        gains += normed_ref[b, feats + 16 : feats + 32].astype(F32)
    for a in range(na):
        sums_ref[a, :cw] = sums[a * cw : (a + 1) * cw]
        sums_ref[a, cw:] = jnp.zeros((16, feats), BF16)
        sums_ref[a, cw:, :toks] = gains.astype(BF16)


def out_products(weights, cot, normed, mine, cw, feats):
    na, (nb, _, toks) = weights.shape[0], normed.shape
    return pl.pallas_call(
        functools.partial(out_kernel, cw, feats),
        out_shape=(
            jax.ShapeDtypeStruct((2 * na, 4 * cw, toks), BF16),
            jax.ShapeDtypeStruct((na, cw + 16, feats), BF16),
        ),
        cost_estimate=pl.CostEstimate(
            flops=4 * na * cw * feats * nb * toks,
            bytes_accessed=2 * (weights.size + 2 * cot.size + normed.size + na * cw * feats),
            transcendentals=0,
        ),
        compiler_params=pltpu.CompilerParams(vmem_limit_bytes=32 * 1024 * 1024),
    )(weights, cot, normed, mine)


def finish_kernel(cw, fw, lines, sums_ref, done_ref, embed_ref, hidden_ref, gains_ref):
    toks = done_ref.shape[1]
    sums = sums_ref[...].astype(F32)
    turned = sums.T
    embed_ref[...] = turned[:fw, :cw]
    hidden_ref[...] = turned[fw:, :cw]
    gains = jnp.concatenate(
        [sums[cw + i : cw + i + 1, :toks] for i in range(lines)], axis=1
    )
    gains_ref[0:1, :] = gains[:, :fw]
    gains_ref[1:2, :] = gains[:, fw : 2 * fw]


def finish(sums, done, cw, fw, lines):
    return pl.pallas_call(
        functools.partial(finish_kernel, cw, fw, lines),
        out_shape=(
            jax.ShapeDtypeStruct((fw, cw), F32),
            jax.ShapeDtypeStruct((fw, cw), F32),
            jax.ShapeDtypeStruct((2, fw), F32),
        ),
        cost_estimate=pl.CostEstimate(
            flops=0, bytes_accessed=2 * sums.size + 8 * fw * cw, transcendentals=0
        ),
    )(sums, done)


def per_device(ids, hidden, table, gain_embed, gain_hidden, proj_embed, proj_hidden, grad_out):
    v = lax.axis_index("vocab")
    nv = lax.axis_size("vocab")
    na, nb = lax.axis_size("z"), lax.axis_size("yhi")
    nd = na * nb
    d = lax.axis_index("z") * nb + lax.axis_index("yhi")
    odd = d % 2 == 1
    toks, fw = hidden.shape
    cw, entries = table.shape
    full = fw * nv

    def swap_route(c):
        return [
            (i * nd + j, (j // 2) * nd + 2 * i + (j % 2 + c) % 2)
            for i in range(nv)
            for j in range(nd)
        ]

    def swap_back(c):
        return [(b, a) for a, b in swap_route(c)]

    def in_order(got0, got1, axis):
        return jnp.concatenate(
            [jnp.where(odd, got1, got0), jnp.where(odd, got0, got1)], axis=axis
        )

    def turn(c):
        return [
            (
                (2 * a2 + b1) * nd + a * nb + 2 * core + x,
                (2 * a2 + core) * nd + a * nb + 2 * b1 + (x + c) % 2,
            )
            for a2 in range(na)
            for b1 in range(2)
            for a in range(na)
            for core in range(2)
            for x in range(2)
        ]

    def turn_back(c):
        return [(b, a) for a, b in turn(c)]

    weights = jnp.concatenate([proj_embed, proj_hidden], axis=0).T
    weights = jnp.pad(weights, ((0, -cw % 128), (0, -2 * fw % 512)))
    weights = lax.all_gather(weights, "z")

    digits = jnp.stack([ids // 256, ids % 256]).astype(BF16)
    digits = in_order(
        lax.ppermute(digits, ALL, swap_route(0)), lax.ppermute(digits, ALL, swap_route(1)), 0
    )
    first, second = grad_out.T[:cw], grad_out.T[cw:]
    cot = in_order(
        lax.ppermute(jnp.where(odd, second, first), ALL, turn(0)),
        lax.ppermute(jnp.where(odd, first, second), ALL, turn(1)),
        0,
    )
    cot = lax.all_gather(
        jnp.concatenate([cot, jnp.pad(digits, ((0, 12), (0, 0)))], axis=0), "vocab"
    )
    digits = cot[:, fw : fw + 4].astype(jnp.int32)
    all_ids = 256 * digits[:, 0::2] + digits[:, 1::2]
    local_ids = (all_ids - v * entries).reshape(nv, 1, 2 * toks)

    shares = grad_products(weights, cot, nb, cw, 2 * fw)
    pieces, shares = lax.optimization_barrier((lookup(local_ids, table), shares))
    grads = lax.psum_scatter(
        shares.reshape(nb * 2 * fw, toks), "yhi", scatter_dimension=0, tiled=True
    ).astype(F32)
    pieces = lax.all_to_all(pieces, "vocab", 0, 0, tiled=True)
    cols = jnp.sum(pieces.astype(F32), axis=0).astype(BF16)
    first, second = cols[:, :toks], cols[:, toks:]
    embed = in_order(
        lax.ppermute(jnp.where(odd, second, first), ALL, swap_route(0)),
        lax.ppermute(jnp.where(odd, first, second), ALL, swap_route(1)),
        0,
    ).astype(F32)

    hid = hidden.T.astype(F32)
    gain_e, gain_h = gain_embed[:, None], gain_hidden[:, None]
    grad_left, grad_right = grads[:fw], grads[fw:]
    dn_embed, dn_hidden = grad_left * gain_e, grad_right * gain_h
    stats = jnp.stack(
        [
            jnp.sum(embed * embed, axis=0),
            jnp.sum(hid * hid, axis=0),
            jnp.sum(dn_embed * embed, axis=0),
            jnp.sum(dn_hidden * hid, axis=0),
        ]
    )
    stats = jnp.sum(gather(stats, "vocab", nv), axis=0)
    inv_embed = lax.rsqrt(stats[0] / full + EPS)[None]
    inv_hidden = lax.rsqrt(stats[1] / full + EPS)[None]
    norm_embed, norm_hidden = embed * inv_embed, hid * inv_hidden
    coef_embed = stats[2][None] * inv_embed / full
    coef_hidden = stats[3][None] * inv_hidden / full
    grad_embedded = (inv_embed * (dn_embed - norm_embed * coef_embed)).astype(BF16)
    grad_hidden = (inv_hidden * (dn_hidden - norm_hidden * coef_hidden)).astype(BF16)

    gains = jnp.concatenate(
        [jnp.sum(grad_left * norm_embed, axis=1), jnp.sum(grad_right * norm_hidden, axis=1)]
    )
    lines = -(-2 * fw // toks)
    gains = jnp.pad(gains, (0, lines * toks - 2 * fw)).reshape(lines, toks)
    gains = jnp.pad(gains, ((0, 16 - lines), (0, 0)))
    gains_high = gains.astype(BF16)
    gains_low = (gains - gains_high.astype(F32)).astype(BF16)
    normed = gather(
        jnp.concatenate(
            [
                (norm_embed * gain_e).astype(BF16),
                (norm_hidden * gain_h).astype(BF16),
                gains_high,
                gains_low,
            ],
            axis=0,
        ),
        "yhi",
        nb,
    )

    low, high = grad_embedded[:cw], grad_embedded[cw:]
    mine = in_order(
        lax.ppermute(jnp.where(odd, high, low), ALL, swap_back(0)),
        lax.ppermute(jnp.where(odd, low, high), ALL, swap_back(1)),
        0,
    )

    terms, weight_terms = out_products(weights, cot, normed, mine, cw, 2 * fw)
    terms = lax.all_to_all(terms, "vocab", 0, 0, tiled=True)
    grad_table = scatter(local_ids, terms, entries)

    terms = jnp.sum(terms[:, :fw].astype(F32), axis=0).astype(BF16)
    first, second = terms[:cw], terms[cw:]
    projected = in_order(
        lax.ppermute(jnp.where(odd, second, first), ALL, turn_back(0)),
        lax.ppermute(jnp.where(odd, first, second), ALL, turn_back(1)),
        0,
    )
    weight_terms = lax.psum_scatter(
        weight_terms.reshape(na * (cw + 16), 2 * fw), "z", scatter_dimension=0, tiled=True
    )
    grad_embed, grad_hid, grad_gains = finish(weight_terms, projected, cw, fw, lines)
    return (projected.T, grad_hidden.T, grad_table, grad_embed, grad_hid, grad_gains)


def solution(mesh):
    nv, nd = mesh.shape["vocab"], mesh.shape["dp"]
    nb = min(4, nd)
    split = Mesh(mesh.devices.reshape(nv, nd // nb, nb), ALL)
    rows = P(DP, "vocab")
    return jax.shard_map(
        per_device,
        mesh=split,
        in_specs=(
            P(DP),
            rows,
            rows,
            P("vocab"),
            P("vocab"),
            P("vocab", DP),
            P("vocab", DP),
            rows,
        ),
        out_specs=(rows, rows, rows, P("vocab", DP), P("vocab", DP), P(None, "vocab")),
        check_vma=False,
    )
```

time: 257 us -> 224 us (0.87)
  the two profiles are of different devices: /device:TPU:56 before, /device:TPU:1 now
where the time goes in v3:
time: 224 us; the launch traced here: 223 us
  starting transfers between devices  70.8 us (32%)
  waiting for transfers between devices  68.7 us (31%)
  blocking collectives  40.2 us (18%)
  Pallas kernels  17.9 us (8%)
  between operations  14 us (6%)
  local copies, waits for them, and re-layouts  5.59 us (2%)
  other arithmetic  5.32 us (2%)
    all_gather x1, blocking collectives, per_device(): lax.all_gather(jnp.concatenate([cot, jnp.pad(digits, ((0, 12), (0, 0)))],...  24.2 us
    all_to_all x1, waiting for transfers between devices, per_device(): terms = lax.all_to_all(terms, 'vocab', 0, 0, tiled=True)  24.1 us
    all_to_all x1, blocking collectives, gather(): lax.all_to_all(jnp.broadcast_to(x[None], (count,) + x.shape), axes, 0, 0,...  16.1 us
    all_to_all x1, waiting for transfers between devices, per_device(): pieces = lax.all_to_all(pieces, 'vocab', 0, 0, tiled=True)  13.6 us
    all_gather x1, waiting for transfers between devices, per_device(): weights = lax.all_gather(weights, 'z')  13.1 us
    all_to_all x1, starting transfers between devices, per_device(): pieces = lax.all_to_all(pieces, 'vocab', 0, 0, tiled=True)  10.3 us
    ppermute x1, starting transfers between devices, per_device(): lax.ppermute(digits, ALL, swap_route(0))  8.84 us
    all_to_all x1, starting transfers between devices, per_device(): terms = lax.all_to_all(terms, 'vocab', 0, 0, tiled=True)  8.55 us
  transfers between devices with their start and end apart: 16, of which 7 were waited for; matrix products, arithmetic and copies ran while one was open for 3% of the time, Pallas kernels for 5%

profile of v3, /device:TPU:1, one launch (start us, length us, event | category | flops | bytes accessed | tf_op | source)
XLA Modules:
  0.0 222.6 jit_solution(11022690044006265463)
XLA Ops:
  7.2 0.0 all-gather.4.cloned.1.call-start
  7.2 0.7 convert_bitcast_fusion
  7.9 8.8 %collective-permute-start.3 = (bf16[2,128]{1,0:T(2,128)(2,1)S(1)}, bf16[2,128]{1,0:T(2,128)(2,1)S(1)}, u32[]{:S(2)}, u32[]{:S(2)}) collective-permute-start(bf16[2,128]{1,0:T(2,128)(2,1)S(1)} %pad_maximum_fusion.6), channel_id=1, source_target_pairs={{0,0},{1,1},{2,32},{3,33},{4,64},{5,65},{6,96},{7,97},{8,128},{9,1... | collective-permute-start | bytes 1544 | tf_op jit(solution)/shard_map/ppermute | solution.py:274
  16.7 1.9 collective-permute-start.2
  18.7 0.8 broadcast_select_fusion.15
  19.5 5.7 %collective-permute-start = (bf16[112,128]{1,0:T(8,128)(2,1)S(1)}, bf16[112,128]{1,0:T(8,128)(2,1)S(1)}, u32[]{:S(2)}, u32[]{:S(2)}) collective-permute-start(bf16[112,128]{1,0:T(8,128)(2,1)S(1)} %get-tuple-element.46), channel_id=1, source_target_pairs={{0,1},{1,0},{2,33},{3,32},{4,5},{5,4},{6,37},{7,36},{8,9},{9,8},{1... | collective-permute-start | bytes 86024 | tf_op jit(solution)/shard_map/ppermute | solution.py:279
  25.2 2.1 collective-permute-start.1
  27.4 0.9 maximum_bitcast_fusion
  28.2 0.7 pad.16
  28.9 0.0 all-gather.4.cloned.1.call-update
  28.9 1.3 copy.28
  30.3 4.2 %collective-permute-done.1 = bf16[112,128]{1,0:T(8,128)(2,1)S(1)} collective-permute-done((bf16[112,128]{1,0:T(8,128)(2,1)S(1)}, bf16[112,128]{1,0:T(8,128)(2,1)S(1)}, u32[]{:S(2)}, u32[]{:S(2)}) %collective-permute-start.1) | collective-permute-done | bytes 28704 | tf_op jit(solution)/shard_map/ppermute | solution.py:278
  34.5 24.2 %all-gather.1 = bf16[3840,128]{1,0:T(8,128)(2,1)S(1)} all-gather(bf16[240,128]{1,0:T(8,128)(2,1)S(1)} %pad_maximum_fusion.1), channel_id=3, replica_groups=mesh['vocab'=16,'z'=8,'yhi'=4] {'vocab'}, dimensions={0}, use_global_device_ids=true | all-gather | bytes 1044480 | tf_op jit(solution)/shard_map/all_gather | solution.py:282
  58.8 5.3 %shard_map.127 = bf16[16,112,256]{2,1,0:T(8,128)(2,1)} custom-call(s32[16,1,256]{2,1,0:T(1,128)S(1)} %bitcast.69, bf16[896,512]{1,0:T(8,128)(2,1)S(1)} %bitcast.68), custom_call_target="tpu_custom_call" | custom-call | flops 3758096384 | bytes 1835008 | tf_op jit(solution)/shard_map/pallas_call | solution.py:56
  64.1 13.1 %all-gather.4.cloned.1.call-done = bf16[1024,512]{0,1:T(8,128)(2,1)} async-done(((bf16[128,512]{0,1:T(8,128)(2,1)}), bf16[1024,512]{0,1:T(8,128)(2,1)}) %all-gather.4.cloned.1.call-update) | async-done | bytes 1048592 | tf_op jit(solution)/shard_map/all_gather | solution.py:270
  77.1 1.5 copy.18
  78.6 1.8 shard_map.128
  80.5 10.3 %all-to-all-start = ((bf16[16,112,256]{2,1,0:T(8,128)(2,1)}), bf16[16,112,256]{2,1,0:T(8,128)(2,1)S(1)}, u32[]{:S(2)}, u32[]{:S(2)}) async-start(bf16[16,112,256]{2,1,0:T(8,128)(2,1)} %shard_map.127), calls=%async_computation | async-start | bytes 1835008 | tf_op jit(solution)/shard_map/all_to_all | solution.py:294
  90.7 0.0 reduce-scatter.3.cloned.1.call-start
  90.8 0.7 reduce-scatter.3.cloned.1.call-update
  91.5 13.6 %all-to-all-done = bf16[16,112,256]{2,1,0:T(8,128)(2,1)S(1)} async-done(((bf16[16,112,256]{2,1,0:T(8,128)(2,1)}), bf16[16,112,256]{2,1,0:T(8,128)(2,1)S(1)}, u32[]{:S(2)}, u32[]{:S(2)}) %all-to-all-start) | async-done | bytes 917536 | tf_op jit(solution)/shard_map/all_to_all | solution.py:294
  105.1 0.1 reduce_sum.87
  105.3 5.2 %collective-permute-start.4 = (bf16[112,128]{1,0:T(8,128)(2,1)S(1)}, bf16[112,128]{1,0:T(8,128)(2,1)S(1)}, u32[]{:S(2)}, u32[]{:S(2)}) collective-permute-start(bf16[112,128]{1,0:T(8,128)(2,1)S(1)} %get-tuple-element.42), channel_id=1, source_target_pairs={{0,1},{1,0},{2,33},{3,32},{4,65},{5,64},{6,97},{7,96},{8,129},{9,1... | collective-permute-start | bytes 86024 | tf_op jit(solution)/shard_map/ppermute | solution.py:299
  110.5 4.3 %collective-permute-start.5 = (bf16[112,128]{1,0:T(8,128)(2,1)S(1)}, bf16[112,128]{1,0:T(8,128)(2,1)S(1)}, u32[]{:S(2)}, u32[]{:S(2)}) collective-permute-start(bf16[112,128]{1,0:T(8,128)(2,1)S(1)} %get-tuple-element.43), channel_id=1, source_target_pairs={{0,0},{1,1},{2,32},{3,33},{4,64},{5,65},{6,96},{7,97},{8,128},{9,1... | collective-permute-start | bytes 86024 | tf_op jit(solution)/shard_map/ppermute | solution.py:298
  114.8 5.7 %reduce-scatter.3.cloned.1.call-done = bf16[448,128]{1,0:T(8,128)(2,1)} async-done(((bf16[1792,128]{1,0:T(8,128)(2,1)}), bf16[448,128]{1,0:T(8,128)(2,1)}) %reduce-scatter.3.cloned.1.call-update) | async-done | bytes 114704 | tf_op jit(solution)/shard_map/reduce_scatter | solution.py:291
  120.5 0.9 convert_element_type.53
  121.5 0.1 fusion.9
  121.6 16.1 %all_to_all.20 = f32[16,4,128]{2,1,0:T(4,128)S(1)} all-to-all(f32[16,4,128]{2,1,0:T(4,128)S(1)} %broadcast_in_dim.4), channel_id=1, replica_groups=mesh['vocab'=16,'z'=8,'yhi'=4] {'vocab'}, dimensions={0} | all-to-all | bytes 65536 | tf_op jit(solution)/shard_map/all_to_all | solution.py:20
  137.8 0.8 fusion.4
  138.5 0.1 fusion.25
  138.6 0.8 broadcast_in_dim.5
  139.5 4.5 %all-to-all-start.2 = ((bf16[4,480,128]{2,1,0:T(8,128)(2,1)}), bf16[4,480,128]{2,1,0:T(8,128)(2,1)S(1)}, u32[]{:S(2)}, u32[]{:S(2)}) async-start(bf16[4,480,128]{2,1,0:T(8,128)(2,1)} %broadcast_in_dim.5), calls=%async_computation.3 | async-start | bytes 983040 | tf_op jit(solution)/shard_map/all_to_all | solution.py:20
  144.0 6.3 %collective-permute-start.6 = (bf16[112,128]{1,0:T(8,128)(2,1)S(1)}, bf16[112,128]{1,0:T(8,128)(2,1)S(1)}, u32[]{:S(2)}, u32[]{:S(2)}) collective-permute-start(bf16[112,128]{1,0:T(8,128)(2,1)S(1)} %get-tuple-element.38), channel_id=1, source_target_pairs={{1,0},{0,1},{33,2},{32,3},{65,4},{64,5},{97,6},{96,7},{129,8},{128... | collective-permute-start | bytes 86024 | tf_op jit(solution)/shard_map/ppermute | solution.py:349
  150.3 3.7 %collective-permute-start.7 = (bf16[112,128]{1,0:T(8,128)(2,1)S(1)}, bf16[112,128]{1,0:T(8,128)(2,1)S(1)}, u32[]{:S(2)}, u32[]{:S(2)}) collective-permute-start(bf16[112,128]{1,0:T(8,128)(2,1)S(1)} %get-tuple-element.39), channel_id=1, source_target_pairs={{0,0},{1,1},{32,2},{33,3},{64,4},{65,5},{96,6},{97,7},{128,8},{129... | collective-permute-start | bytes 86024 | tf_op jit(solution)/shard_map/ppermute | solution.py:348
  154.0 5.1 %collective-permute-done.6 = bf16[112,128]{1,0:T(8,128)(2,1)S(1)} collective-permute-done((bf16[112,128]{1,0:T(8,128)(2,1)S(1)}, bf16[112,128]{1,0:T(8,128)(2,1)S(1)}, u32[]{:S(2)}, u32[]{:S(2)}) %collective-permute-start.6) | collective-permute-done | bytes 28704 | tf_op jit(solution)/shard_map/ppermute | solution.py:349
  159.1 1.4 collective-permute-done.7
  160.6 2.6 %shard_map.129 = (bf16[16,448,128]{2,1,0:T(8,128)(2,1)S(1)}, bf16[8,128,448]{2,1,0:T(8,128)(2,1)}) custom-call(bf16[8,128,512]{2,1,0:T(8,128)(2,1)S(1)} %bitcast.64, bf16[16,240,128]{2,1,0:T(8,128)(2,1)S(1)} %bitcast.67, bf16[4,480,128]{2,1,0:T(8,128)(2,1)S(1)} %all-to-all-done.2.normed_ref, bf16[224,128]{1,0:T(8,128)(2,1)S(1)} %pad_maximum_fusion.3.mine_ref), custom_call_target="tpu_custom_call" | custom-call | flops 822083584 | bytes 4308992 | tf_op jit(solution)/shard_map/pallas_call | solution.py:184
  163.2 1.2 copy-done
  164.4 8.6 %all-to-all-start.3 = ((bf16[16,448,128]{2,1,0:T(8,128)(2,1)}), bf16[16,448,128]{2,1,0:T(8,128)(2,1)S(1)}, u32[]{:S(2)}, u32[]{:S(2)}) async-start(bf16[16,448,128]{2,1,0:T(8,128)(2,1)} %copy-done), calls=%async_computation.4 | async-start | bytes 3670016 | tf_op jit(solution)/shard_map/all_to_all | solution.py:354
  172.9 0.0 reduce-scatter.5.cloned.1.call-start
  173.0 0.7 reduce-scatter.5.cloned.1.call-update
  173.7 24.1 %all-to-all-done.3.rows_ref = bf16[16,448,128]{2,1,0:T(8,128)(2,1)S(1)} async-done(((bf16[16,448,128]{2,1,0:T(8,128)(2,1)}), bf16[16,448,128]{2,1,0:T(8,128)(2,1)S(1)}, u32[]{:S(2)}, u32[]{:S(2)}) %all-to-all-start.3) | async-done | bytes 1835040 | tf_op jit(solution)/shard_map/all_to_all | solution.py:354
  197.8 0.1 slice_reduce_fusion
  197.9 1.9 collective-permute-start.8
  199.9 7.3 %collective-permute-start.9 = (bf16[112,128]{1,0:T(8,128)(2,1)S(1)}, bf16[112,128]{1,0:T(8,128)(2,1)S(1)}, u32[]{:S(2)}, u32[]{:S(2)}) collective-permute-start(bf16[112,128]{1,0:T(8,128)(2,1)S(1)} %get-tuple-element.35), channel_id=1, source_target_pairs={{0,0},{1,1},{32,2},{33,3},{4,4},{5,5},{36,6},{37,7},{8,8},{9,9},{4... | collective-permute-start | bytes 86024 | tf_op jit(solution)/shard_map/ppermute | solution.py:360
  207.1 6.6 %shard_map.130 = f32[112,4096]{1,0:T(8,128)} custom-call(s32[16,1,256]{2,1,0:T(1,128)S(1)} %bitcast.70, bf16[16,448,128]{2,1,0:T(8,128)(2,1)S(1)} %all-to-all-done.3.rows_ref), custom_call_target="tpu_custom_call" | custom-call | flops 3758096384 | bytes 2752512 | tf_op jit(solution)/shard_map/pallas_call | solution.py:105
  213.7 0.7 pad_maximum_fusion.4
  214.4 1.7 shard_map.131
  (39 shorter events, 0.3 us)
Async XLA Ops:
  7.2 70.0 %all-gather.4.cloned.1.call-start = ((), (), s32[]{:S(2)}) async-start(), calls=%async_computation.8 | async-start | bytes 1179648 | tf_op jit(solution)/shard_map/all_gather | solution.py:270
  7.9 22.3 %collective-permute-start.3 = (bf16[2,128]{1,0:T(2,128)(2,1)S(1)}, bf16[2,128]{1,0:T(2,128)(2,1)S(1)}, u32[]{:S(2)}, u32[]{:S(2)}) collective-permute-start(bf16[2,128]{1,0:T(2,128)(2,1)S(1)} %pad_maximum_fusion.6), channel_id=1, source_target_pairs={{0,0},{1,1},{2,32},{3,33},{4,64},{5,65},{6,96},{7,97},{8,128},{9,1... | collective-permute-start | bytes 1544 | tf_op jit(solution)/shard_map/ppermute | solution.py:274
  16.7 13.5 %collective-permute-start.2 = (bf16[2,128]{1,0:T(2,128)(2,1)S(1)}, bf16[2,128]{1,0:T(2,128)(2,1)S(1)}, u32[]{:S(2)}, u32[]{:S(2)}) collective-permute-start(bf16[2,128]{1,0:T(2,128)(2,1)S(1)} %pad_maximum_fusion.6), channel_id=1, source_target_pairs={{0,1},{1,0},{2,33},{3,32},{4,65},{5,64},{6,97},{7,96},{8,129},{9,1... | collective-permute-start | bytes 1544 | tf_op jit(solution)/shard_map/ppermute | solution.py:274
  19.5 10.8 %collective-permute-start = (bf16[112,128]{1,0:T(8,128)(2,1)S(1)}, bf16[112,128]{1,0:T(8,128)(2,1)S(1)}, u32[]{:S(2)}, u32[]{:S(2)}) collective-permute-start(bf16[112,128]{1,0:T(8,128)(2,1)S(1)} %get-tuple-element.46), channel_id=1, source_target_pairs={{0,1},{1,0},{2,33},{3,32},{4,5},{5,4},{6,37},{7,36},{8,9},{9,8},{1... | collective-permute-start | bytes 86024 | tf_op jit(solution)/shard_map/ppermute | solution.py:279
  25.2 9.3 %collective-permute-start.1 = (bf16[112,128]{1,0:T(8,128)(2,1)S(1)}, bf16[112,128]{1,0:T(8,128)(2,1)S(1)}, u32[]{:S(2)}, u32[]{:S(2)}) collective-permute-start(bf16[112,128]{1,0:T(8,128)(2,1)S(1)} %get-tuple-element.47), channel_id=1, source_target_pairs={{0,0},{1,1},{2,32},{3,33},{4,4},{5,5},{6,36},{7,37},{8,8},{9,9},{1... | collective-permute-start | bytes 86024 | tf_op jit(solution)/shard_map/ppermute | solution.py:278
  80.5 41.0 %copy-start.1 = (bf16[128,224]{0,1:T(8,128)(2,1)S(1)}, bf16[128,224]{0,1:T(8,128)(2,1)}, u32[]{:S(2)}) copy-start(bf16[128,224]{0,1:T(8,128)(2,1)} %param.9) | copy-start | bytes 172036
  80.5 41.0 %copy-start.2 = (f32[224]{0:T(256)S(1)}, f32[224]{0:T(256)}, u32[]{:S(2)}) copy-start(f32[224]{0:T(256)} %param.11) | copy-start | bytes 2692
  80.5 41.0 %copy-start.3 = (f32[224]{0:T(256)S(1)}, f32[224]{0:T(256)}, u32[]{:S(2)}) copy-start(f32[224]{0:T(256)} %param.12) | copy-start | bytes 2692
  80.5 24.6 %all-to-all-start = ((bf16[16,112,256]{2,1,0:T(8,128)(2,1)}), bf16[16,112,256]{2,1,0:T(8,128)(2,1)S(1)}, u32[]{:S(2)}, u32[]{:S(2)}) async-start(bf16[16,112,256]{2,1,0:T(8,128)(2,1)} %shard_map.127), calls=%async_computation | async-start | bytes 1835008 | tf_op jit(solution)/shard_map/all_to_all | solution.py:294
  90.7 29.8 %reduce-scatter.3.cloned.1.call-start = ((), (), s32[]{:S(2)}) async-start(), calls=%async_computation.6 | async-start | bytes 573440 | tf_op jit(solution)/shard_map/reduce_scatter | solution.py:291
  105.3 16.1 %collective-permute-start.4 = (bf16[112,128]{1,0:T(8,128)(2,1)S(1)}, bf16[112,128]{1,0:T(8,128)(2,1)S(1)}, u32[]{:S(2)}, u32[]{:S(2)}) collective-permute-start(bf16[112,128]{1,0:T(8,128)(2,1)S(1)} %get-tuple-element.42), channel_id=1, source_target_pairs={{0,1},{1,0},{2,33},{3,32},{4,65},{5,64},{6,97},{7,96},{8,129},{9,1... | collective-permute-start | bytes 86024 | tf_op jit(solution)/shard_map/ppermute | solution.py:299
  110.5 10.9 %collective-permute-start.5 = (bf16[112,128]{1,0:T(8,128)(2,1)S(1)}, bf16[112,128]{1,0:T(8,128)(2,1)S(1)}, u32[]{:S(2)}, u32[]{:S(2)}) collective-permute-start(bf16[112,128]{1,0:T(8,128)(2,1)S(1)} %get-tuple-element.43), channel_id=1, source_target_pairs={{0,0},{1,1},{2,32},{3,33},{4,64},{5,65},{6,96},{7,97},{8,128},{9,1... | collective-permute-start | bytes 86024 | tf_op jit(solution)/shard_map/ppermute | solution.py:298
  139.5 21.1 %all-to-all-start.2 = ((bf16[4,480,128]{2,1,0:T(8,128)(2,1)}), bf16[4,480,128]{2,1,0:T(8,128)(2,1)S(1)}, u32[]{:S(2)}, u32[]{:S(2)}) async-start(bf16[4,480,128]{2,1,0:T(8,128)(2,1)} %broadcast_in_dim.5), calls=%async_computation.3 | async-start | bytes 983040 | tf_op jit(solution)/shard_map/all_to_all | solution.py:20
  144.0 15.1 %collective-permute-start.6 = (bf16[112,128]{1,0:T(8,128)(2,1)S(1)}, bf16[112,128]{1,0:T(8,128)(2,1)S(1)}, u32[]{:S(2)}, u32[]{:S(2)}) collective-permute-start(bf16[112,128]{1,0:T(8,128)(2,1)S(1)} %get-tuple-element.38), channel_id=1, source_target_pairs={{1,0},{0,1},{33,2},{32,3},{65,4},{64,5},{97,6},{96,7},{129,8},{128... | collective-permute-start | bytes 86024 | tf_op jit(solution)/shard_map/ppermute | solution.py:349
  150.3 10.2 %collective-permute-start.7 = (bf16[112,128]{1,0:T(8,128)(2,1)S(1)}, bf16[112,128]{1,0:T(8,128)(2,1)S(1)}, u32[]{:S(2)}, u32[]{:S(2)}) collective-permute-start(bf16[112,128]{1,0:T(8,128)(2,1)S(1)} %get-tuple-element.39), channel_id=1, source_target_pairs={{0,0},{1,1},{32,2},{33,3},{64,4},{65,5},{96,6},{97,7},{128,8},{129... | collective-permute-start | bytes 86024 | tf_op jit(solution)/shard_map/ppermute | solution.py:348
  163.2 1.2 copy-start
  164.4 33.4 %all-to-all-start.3 = ((bf16[16,448,128]{2,1,0:T(8,128)(2,1)}), bf16[16,448,128]{2,1,0:T(8,128)(2,1)S(1)}, u32[]{:S(2)}, u32[]{:S(2)}) async-start(bf16[16,448,128]{2,1,0:T(8,128)(2,1)} %copy-done), calls=%async_computation.4 | async-start | bytes 3670016 | tf_op jit(solution)/shard_map/all_to_all | solution.py:354
  172.9 41.5 %reduce-scatter.5.cloned.1.call-start = ((), (), s32[]{:S(2)}) async-start(), calls=%async_computation.7 | async-start | bytes 1179648 | tf_op jit(solution)/shard_map/reduce_scatter | solution.py:364
  197.9 15.8 %collective-permute-start.8 = (bf16[112,128]{1,0:T(8,128)(2,1)S(1)}, bf16[112,128]{1,0:T(8,128)(2,1)S(1)}, u32[]{:S(2)}, u32[]{:S(2)}) collective-permute-start(bf16[112,128]{1,0:T(8,128)(2,1)S(1)} %get-tuple-element.34), channel_id=1, source_target_pairs={{1,0},{0,1},{33,2},{32,3},{5,4},{4,5},{37,6},{36,7},{9,8},{8,9},{4... | collective-permute-start | bytes 86024 | tf_op jit(solution)/shard_map/ppermute | solution.py:361
  199.9 13.9 %collective-permute-start.9 = (bf16[112,128]{1,0:T(8,128)(2,1)S(1)}, bf16[112,128]{1,0:T(8,128)(2,1)S(1)}, u32[]{:S(2)}, u32[]{:S(2)}) collective-permute-start(bf16[112,128]{1,0:T(8,128)(2,1)S(1)} %get-tuple-element.35), channel_id=1, source_target_pairs={{0,0},{1,1},{32,2},{33,3},{4,4},{5,5},{36,6},{37,7},{8,8},{9,9},{4... | collective-permute-start | bytes 86024 | tf_op jit(solution)/shard_map/ppermute | solution.py:360
Sparse Core Ops, SparseCore 0:
  29.1 48.0 all-gather.3
  94.4 26.0 reduce-scatter.2
  176.8 33.2 reduce-scatter.4

commit v4 on v3

--- a/solution.py
+++ b/solution.py
@@ -100,14 +100,14 @@
 
 def scatter(ids, values, entries):
     blocks, rows, toks = values.shape
-    cols = rows // 4
+    cols = rows // 2
     parts = 4
     return pl.pallas_call(
         scatter_kernel,
         grid=(blocks // parts,),
         in_specs=[
             pl.BlockSpec((parts, 1, 2 * toks), lambda i: (i, 0, 0)),
-            pl.BlockSpec((parts, 2 * cols, toks), lambda i: (i, 1, 0)),
+            pl.BlockSpec((parts, 2 * cols, toks), lambda i: (i, 0, 0)),
         ],
         out_specs=pl.BlockSpec((cols, entries), lambda i: (0, 0)),
         out_shape=jax.ShapeDtypeStruct((cols, entries), F32),
@@ -152,7 +152,7 @@
     )(weights, cot)
 
 
-def out_kernel(cw, feats, weights_ref, cot_ref, normed_ref, mine_ref, out_ref, sums_ref):
+def out_kernel(cw, feats, weights_ref, cot_ref, normed_ref, out_ref, sums_ref):
     na, nb = weights_ref.shape[0], normed_ref.shape[0]
     toks = normed_ref.shape[2]
     weights = jnp.concatenate([weights_ref[a, :cw, :feats] for a in range(na)], axis=0)
@@ -161,9 +161,6 @@
         for a in range(na):
             half = b % 2 * cw
             out_ref[2 * a + b // 2, half : half + cw] = terms[a * cw : (a + 1) * cw]
-    mine = mine_ref[...]
-    for i in range(out_ref.shape[0]):
-        out_ref[i, 2 * cw :] = mine
     cot = jnp.concatenate([cot_columns(cot_ref, b, cw) for b in range(nb)], axis=1)
     normed = jnp.concatenate([normed_ref[b, :feats] for b in range(nb)], axis=1)
     sums = lax.dot_general(
@@ -179,12 +176,12 @@
         sums_ref[a, cw:, :toks] = gains.astype(BF16)
 
 
-def out_products(weights, cot, normed, mine, cw, feats):
+def out_products(weights, cot, normed, cw, feats):
     na, (nb, _, toks) = weights.shape[0], normed.shape
     return pl.pallas_call(
         functools.partial(out_kernel, cw, feats),
         out_shape=(
-            jax.ShapeDtypeStruct((2 * na, 4 * cw, toks), BF16),
+            jax.ShapeDtypeStruct((2 * na, 2 * cw, toks), BF16),
             jax.ShapeDtypeStruct((na, cw + 16, feats), BF16),
         ),
         cost_estimate=pl.CostEstimate(
@@ -193,7 +190,7 @@
             transcendentals=0,
         ),
         compiler_params=pltpu.CompilerParams(vmem_limit_bytes=32 * 1024 * 1024),
-    )(weights, cot, normed, mine)
+    )(weights, cot, normed)
 
 
 def finish_kernel(cw, fw, lines, sums_ref, done_ref, embed_ref, hidden_ref, gains_ref):
@@ -266,8 +263,7 @@
         return [(b, a) for a, b in turn(c)]
 
     weights = jnp.concatenate([proj_embed, proj_hidden], axis=0).T
-    weights = jnp.pad(weights, ((0, -cw % 128), (0, -2 * fw % 512)))
-    weights = lax.all_gather(weights, "z")
+    weights = gather(weights, "z", na)
 
     digits = jnp.stack([ids // 256, ids % 256]).astype(BF16)
     digits = in_order(
@@ -350,11 +346,13 @@
         0,
     )
 
-    terms, weight_terms = out_products(weights, cot, normed, mine, cw, 2 * fw)
+    normed, mine = lax.optimization_barrier((normed, mine))
+    terms, weight_terms = out_products(weights, cot, normed, cw, 2 * fw)
+    mine, weight_terms = lax.optimization_barrier((mine, weight_terms))
+    grad_table = scatter(local_ids, lax.all_gather(mine, "vocab"), entries)
+
     terms = lax.all_to_all(terms, "vocab", 0, 0, tiled=True)
-    grad_table = scatter(local_ids, terms, entries)
-
-    terms = jnp.sum(terms[:, :fw].astype(F32), axis=0).astype(BF16)
+    terms = jnp.sum(terms.astype(F32), axis=0).astype(BF16)
     first, second = terms[:cw], terms[cw:]
     projected = in_order(
         lax.ppermute(jnp.where(odd, second, first), ALL, turn_back(0)),

time: 224 us -> 218 us (0.973)
  waiting for transfers between devices: 68.7 us -> 30.7 us
  blocking collectives: 40.2 us -> 64.1 us
  starting transfers between devices: 70.8 us -> 82.4 us
  local copies, waits for them, and re-layouts: 5.59 us -> 3.04 us
    all_gather x0 -> x1, blocking collectives: none -> 28.7 us  [per_device(): grad_table = scatter(local_ids, lax.all_gather(mine, 'vocab'), entries)]
    all_to_all x1, waiting for transfers between devices: 24.1 us -> 0.01 us  [per_device(): terms = lax.all_to_all(terms, 'vocab', 0, 0, tiled=True)]
    all_to_all x1 -> x2, starting transfers between devices: 4.49 us -> 18.7 us  [gather(): lax.all_to_all(jnp.broadcast_to(x[None], (count,) + x.shape), axes, 0, 0,...]
    all_gather x1 -> x0, waiting for transfers between devices: 13.1 us -> none  [per_device(): weights = lax.all_gather(weights, 'z')]
    all_to_all x1, starting transfers between devices: 10.3 us -> 3.71 us  [per_device(): pieces = lax.all_to_all(pieces, 'vocab', 0, 0, tiled=True)]
    all_gather x1, blocking collectives: 24.2 us -> 19.6 us  [per_device(): lax.all_gather(jnp.concatenate([cot, jnp.pad(digits, ((0, 12), (0, 0)))],...]
    ppermute x1, waiting for transfers between devices: 4.24 us -> 0.01 us  [per_device(): lax.ppermute(jnp.where(odd, second, first), ALL, turn(0))]
    reduce_scatter x1, waiting for transfers between devices: 5.69 us -> 8.9 us  [per_device(): lax.psum_scatter(shares.reshape(nb * 2 * fw, toks), 'yhi', scatter_dimens...]
  transfers between devices with their start and end apart: 16 -> 16, of which waited for: 7 -> 4; matrix products, arithmetic and copies ran while one was open for 3% -> 2% of each run, Pallas kernels for 5% -> 5%
where the time goes in v4:
time: 218 us; the launch traced here: 217 us
  starting transfers between devices  82.4 us (38%)
  blocking collectives  64.1 us (29%)
  waiting for transfers between devices  30.7 us (14%)
  Pallas kernels  17.3 us (8%)
  between operations  14.4 us (7%)
  other arithmetic  5.41 us (2%)
  local copies, waits for them, and re-layouts  3.04 us (1%)
    all_gather x1, blocking collectives, per_device(): grad_table = scatter(local_ids, lax.all_gather(mine, 'vocab'), entries)  28.7 us
    all_gather x1, blocking collectives, per_device(): lax.all_gather(jnp.concatenate([cot, jnp.pad(digits, ((0, 12), (0, 0)))],...  19.6 us
    all_to_all x2, starting transfers between devices, gather(): lax.all_to_all(jnp.broadcast_to(x[None], (count,) + x.shape), axes, 0, 0,...  18.7 us
    all_to_all x1, blocking collectives, gather(): lax.all_to_all(jnp.broadcast_to(x[None], (count,) + x.shape), axes, 0, 0,...  15.8 us
    all_to_all x1, waiting for transfers between devices, per_device(): pieces = lax.all_to_all(pieces, 'vocab', 0, 0, tiled=True)  13.7 us
    all_to_all x1, starting transfers between devices, per_device(): terms = lax.all_to_all(terms, 'vocab', 0, 0, tiled=True)  11.1 us
    reduce_scatter x1, waiting for transfers between devices, per_device(): lax.psum_scatter(shares.reshape(nb * 2 * fw, toks), 'yhi', scatter_dimens...  8.9 us
    ppermute x1, starting transfers between devices, per_device(): lax.ppermute(digits, ALL, swap_route(0))  8.84 us
  transfers between devices with their start and end apart: 16, of which 4 were waited for; matrix products, arithmetic and copies ran while one was open for 2% of the time, Pallas kernels for 5%

profile of v4, /device:TPU:1, one launch (start us, length us, event | category | flops | bytes accessed | tf_op | source)
XLA Modules:
  0.0 217.4 jit_solution(9584036929807725777)
XLA Ops:
  7.2 0.7 convert_bitcast_fusion
  7.9 8.8 %collective-permute-start.3 = (bf16[2,128]{1,0:T(2,128)(2,1)S(1)}, bf16[2,128]{1,0:T(2,128)(2,1)S(1)}, u32[]{:S(2)}, u32[]{:S(2)}) collective-permute-start(bf16[2,128]{1,0:T(2,128)(2,1)S(1)} %pad_maximum_fusion.6), channel_id=1, source_target_pairs={{0,0},{1,1},{2,32},{3,33},{4,64},{5,65},{6,96},{7,97},{8,128},{9,1... | collective-permute-start | bytes 1544 | tf_op jit(solution)/shard_map/ppermute | solution.py:270
  16.8 1.9 collective-permute-start.2
  18.7 0.8 broadcast_select_fusion.15
  19.5 5.7 %collective-permute-start = (bf16[112,128]{1,0:T(8,128)(2,1)S(1)}, bf16[112,128]{1,0:T(8,128)(2,1)S(1)}, u32[]{:S(2)}, u32[]{:S(2)}) collective-permute-start(bf16[112,128]{1,0:T(8,128)(2,1)S(1)} %get-tuple-element.54), channel_id=1, source_target_pairs={{0,1},{1,0},{2,33},{3,32},{4,5},{5,4},{6,37},{7,36},{8,9},{9,8},{1... | collective-permute-start | bytes 86024 | tf_op jit(solution)/shard_map/ppermute | solution.py:275
  25.2 2.1 collective-permute-start.1
  27.4 0.9 maximum_bitcast_fusion
  28.3 0.1 copy.18
  28.4 1.0 broadcast_in_dim.6
  29.4 15.2 %all-to-all-start = ((bf16[8,112,448]{2,1,0:T(8,128)(2,1)}), bf16[8,112,448]{2,1,0:T(8,128)(2,1)S(1)}, u32[]{:S(2)}, u32[]{:S(2)}) async-start(bf16[8,112,448]{2,1,0:T(8,128)(2,1)} %broadcast_in_dim.6), calls=%async_computation | async-start | bytes 1835008 | tf_op jit(solution)/shard_map/all_to_all | solution.py:20
  44.6 0.1 copy.28
  44.7 0.0 collective-permute-done.2
  44.8 0.0 collective-permute-done
  44.8 0.0 collective-permute-done.1
  44.8 19.6 %all-gather = bf16[3840,128]{1,0:T(8,128)(2,1)S(1)} all-gather(bf16[240,128]{1,0:T(8,128)(2,1)S(1)} %pad_maximum_fusion.1), channel_id=2, replica_groups=mesh['vocab'=16,'z'=8,'yhi'=4] {'vocab'}, dimensions={0}, use_global_device_ids=true | all-gather | bytes 1044480 | tf_op jit(solution)/shard_map/all_gather | solution.py:278
  64.6 4.6 %shard_map.127 = bf16[16,112,256]{2,1,0:T(8,128)(2,1)S(1)} custom-call(s32[16,1,256]{2,1,0:T(1,128)S(1)} %bitcast.68, bf16[896,512]{1,0:T(8,128)(2,1)S(1)} %bitcast.66), custom_call_target="tpu_custom_call" | custom-call | flops 3758096384 | bytes 1835008 | tf_op jit(solution)/shard_map/pallas_call | solution.py:56
  69.2 0.9 copy-done
  70.1 1.8 shard_map.128
  71.9 3.7 %all-to-all-start.1 = ((bf16[16,112,256]{2,1,0:T(8,128)(2,1)}), bf16[16,112,256]{2,1,0:T(8,128)(2,1)S(1)}, u32[]{:S(2)}, u32[]{:S(2)}) async-start(bf16[16,112,256]{2,1,0:T(8,128)(2,1)} %copy-done), calls=%async_computation.1 | async-start | bytes 1835008 | tf_op jit(solution)/shard_map/all_to_all | solution.py:290
  75.6 0.0 reduce-scatter.3.cloned.1.call-start
  75.6 0.7 reduce-scatter.3.cloned.1.call-update
  76.3 13.7 %all-to-all-done.1 = bf16[16,112,256]{2,1,0:T(8,128)(2,1)S(1)} async-done(((bf16[16,112,256]{2,1,0:T(8,128)(2,1)}), bf16[16,112,256]{2,1,0:T(8,128)(2,1)S(1)}, u32[]{:S(2)}, u32[]{:S(2)}) %all-to-all-start.1) | async-done | bytes 917536 | tf_op jit(solution)/shard_map/all_to_all | solution.py:290
  90.1 0.1 reduce_sum.87
  90.2 8.3 %collective-permute-start.4 = (bf16[112,128]{1,0:T(8,128)(2,1)S(1)}, bf16[112,128]{1,0:T(8,128)(2,1)S(1)}, u32[]{:S(2)}, u32[]{:S(2)}) collective-permute-start(bf16[112,128]{1,0:T(8,128)(2,1)S(1)} %get-tuple-element.50), channel_id=1, source_target_pairs={{0,1},{1,0},{2,33},{3,32},{4,65},{5,64},{6,97},{7,96},{8,129},{9,1... | collective-permute-start | bytes 86024 | tf_op jit(solution)/shard_map/ppermute | solution.py:295
  98.5 3.5 %collective-permute-start.5 = (bf16[112,128]{1,0:T(8,128)(2,1)S(1)}, bf16[112,128]{1,0:T(8,128)(2,1)S(1)}, u32[]{:S(2)}, u32[]{:S(2)}) collective-permute-start(bf16[112,128]{1,0:T(8,128)(2,1)S(1)} %get-tuple-element.51), channel_id=1, source_target_pairs={{0,0},{1,1},{2,32},{3,33},{4,64},{5,65},{6,96},{7,97},{8,128},{9,1... | collective-permute-start | bytes 86024 | tf_op jit(solution)/shard_map/ppermute | solution.py:294
  102.0 8.9 %reduce-scatter.3.cloned.1.call-done = bf16[448,128]{1,0:T(8,128)(2,1)} async-done(((bf16[1792,128]{1,0:T(8,128)(2,1)}), bf16[448,128]{1,0:T(8,128)(2,1)}) %reduce-scatter.3.cloned.1.call-update) | async-done | bytes 114704 | tf_op jit(solution)/shard_map/reduce_scatter | solution.py:287
  110.9 0.9 convert_element_type.51
  111.8 0.1 fusion.9
  112.0 15.8 %all_to_all.25 = f32[16,4,128]{2,1,0:T(4,128)S(1)} all-to-all(f32[16,4,128]{2,1,0:T(4,128)S(1)} %broadcast_in_dim.7), channel_id=1, replica_groups=mesh['vocab'=16,'z'=8,'yhi'=4] {'vocab'}, dimensions={0} | all-to-all | bytes 65536 | tf_op jit(solution)/shard_map/all_to_all | solution.py:20
  127.9 0.8 fusion.4
  128.7 0.1 fusion.25
  128.8 0.8 broadcast_in_dim.8
  129.6 3.5 %all-to-all-start.3 = ((bf16[4,480,128]{2,1,0:T(8,128)(2,1)}), bf16[4,480,128]{2,1,0:T(8,128)(2,1)S(1)}, u32[]{:S(2)}, u32[]{:S(2)}) async-start(bf16[4,480,128]{2,1,0:T(8,128)(2,1)} %broadcast_in_dim.8), calls=%async_computation.4 | async-start | bytes 983040 | tf_op jit(solution)/shard_map/all_to_all | solution.py:20
  133.1 6.0 %collective-permute-start.6 = (bf16[112,128]{1,0:T(8,128)(2,1)S(1)}, bf16[112,128]{1,0:T(8,128)(2,1)S(1)}, u32[]{:S(2)}, u32[]{:S(2)}) collective-permute-start(bf16[112,128]{1,0:T(8,128)(2,1)S(1)} %get-tuple-element.46), channel_id=1, source_target_pairs={{1,0},{0,1},{33,2},{32,3},{65,4},{64,5},{97,6},{96,7},{129,8},{128... | collective-permute-start | bytes 86024 | tf_op jit(solution)/shard_map/ppermute | solution.py:345
  139.1 3.7 %collective-permute-start.7 = (bf16[112,128]{1,0:T(8,128)(2,1)S(1)}, bf16[112,128]{1,0:T(8,128)(2,1)S(1)}, u32[]{:S(2)}, u32[]{:S(2)}) collective-permute-start(bf16[112,128]{1,0:T(8,128)(2,1)S(1)} %get-tuple-element.47), channel_id=1, source_target_pairs={{0,0},{1,1},{32,2},{33,3},{64,4},{65,5},{96,6},{97,7},{128,8},{129... | collective-permute-start | bytes 86024 | tf_op jit(solution)/shard_map/ppermute | solution.py:344
  142.8 5.4 %collective-permute-done.6 = bf16[112,128]{1,0:T(8,128)(2,1)S(1)} collective-permute-done((bf16[112,128]{1,0:T(8,128)(2,1)S(1)}, bf16[112,128]{1,0:T(8,128)(2,1)S(1)}, u32[]{:S(2)}, u32[]{:S(2)}) %collective-permute-start.6) | collective-permute-done | bytes 28704 | tf_op jit(solution)/shard_map/ppermute | solution.py:345
  148.2 1.3 collective-permute-done.7
  149.5 2.8 %shard_map.129 = (bf16[16,224,128]{2,1,0:T(8,128)(2,1)}, bf16[8,128,448]{2,1,0:T(8,128)(2,1)}) custom-call(bf16[8,112,448]{2,1,0:T(8,128)(2,1)S(1)} %all-to-all-done.weights_ref, bf16[16,240,128]{2,1,0:T(8,128)(2,1)S(1)} %bitcast.65, bf16[4,480,128]{2,1,0:T(8,128)(2,1)S(1)} %all-to-all-done.3.normed_ref), custom_call_target="tpu_custom_call" | custom-call | flops 822083584 | bytes 4063232 | tf_op jit(solution)/shard_map/pallas_call | solution.py:181
  152.3 11.1 %all-to-all-start.4 = ((bf16[16,224,128]{2,1,0:T(8,128)(2,1)}), bf16[16,224,128]{2,1,0:T(8,128)(2,1)S(1)}, u32[]{:S(2)}, u32[]{:S(2)}) async-start(bf16[16,224,128]{2,1,0:T(8,128)(2,1)} %get-tuple-element.20), calls=%async_computation.5 | async-start | bytes 1835008 | tf_op jit(solution)/shard_map/all_to_all | solution.py:354
  163.4 0.0 reduce-scatter.5.cloned.1.call-start
  163.5 0.7 reduce-scatter.5.cloned.1.call-update
  164.2 28.7 %all-gather.1 = bf16[3584,128]{1,0:T(8,128)(2,1)S(1)} all-gather(bf16[224,128]{1,0:T(8,128)(2,1)S(1)} %pad_maximum_fusion.3), channel_id=3, replica_groups=mesh['vocab'=16,'z'=8,'yhi'=4] {'vocab'}, dimensions={0}, use_global_device_ids=true | all-gather | bytes 974848 | tf_op jit(solution)/shard_map/all_gather | solution.py:352
  192.8 0.1 reduce_sum.95
  193.0 1.9 collective-permute-start.8
  194.9 6.8 %collective-permute-start.9 = (bf16[112,128]{1,0:T(8,128)(2,1)S(1)}, bf16[112,128]{1,0:T(8,128)(2,1)S(1)}, u32[]{:S(2)}, u32[]{:S(2)}) collective-permute-start(bf16[112,128]{1,0:T(8,128)(2,1)S(1)} %get-tuple-element.43), channel_id=1, source_target_pairs={{0,0},{1,1},{32,2},{33,3},{4,4},{5,5},{36,6},{37,7},{8,8},{9,9},{4... | collective-permute-start | bytes 86024 | tf_op jit(solution)/shard_map/ppermute | solution.py:358
  201.7 6.5 %shard_map.130 = f32[112,4096]{1,0:T(8,128)} custom-call(s32[16,1,256]{2,1,0:T(1,128)S(1)} %bitcast.69, bf16[16,224,128]{2,1,0:T(8,128)(2,1)S(1)} %bitcast.67), custom_call_target="tpu_custom_call" | custom-call | flops 3758096384 | bytes 2752512 | tf_op jit(solution)/shard_map/pallas_call | solution.py:105
  208.2 0.7 pad_maximum_fusion.4
  208.9 1.7 shard_map.131
  (41 shorter events, 0.3 us)
Async XLA Ops:
  7.2 37.4 %copy-start.1 = (bf16[112,4096]{1,0:T(8,128)(2,1)S(1)}, bf16[112,4096]{1,0:T(8,128)(2,1)}, u32[]{:S(2)}) copy-start(bf16[112,4096]{1,0:T(8,128)(2,1)} %param.10) | copy-start | bytes 2752516
  7.9 36.8 %collective-permute-start.3 = (bf16[2,128]{1,0:T(2,128)(2,1)S(1)}, bf16[2,128]{1,0:T(2,128)(2,1)S(1)}, u32[]{:S(2)}, u32[]{:S(2)}) collective-permute-start(bf16[2,128]{1,0:T(2,128)(2,1)S(1)} %pad_maximum_fusion.6), channel_id=1, source_target_pairs={{0,0},{1,1},{2,32},{3,33},{4,64},{5,65},{6,96},{7,97},{8,128},{9,1... | collective-permute-start | bytes 1544 | tf_op jit(solution)/shard_map/ppermute | solution.py:270
  16.8 27.9 %collective-permute-start.2 = (bf16[2,128]{1,0:T(2,128)(2,1)S(1)}, bf16[2,128]{1,0:T(2,128)(2,1)S(1)}, u32[]{:S(2)}, u32[]{:S(2)}) collective-permute-start(bf16[2,128]{1,0:T(2,128)(2,1)S(1)} %pad_maximum_fusion.6), channel_id=1, source_target_pairs={{0,1},{1,0},{2,33},{3,32},{4,65},{5,64},{6,97},{7,96},{8,129},{9,1... | collective-permute-start | bytes 1544 | tf_op jit(solution)/shard_map/ppermute | solution.py:270
  19.5 25.3 %collective-permute-start = (bf16[112,128]{1,0:T(8,128)(2,1)S(1)}, bf16[112,128]{1,0:T(8,128)(2,1)S(1)}, u32[]{:S(2)}, u32[]{:S(2)}) collective-permute-start(bf16[112,128]{1,0:T(8,128)(2,1)S(1)} %get-tuple-element.54), channel_id=1, source_target_pairs={{0,1},{1,0},{2,33},{3,32},{4,5},{5,4},{6,37},{7,36},{8,9},{9,8},{1... | collective-permute-start | bytes 86024 | tf_op jit(solution)/shard_map/ppermute | solution.py:275
  25.2 19.5 %collective-permute-start.1 = (bf16[112,128]{1,0:T(8,128)(2,1)S(1)}, bf16[112,128]{1,0:T(8,128)(2,1)S(1)}, u32[]{:S(2)}, u32[]{:S(2)}) collective-permute-start(bf16[112,128]{1,0:T(8,128)(2,1)S(1)} %get-tuple-element.55), channel_id=1, source_target_pairs={{0,0},{1,1},{2,32},{3,33},{4,4},{5,5},{6,36},{7,37},{8,8},{9,9},{1... | collective-permute-start | bytes 86024 | tf_op jit(solution)/shard_map/ppermute | solution.py:274
  29.4 40.7 %all-to-all-start = ((bf16[8,112,448]{2,1,0:T(8,128)(2,1)}), bf16[8,112,448]{2,1,0:T(8,128)(2,1)S(1)}, u32[]{:S(2)}, u32[]{:S(2)}) async-start(bf16[8,112,448]{2,1,0:T(8,128)(2,1)} %broadcast_in_dim.6), calls=%async_computation | async-start | bytes 1835008 | tf_op jit(solution)/shard_map/all_to_all | solution.py:20
  69.1 0.9 copy-start
  71.9 40.0 %copy-start.2 = (bf16[128,224]{0,1:T(8,128)(2,1)S(1)}, bf16[128,224]{0,1:T(8,128)(2,1)}, u32[]{:S(2)}) copy-start(bf16[128,224]{0,1:T(8,128)(2,1)} %param.9) | copy-start | bytes 172036
  71.9 40.0 %copy-start.3 = (f32[224]{0:T(256)S(1)}, f32[224]{0:T(256)}, u32[]{:S(2)}) copy-start(f32[224]{0:T(256)} %param.11) | copy-start | bytes 2692
  71.9 40.0 %copy-start.4 = (f32[224]{0:T(256)S(1)}, f32[224]{0:T(256)}, u32[]{:S(2)}) copy-start(f32[224]{0:T(256)} %param.12) | copy-start | bytes 2692
  71.9 18.2 %all-to-all-start.1 = ((bf16[16,112,256]{2,1,0:T(8,128)(2,1)}), bf16[16,112,256]{2,1,0:T(8,128)(2,1)S(1)}, u32[]{:S(2)}, u32[]{:S(2)}) async-start(bf16[16,112,256]{2,1,0:T(8,128)(2,1)} %copy-done), calls=%async_computation.1 | async-start | bytes 1835008 | tf_op jit(solution)/shard_map/all_to_all | solution.py:290
  75.6 35.3 %reduce-scatter.3.cloned.1.call-start = ((), (), s32[]{:S(2)}) async-start(), calls=%async_computation.7 | async-start | bytes 573440 | tf_op jit(solution)/shard_map/reduce_scatter | solution.py:287
  90.2 21.6 %collective-permute-start.4 = (bf16[112,128]{1,0:T(8,128)(2,1)S(1)}, bf16[112,128]{1,0:T(8,128)(2,1)S(1)}, u32[]{:S(2)}, u32[]{:S(2)}) collective-permute-start(bf16[112,128]{1,0:T(8,128)(2,1)S(1)} %get-tuple-element.50), channel_id=1, source_target_pairs={{0,1},{1,0},{2,33},{3,32},{4,65},{5,64},{6,97},{7,96},{8,129},{9,1... | collective-permute-start | bytes 86024 | tf_op jit(solution)/shard_map/ppermute | solution.py:295
  98.5 13.3 %collective-permute-start.5 = (bf16[112,128]{1,0:T(8,128)(2,1)S(1)}, bf16[112,128]{1,0:T(8,128)(2,1)S(1)}, u32[]{:S(2)}, u32[]{:S(2)}) collective-permute-start(bf16[112,128]{1,0:T(8,128)(2,1)S(1)} %get-tuple-element.51), channel_id=1, source_target_pairs={{0,0},{1,1},{2,32},{3,33},{4,64},{5,65},{6,96},{7,97},{8,128},{9,1... | collective-permute-start | bytes 86024 | tf_op jit(solution)/shard_map/ppermute | solution.py:294
  129.6 19.9 %all-to-all-start.3 = ((bf16[4,480,128]{2,1,0:T(8,128)(2,1)}), bf16[4,480,128]{2,1,0:T(8,128)(2,1)S(1)}, u32[]{:S(2)}, u32[]{:S(2)}) async-start(bf16[4,480,128]{2,1,0:T(8,128)(2,1)} %broadcast_in_dim.8), calls=%async_computation.4 | async-start | bytes 983040 | tf_op jit(solution)/shard_map/all_to_all | solution.py:20
  133.1 15.2 %collective-permute-start.6 = (bf16[112,128]{1,0:T(8,128)(2,1)S(1)}, bf16[112,128]{1,0:T(8,128)(2,1)S(1)}, u32[]{:S(2)}, u32[]{:S(2)}) collective-permute-start(bf16[112,128]{1,0:T(8,128)(2,1)S(1)} %get-tuple-element.46), channel_id=1, source_target_pairs={{1,0},{0,1},{33,2},{32,3},{65,4},{64,5},{97,6},{96,7},{129,8},{128... | collective-permute-start | bytes 86024 | tf_op jit(solution)/shard_map/ppermute | solution.py:345
  139.1 10.4 %collective-permute-start.7 = (bf16[112,128]{1,0:T(8,128)(2,1)S(1)}, bf16[112,128]{1,0:T(8,128)(2,1)S(1)}, u32[]{:S(2)}, u32[]{:S(2)}) collective-permute-start(bf16[112,128]{1,0:T(8,128)(2,1)S(1)} %get-tuple-element.47), channel_id=1, source_target_pairs={{0,0},{1,1},{32,2},{33,3},{64,4},{65,5},{96,6},{97,7},{128,8},{129... | collective-permute-start | bytes 86024 | tf_op jit(solution)/shard_map/ppermute | solution.py:344
  152.3 40.5 %all-to-all-start.4 = ((bf16[16,224,128]{2,1,0:T(8,128)(2,1)}), bf16[16,224,128]{2,1,0:T(8,128)(2,1)S(1)}, u32[]{:S(2)}, u32[]{:S(2)}) async-start(bf16[16,224,128]{2,1,0:T(8,128)(2,1)} %get-tuple-element.20), calls=%async_computation.5 | async-start | bytes 1835008 | tf_op jit(solution)/shard_map/all_to_all | solution.py:354
  163.4 45.5 %reduce-scatter.5.cloned.1.call-start = ((), (), s32[]{:S(2)}) async-start(), calls=%async_computation.8 | async-start | bytes 1179648 | tf_op jit(solution)/shard_map/reduce_scatter | solution.py:362
  193.0 15.2 %collective-permute-start.8 = (bf16[112,128]{1,0:T(8,128)(2,1)S(1)}, bf16[112,128]{1,0:T(8,128)(2,1)S(1)}, u32[]{:S(2)}, u32[]{:S(2)}) collective-permute-start(bf16[112,128]{1,0:T(8,128)(2,1)S(1)} %get-tuple-element.42), channel_id=1, source_target_pairs={{1,0},{0,1},{33,2},{32,3},{5,4},{4,5},{37,6},{36,7},{9,8},{8,9},{4... | collective-permute-start | bytes 86024 | tf_op jit(solution)/shard_map/ppermute | solution.py:359
  194.9 13.3 %collective-permute-start.9 = (bf16[112,128]{1,0:T(8,128)(2,1)S(1)}, bf16[112,128]{1,0:T(8,128)(2,1)S(1)}, u32[]{:S(2)}, u32[]{:S(2)}) collective-permute-start(bf16[112,128]{1,0:T(8,128)(2,1)S(1)} %get-tuple-element.43), channel_id=1, source_target_pairs={{0,0},{1,1},{32,2},{33,3},{4,4},{5,5},{36,6},{37,7},{8,8},{9,9},{4... | collective-permute-start | bytes 86024 | tf_op jit(solution)/shard_map/ppermute | solution.py:358
Sparse Core Ops, SparseCore 0:
  79.8 30.9 reduce-scatter.2
  167.3 31.8 reduce-scatter.4

commit v5 on v4

--- a/solution.py
+++ b/solution.py
@@ -13,7 +13,8 @@
 BF16 = jnp.bfloat16
 F32 = jnp.float32
 DP = ("z", "yhi")
-ALL = ("vocab", "z", "yhi")
+ALL = ("chip", "core", "z", "yhi")
+VOCAB = ("chip", "core")
 
 
 def gather(x, axes, count):
@@ -71,13 +72,22 @@
     )(ids, stacked)
 
 
-def scatter_kernel(ids_ref, rows_ref, out_ref):
+def scatter_kernel(ids_ref, own_ref, other_ref, out_ref, done_ref):
     width = out_ref.shape[1] // GROUPS
     cols = out_ref.shape[0]
     parts = ids_ref.shape[0]
+    step = pl.program_id(0)
+    own = 2 * step < pl.num_programs(0)
     ids = jnp.concatenate([ids_ref[i] for i in range(parts)], axis=1)
     values = jnp.concatenate(
-        [rows_ref[i, j * cols : (j + 1) * cols] for i in range(parts) for j in range(2)], axis=1
+        [
+            jnp.where(
+                own, own_ref[i, j * cols : (j + 1) * cols], other_ref[i, j * cols : (j + 1) * cols]
+            )
+            for i in range(parts)
+            for j in range(2)
+        ],
+        axis=1,
     )
     group = group_of(ids, width)
     spread = jnp.concatenate(
@@ -86,6 +96,7 @@
     sums = lax.dot_general(
         spread, one_hot_of(ids, width), (((1,), (1,)), ((), ())), preferred_element_type=F32
     )
+    done_ref[...] = jnp.zeros_like(done_ref)
 
     @pl.when(pl.program_id(0) == 0)
     def _():
@@ -98,70 +109,96 @@
             out_ref[:, k * width : (k + 1) * width] += sums[k * cols : (k + 1) * cols]
 
 
-def scatter(ids, values, entries):
-    blocks, rows, toks = values.shape
+def scatter(ids, own, other, entries):
+    blocks, rows, toks = own.shape
     cols = rows // 2
     parts = 4
+    half = blocks // parts
     return pl.pallas_call(
         scatter_kernel,
-        grid=(blocks // parts,),
+        grid=(2 * half,),
         in_specs=[
             pl.BlockSpec((parts, 1, 2 * toks), lambda i: (i, 0, 0)),
-            pl.BlockSpec((parts, 2 * cols, toks), lambda i: (i, 0, 0)),
+            pl.BlockSpec((parts, 2 * cols, toks), lambda i: (jnp.minimum(i, half - 1), 0, 0)),
+            pl.BlockSpec((parts, 2 * cols, toks), lambda i: (jnp.maximum(i - half, 0), 0, 0)),
         ],
-        out_specs=pl.BlockSpec((cols, entries), lambda i: (0, 0)),
-        out_shape=jax.ShapeDtypeStruct((cols, entries), F32),
+        out_specs=(
+            pl.BlockSpec((cols, entries), lambda i: (0, 0)),
+            pl.BlockSpec((8, 128), lambda i: (0, 0)),
+        ),
+        out_shape=(
+            jax.ShapeDtypeStruct((cols, entries), F32),
+            jax.ShapeDtypeStruct((8, 128), F32),
+        ),
         cost_estimate=pl.CostEstimate(
-            flops=4 * blocks * toks * cols * entries,
-            bytes_accessed=cols * (4 * entries + 4 * blocks * toks),
+            flops=8 * blocks * toks * cols * entries,
+            bytes_accessed=cols * (4 * entries + 8 * blocks * toks),
             transcendentals=0,
         ),
         compiler_params=pltpu.CompilerParams(vmem_limit_bytes=32 * 1024 * 1024),
-    )(ids, values)
-
-
-def cot_columns(cot_ref, b, cw):
+    )(ids, own, other)
+
+
+def cot_columns(core, own_ref, other_ref, b, cw):
     half = b % 2 * cw
+    own = core == b // 2
     return jnp.concatenate(
-        [cot_ref[i, half : half + cw] for i in range(b // 2, cot_ref.shape[0], 2)], axis=0
-    )
-
-
-def grad_kernel(cw, weights_ref, cot_ref, out_ref):
+        [
+            jnp.where(own, own_ref[i, half : half + cw], other_ref[i, half : half + cw])
+            for i in range(own_ref.shape[0])
+        ],
+        axis=0,
+    )
+
+
+def grad_kernel(cw, place_ref, weights_ref, own_ref, other_ref, out_ref):
     nb, feats, _ = out_ref.shape
-    weights = jnp.concatenate(
-        [weights_ref[a, :cw, :feats] for a in range(weights_ref.shape[0])], axis=0
-    ).T
+    weights = jnp.concatenate([weights_ref[a] for a in range(weights_ref.shape[0])], axis=0).T
     for b in range(nb):
-        out_ref[b] = jnp.dot(
-            weights, cot_columns(cot_ref, b, cw), preferred_element_type=F32
-        ).astype(BF16)
-
-
-def grad_products(weights, cot, nb, cw, feats):
-    na, toks = weights.shape[0], cot.shape[2]
+        share = jnp.dot(
+            weights,
+            cot_columns(place_ref[0], own_ref, other_ref, b, cw),
+            preferred_element_type=F32,
+        )
+        out_ref[lax.rem(b + nb - place_ref[1], nb)] = share.astype(BF16)
+
+
+def grad_products(place, weights, own, other, nb):
+    na, cw, feats = weights.shape
+    toks = own.shape[2]
+    whole = pl.BlockSpec(memory_space=pltpu.VMEM)
     return pl.pallas_call(
         functools.partial(grad_kernel, cw),
+        in_specs=[pl.BlockSpec(memory_space=pltpu.SMEM), whole, whole, whole],
         out_shape=jax.ShapeDtypeStruct((nb, feats, toks), BF16),
         cost_estimate=pl.CostEstimate(
             flops=2 * na * cw * feats * nb * toks,
-            bytes_accessed=2 * (weights.size + cot.size + nb * feats * toks),
+            bytes_accessed=2 * (weights.size + 2 * own.size + nb * feats * toks),
             transcendentals=0,
         ),
         compiler_params=pltpu.CompilerParams(vmem_limit_bytes=16 * 1024 * 1024),
-    )(weights, cot)
-
-
-def out_kernel(cw, feats, weights_ref, cot_ref, normed_ref, out_ref, sums_ref):
-    na, nb = weights_ref.shape[0], normed_ref.shape[0]
-    toks = normed_ref.shape[2]
-    weights = jnp.concatenate([weights_ref[a, :cw, :feats] for a in range(na)], axis=0)
-    for b in range(nb):
-        terms = jnp.dot(weights, normed_ref[b, :feats], preferred_element_type=F32).astype(BF16)
+    )(place, weights, own, other)
+
+
+def out_kernel(
+    place_ref, weights_ref, own_ref, other_ref, normed_ref, keep_ref, send_ref, top_ref, low_ref
+):
+    na, cw, feats = weights_ref.shape
+    nb, _, toks = normed_ref.shape
+    core = place_ref[0]
+    weights = jnp.concatenate([weights_ref[a] for a in range(na)], axis=0)
+    terms = [
+        jnp.dot(weights, normed_ref[b, :feats], preferred_element_type=F32) for b in range(nb)
+    ]
+    for x in range(2):
+        keep = jnp.where(core == 0, terms[x], terms[x + 2]).astype(BF16)
+        send = jnp.where(core == 0, terms[x + 2], terms[x]).astype(BF16)
         for a in range(na):
-            half = b % 2 * cw
-            out_ref[2 * a + b // 2, half : half + cw] = terms[a * cw : (a + 1) * cw]
-    cot = jnp.concatenate([cot_columns(cot_ref, b, cw) for b in range(nb)], axis=1)
+            keep_ref[a, x * cw : (x + 1) * cw] = keep[a * cw : (a + 1) * cw]
+            send_ref[a, x * cw : (x + 1) * cw] = send[a * cw : (a + 1) * cw]
+    cot = jnp.concatenate(
+        [cot_columns(core, own_ref, other_ref, b, cw) for b in range(nb)], axis=1
+    )
     normed = jnp.concatenate([normed_ref[b, :feats] for b in range(nb)], axis=1)
     sums = lax.dot_general(
         cot, normed, (((1,), (1,)), ((), ())), preferred_element_type=F32
@@ -170,32 +207,39 @@
     for b in range(nb):
         gains += normed_ref[b, feats : feats + 16].astype(F32)
         gains += normed_ref[b, feats + 16 : feats + 32].astype(F32)
+    half = top_ref.shape[1]
     for a in range(na):
-        sums_ref[a, :cw] = sums[a * cw : (a + 1) * cw]
-        sums_ref[a, cw:] = jnp.zeros((16, feats), BF16)
-        sums_ref[a, cw:, :toks] = gains.astype(BF16)
-
-
-def out_products(weights, cot, normed, cw, feats):
-    na, (nb, _, toks) = weights.shape[0], normed.shape
+        top_ref[a] = sums[a * cw : a * cw + half]
+        low_ref[a, : cw - half] = sums[a * cw + half : (a + 1) * cw]
+        low_ref[a, cw - half :] = jnp.zeros((16, feats), BF16)
+        low_ref[a, cw - half :, :toks] = gains.astype(BF16)
+
+
+def out_products(place, weights, own, other, normed):
+    na, cw, feats = weights.shape
+    nb, _, toks = normed.shape
+    whole = pl.BlockSpec(memory_space=pltpu.VMEM)
     return pl.pallas_call(
-        functools.partial(out_kernel, cw, feats),
+        out_kernel,
+        in_specs=[pl.BlockSpec(memory_space=pltpu.SMEM), whole, whole, whole, whole],
         out_shape=(
-            jax.ShapeDtypeStruct((2 * na, 2 * cw, toks), BF16),
-            jax.ShapeDtypeStruct((na, cw + 16, feats), BF16),
+            jax.ShapeDtypeStruct((na, 2 * cw, toks), BF16),
+            jax.ShapeDtypeStruct((na, 2 * cw, toks), BF16),
+            jax.ShapeDtypeStruct((na, (cw + 16) // 2, feats), BF16),
+            jax.ShapeDtypeStruct((na, (cw + 16) // 2, feats), BF16),
         ),
         cost_estimate=pl.CostEstimate(
             flops=4 * na * cw * feats * nb * toks,
-            bytes_accessed=2 * (weights.size + 2 * cot.size + normed.size + na * cw * feats),
+            bytes_accessed=2 * (weights.size + 4 * own.size + normed.size + na * cw * feats),
             transcendentals=0,
         ),
         compiler_params=pltpu.CompilerParams(vmem_limit_bytes=32 * 1024 * 1024),
-    )(weights, cot, normed)
-
-
-def finish_kernel(cw, fw, lines, sums_ref, done_ref, embed_ref, hidden_ref, gains_ref):
-    toks = done_ref.shape[1]
-    sums = sums_ref[...].astype(F32)
+    )(place, weights, own, other, normed)
+
+
+def finish_kernel(cw, toks, lines, top_ref, low_ref, done_ref, embed_ref, hidden_ref, gains_ref):
+    fw = embed_ref.shape[0]
+    sums = jnp.concatenate([top_ref[...].astype(F32), low_ref[...].astype(F32)], axis=0)
     turned = sums.T
     embed_ref[...] = turned[:fw, :cw]
     hidden_ref[...] = turned[fw:, :cw]
@@ -206,26 +250,31 @@
     gains_ref[1:2, :] = gains[:, fw : 2 * fw]
 
 
-def finish(sums, done, cw, fw, lines):
+def finish(top, low, done, cw, toks, lines):
+    fw = top.shape[1] // 2
     return pl.pallas_call(
-        functools.partial(finish_kernel, cw, fw, lines),
+        functools.partial(finish_kernel, cw, toks, lines),
         out_shape=(
             jax.ShapeDtypeStruct((fw, cw), F32),
             jax.ShapeDtypeStruct((fw, cw), F32),
             jax.ShapeDtypeStruct((2, fw), F32),
         ),
         cost_estimate=pl.CostEstimate(
-            flops=0, bytes_accessed=2 * sums.size + 8 * fw * cw, transcendentals=0
-        ),
-    )(sums, done)
+            flops=0, bytes_accessed=4 * top.size + 8 * fw * cw, transcendentals=0
+        ),
+    )(top, low, done)
 
 
 def per_device(ids, hidden, table, gain_embed, gain_hidden, proj_embed, proj_hidden, grad_out):
-    v = lax.axis_index("vocab")
-    nv = lax.axis_size("vocab")
+    core = lax.axis_index("core")
+    v = 2 * lax.axis_index("chip") + core
+    nc = lax.axis_size("chip")
+    nv = 2 * nc
     na, nb = lax.axis_size("z"), lax.axis_size("yhi")
     nd = na * nb
-    d = lax.axis_index("z") * nb + lax.axis_index("yhi")
+    yhi = lax.axis_index("yhi")
+    d = lax.axis_index("z") * nb + yhi
+    place = jnp.stack([core, yhi]).astype(jnp.int32)
     odd = d % 2 == 1
     toks, fw = hidden.shape
     cw, entries = table.shape
@@ -262,6 +311,9 @@
     def turn_back(c):
         return [(b, a) for a, b in turn(c)]
 
+    def flip(x):
+        return lax.ppermute(x, "core", [(0, 1), (1, 0)])
+
     weights = jnp.concatenate([proj_embed, proj_hidden], axis=0).T
     weights = gather(weights, "z", na)
 
@@ -275,19 +327,27 @@
         lax.ppermute(jnp.where(odd, first, second), ALL, turn(1)),
         0,
     )
-    cot = lax.all_gather(
-        jnp.concatenate([cot, jnp.pad(digits, ((0, 12), (0, 0)))], axis=0), "vocab"
-    )
-    digits = cot[:, fw : fw + 4].astype(jnp.int32)
-    all_ids = 256 * digits[:, 0::2] + digits[:, 1::2]
-    local_ids = (all_ids - v * entries).reshape(nv, 1, 2 * toks)
-
-    shares = grad_products(weights, cot, nb, cw, 2 * fw)
-    pieces, shares = lax.optimization_barrier((lookup(local_ids, table), shares))
-    grads = lax.psum_scatter(
-        shares.reshape(nb * 2 * fw, toks), "yhi", scatter_dimension=0, tiled=True
-    ).astype(F32)
-    pieces = lax.all_to_all(pieces, "vocab", 0, 0, tiled=True)
+    cot = jnp.concatenate([cot, jnp.pad(digits, ((0, 12), (0, 0)))], axis=0)
+    cot, weights = lax.optimization_barrier((cot, weights))
+    own = gather(cot, "chip", nc)
+    other = flip(own)
+
+    def ids_of(cot):
+        digits = cot[:, fw : fw + 4].astype(jnp.int32)
+        all_ids = 256 * digits[:, 0::2] + digits[:, 1::2]
+        return (all_ids - v * entries).reshape(nc, 1, 2 * toks)
+
+    own_ids, other_ids = ids_of(own), ids_of(other)
+
+    shares = grad_products(place, weights, own, other, nb)
+    grads = shares[0].astype(F32)
+    for k in range(1, nb):
+        grads += lax.ppermute(
+            shares[k], "yhi", [(i, (i + k) % nb) for i in range(nb)]
+        ).astype(F32)
+
+    pieces = lookup(own_ids, table) + flip(lookup(other_ids, table))
+    pieces = lax.all_to_all(pieces, "chip", 0, 0, tiled=True)
     cols = jnp.sum(pieces.astype(F32), axis=0).astype(BF16)
     first, second = cols[:, :toks], cols[:, toks:]
     embed = in_order(
@@ -308,7 +368,7 @@
             jnp.sum(dn_hidden * hid, axis=0),
         ]
     )
-    stats = jnp.sum(gather(stats, "vocab", nv), axis=0)
+    stats = jnp.sum(gather(stats + flip(stats), "chip", nc), axis=0)
     inv_embed = lax.rsqrt(stats[0] / full + EPS)[None]
     inv_hidden = lax.rsqrt(stats[1] / full + EPS)[None]
     norm_embed, norm_hidden = embed * inv_embed, hid * inv_hidden
@@ -347,30 +407,37 @@
     )
 
     normed, mine = lax.optimization_barrier((normed, mine))
-    terms, weight_terms = out_products(weights, cot, normed, cw, 2 * fw)
-    mine, weight_terms = lax.optimization_barrier((mine, weight_terms))
-    grad_table = scatter(local_ids, lax.all_gather(mine, "vocab"), entries)
-
-    terms = lax.all_to_all(terms, "vocab", 0, 0, tiled=True)
-    terms = jnp.sum(terms.astype(F32), axis=0).astype(BF16)
+    keep, send, top, low_half = out_products(place, weights, own, other, normed)
+    terms = (keep.astype(F32) + flip(send).astype(F32)).astype(BF16)
+    mine = jnp.broadcast_to(mine[None], (nc,) + mine.shape)
+    both = lax.all_to_all(
+        jnp.concatenate([terms, mine], axis=1), "chip", 0, 0, tiled=True
+    )
+    own_rows = both[:, fw:]
+    grad_table, done = scatter(
+        jnp.concatenate([own_ids, other_ids], axis=0), own_rows, flip(own_rows), entries
+    )
+
+    terms = jnp.sum(both[:, :fw].astype(F32), axis=0).astype(BF16)
     first, second = terms[:cw], terms[cw:]
     projected = in_order(
         lax.ppermute(jnp.where(odd, second, first), ALL, turn_back(0)),
         lax.ppermute(jnp.where(odd, first, second), ALL, turn_back(1)),
         0,
     )
-    weight_terms = lax.psum_scatter(
-        weight_terms.reshape(na * (cw + 16), 2 * fw), "z", scatter_dimension=0, tiled=True
-    )
-    grad_embed, grad_hid, grad_gains = finish(weight_terms, projected, cw, fw, lines)
+    top, low_half = (
+        lax.psum_scatter(x.reshape(-1, 2 * fw), "z", scatter_dimension=0, tiled=True)
+        for x in (top, low_half)
+    )
+    grad_embed, grad_hid, grad_gains = finish(top, low_half, done, cw, toks, lines)
     return (projected.T, grad_hidden.T, grad_table, grad_embed, grad_hid, grad_gains)
 
 
 def solution(mesh):
     nv, nd = mesh.shape["vocab"], mesh.shape["dp"]
     nb = min(4, nd)
-    split = Mesh(mesh.devices.reshape(nv, nd // nb, nb), ALL)
-    rows = P(DP, "vocab")
+    split = Mesh(mesh.devices.reshape(nv // 2, 2, nd // nb, nb), ALL)
+    rows = P(DP, VOCAB)
     return jax.shard_map(
         per_device,
         mesh=split,
@@ -378,12 +445,12 @@
             P(DP),
             rows,
             rows,
-            P("vocab"),
-            P("vocab"),
-            P("vocab", DP),
-            P("vocab", DP),
+            P(VOCAB),
+            P(VOCAB),
+            P(VOCAB, DP),
+            P(VOCAB, DP),
             rows,
         ),
-        out_specs=(rows, rows, rows, P("vocab", DP), P("vocab", DP), P(None, "vocab")),
+        out_specs=(rows, rows, rows, P(VOCAB, DP), P(VOCAB, DP), P(None, VOCAB)),
         check_vma=False,
     )

time: 218 us -> 258 us (1.18); the launches traced: 217 us -> 253 us
  waiting for transfers between devices: 30.7 us -> 79.6 us
  blocking collectives: 64.1 us -> 31 us
  starting transfers between devices: 82.4 us -> 99.4 us
    all_gather x2 -> x0, blocking collectives: 48.3 us -> none  [the longest x1 28.7 us: per_device(): grad_table = scatter(local_ids, lax.all_gather(mine, 'vocab'), entries)]
    reduce_scatter x2, waiting for transfers between devices: 8.9 us -> 42.3 us  [per_device(): lax.psum_scatter(x.reshape(-1, 2 * fw), 'z', scatter_dimension=0, tiled=T...]
    ppermute x0 -> x8, starting transfers between devices: none -> 24.1 us  [the longest x3 13.3 us: per_device(): lax.ppermute(shares[k], 'yhi', [(i, (i + k) % nb) for i in range(nb)])]
    all_to_all x1 -> x2, blocking collectives: 15.8 us -> 31 us  [gather(): lax.all_to_all(jnp.broadcast_to(x[None], (count,) + x.shape), axes, 0, 0,...]
    ppermute x1, waiting for transfers between devices: 0.01 us -> 7.25 us  [per_device(): lax.ppermute(jnp.where(odd, second, first), ALL, turn(0))]
    ppermute x1, starting transfers between devices: 8.25 us -> 3.13 us  [per_device(): lax.ppermute(jnp.where(odd, first, second), ALL, swap_route(1))]
    ppermute x1, waiting for transfers between devices: 0.01 us -> 4.42 us  [per_device(): lax.ppermute(jnp.where(odd, second, first), ALL, swap_route(0))]
    all_to_all x2, starting transfers between devices: 18.7 us -> 14.9 us  [gather(): lax.all_to_all(jnp.broadcast_to(x[None], (count,) + x.shape), axes, 0, 0,...]
  transfers between devices with their start and end apart: 16 -> 24, of which waited for: 4 -> 13; matrix products, arithmetic and copies ran while one was open for 2% -> 2% of each run, Pallas kernels for 5% -> 4%
where the time goes in v5:
time: 258 us; the launch traced here: 253 us
  starting transfers between devices  99.4 us (39%)
  waiting for transfers between devices  79.6 us (31%)
  blocking collectives  31 us (12%)
  Pallas kernels  17.4 us (7%)
  between operations  14.5 us (6%)
  other arithmetic  5.9 us (2%)
  local copies, waits for them, and re-layouts  4.75 us (2%)
    reduce_scatter x2, waiting for transfers between devices, per_device(): lax.psum_scatter(x.reshape(-1, 2 * fw), 'z', scatter_dimension=0, tiled=T...  42.3 us
    all_to_all x2, blocking collectives, gather(): lax.all_to_all(jnp.broadcast_to(x[None], (count,) + x.shape), axes, 0, 0,...  31 us
    all_to_all x2, starting transfers between devices, gather(): lax.all_to_all(jnp.broadcast_to(x[None], (count,) + x.shape), axes, 0, 0,...  14.9 us
    ppermute x3, starting transfers between devices, per_device(): lax.ppermute(shares[k], 'yhi', [(i, (i + k) % nb) for i in range(nb)])  13.3 us
    all_to_all x1, starting transfers between devices, per_device(): lax.all_to_all(jnp.concatenate([terms, mine], axis=1), 'chip', 0, 0, tile...  12.2 us
    all_to_all x1, waiting for transfers between devices, per_device(): lax.all_to_all(jnp.concatenate([terms, mine], axis=1), 'chip', 0, 0, tile...  12.1 us
    ppermute x5, starting transfers between devices, flip(): return lax.ppermute(x, 'core', [(0, 1), (1, 0)])  10.8 us
    ppermute x1, starting transfers between devices, per_device(): lax.ppermute(digits, ALL, swap_route(0))  8.29 us
  transfers between devices with their start and end apart: 24, of which 13 were waited for; matrix products, arithmetic and copies ran while one was open for 2% of the time, Pallas kernels for 4%

profile of v5, /device:TPU:1, one launch (start us, length us, event | category | flops | bytes accessed | tf_op | source)
XLA Modules:
  0.0 252.7 jit_solution(3633883718368415474)
XLA Ops:
  7.2 0.9 maximum_bitcast_fusion
  8.2 1.0 broadcast_in_dim.10
  9.2 10.9 %all-to-all-start = ((bf16[8,112,448]{2,1,0:T(8,128)(2,1)}), bf16[8,112,448]{2,1,0:T(8,128)(2,1)S(1)}, u32[]{:S(2)}, u32[]{:S(2)}) async-start(bf16[8,112,448]{2,1,0:T(8,128)(2,1)} %broadcast_in_dim.10), calls=%async_computation | async-start | bytes 1835008 | tf_op jit(solution)/shard_map/all_to_all | solution.py:21
  20.1 8.3 %collective-permute-start.3 = (bf16[2,128]{1,0:T(2,128)(2,1)S(1)}, bf16[2,128]{1,0:T(2,128)(2,1)S(1)}, u32[]{:S(2)}, u32[]{:S(2)}) collective-permute-start(bf16[2,128]{1,0:T(2,128)(2,1)S(1)} %pad_maximum_fusion.6), channel_id=1, source_target_pairs={{0,0},{1,1},{2,32},{3,33},{4,64},{5,65},{6,96},{7,97},{8,128},{9,1... | collective-permute-start | bytes 1544 | tf_op jit(solution)/shard_map/ppermute | solution.py:322
  28.4 1.9 collective-permute-start.2
  30.4 5.8 %collective-permute-start = (bf16[112,128]{1,0:T(8,128)(2,1)S(1)}, bf16[112,128]{1,0:T(8,128)(2,1)S(1)}, u32[]{:S(2)}, u32[]{:S(2)}) collective-permute-start(bf16[112,128]{1,0:T(8,128)(2,1)S(1)} %get-tuple-element.61), channel_id=1, source_target_pairs={{0,1},{1,0},{2,33},{3,32},{4,5},{5,4},{6,37},{7,36},{8,9},{9,8},{1... | collective-permute-start | bytes 86024 | tf_op jit(solution)/shard_map/ppermute | solution.py:327
  36.1 2.1 collective-permute-start.1
  38.4 7.2 %collective-permute-done.1 = bf16[112,128]{1,0:T(8,128)(2,1)S(1)} collective-permute-done((bf16[112,128]{1,0:T(8,128)(2,1)S(1)}, bf16[112,128]{1,0:T(8,128)(2,1)S(1)}, u32[]{:S(2)}, u32[]{:S(2)}) %collective-permute-start.1) | collective-permute-done | bytes 28704 | tf_op jit(solution)/shard_map/ppermute | solution.py:326
  45.6 0.8 all-to-all-done.weights_ref
  46.5 16.1 %all_to_all.30.own_ref = bf16[8,240,128]{2,1,0:T(8,128)(2,1)S(1)} all-to-all(bf16[8,240,128]{2,1,0:T(8,128)(2,1)S(1)} %broadcast_in_dim.11), channel_id=1, replica_groups=mesh['chip'=8,'core'=2,'z'=8,'yhi'=4] {'chip'}, dimensions={0} | all-to-all | bytes 983040 | tf_op jit(solution)/shard_map/all_to_all | solution.py:21
  62.6 1.9 collective-permute-start.4
  64.5 1.3 copy.28
  66.4 2.3 shard_map.128
  68.7 2.0 collective-permute-start.5
  70.8 2.3 shard_map.127
  73.1 0.9 add.65
  74.0 3.5 %all-to-all-start.2 = ((bf16[8,112,256]{2,1,0:T(8,128)(2,1)}), bf16[8,112,256]{2,1,0:T(8,128)(2,1)S(1)}, u32[]{:S(2)}, u32[]{:S(2)}) async-start(bf16[8,112,256]{2,1,0:T(8,128)(2,1)} %add.65), calls=%async_computation.2 | async-start | bytes 917504 | tf_op jit(solution)/shard_map/all_to_all | solution.py:350
  77.6 1.6 shard_map.129
  79.8 3.9 %collective-permute-start.8 = (bf16[448,128]{1,0:T(8,128)(2,1)}, bf16[448,128]{1,0:T(8,128)(2,1)S(1)}, u32[]{:S(2)}, u32[]{:S(2)}) collective-permute-start(bf16[448,128]{1,0:T(8,128)(2,1)} %get-tuple-element.40), channel_id=1, source_target_pairs={{0,1},{1,2},{2,3},{3,0},{4,5},{5,6},{6,7},{7,4},{8,9},{9,10},{10,1... | collective-permute-start | bytes 344072 | tf_op jit(solution)/shard_map/ppermute | solution.py:345
  83.7 3.5 %collective-permute-start.10 = (bf16[448,128]{1,0:T(8,128)(2,1)S(1)}, bf16[448,128]{1,0:T(8,128)(2,1)S(1)}, u32[]{:S(2)}, u32[]{:S(2)}) collective-permute-start(bf16[448,128]{1,0:T(8,128)(2,1)S(1)} %get-tuple-element.41), channel_id=1, source_target_pairs={{0,3},{1,0},{2,1},{3,2},{4,7},{5,4},{6,5},{7,6},{8,11},{9,8},{10,9... | collective-permute-start | bytes 344072 | tf_op jit(solution)/shard_map/ppermute | solution.py:345
  87.2 5.9 %collective-permute-start.9 = (bf16[448,128]{1,0:T(8,128)(2,1)S(1)}, bf16[448,128]{1,0:T(8,128)(2,1)}, u32[]{:S(2)}, u32[]{:S(2)}) collective-permute-start(bf16[448,128]{1,0:T(8,128)(2,1)S(1)} %get-tuple-element.42), channel_id=1, source_target_pairs={{0,2},{1,3},{2,0},{3,1},{4,6},{5,7},{6,4},{7,5},{8,10},{9,11},{10,... | collective-permute-start | bytes 344072 | tf_op jit(solution)/shard_map/ppermute | solution.py:345
  93.2 3.1 %collective-permute-start.6 = (bf16[112,128]{1,0:T(8,128)(2,1)S(1)}, bf16[112,128]{1,0:T(8,128)(2,1)S(1)}, u32[]{:S(2)}, u32[]{:S(2)}) collective-permute-start(bf16[112,128]{1,0:T(8,128)(2,1)S(1)} %get-tuple-element.57), channel_id=1, source_target_pairs={{0,1},{1,0},{2,33},{3,32},{4,65},{5,64},{6,97},{7,96},{8,129},{9,1... | collective-permute-start | bytes 86024 | tf_op jit(solution)/shard_map/ppermute | solution.py:355
  96.4 3.5 %collective-permute-start.7 = (bf16[112,128]{1,0:T(8,128)(2,1)S(1)}, bf16[112,128]{1,0:T(8,128)(2,1)S(1)}, u32[]{:S(2)}, u32[]{:S(2)}) collective-permute-start(bf16[112,128]{1,0:T(8,128)(2,1)S(1)} %get-tuple-element.58), channel_id=1, source_target_pairs={{0,0},{1,1},{2,32},{3,33},{4,64},{5,65},{6,96},{7,97},{8,128},{9,1... | collective-permute-start | bytes 86024 | tf_op jit(solution)/shard_map/ppermute | solution.py:354
  99.9 1.0 fusion.1
  101.0 4.4 %collective-permute-done.7 = bf16[112,128]{1,0:T(8,128)(2,1)S(1)} collective-permute-done((bf16[112,128]{1,0:T(8,128)(2,1)S(1)}, bf16[112,128]{1,0:T(8,128)(2,1)S(1)}, u32[]{:S(2)}, u32[]{:S(2)}) %collective-permute-start.7) | collective-permute-done | bytes 28704 | tf_op jit(solution)/shard_map/ppermute | solution.py:354
  105.7 1.9 collective-permute-start.11
  107.6 1.1 collective-permute-done.11
  108.7 14.9 %all_to_all.31 = f32[8,4,128]{2,1,0:T(4,128)S(1)} all-to-all(f32[8,4,128]{2,1,0:T(4,128)S(1)} %broadcast_in_dim.12), channel_id=1, replica_groups=mesh['chip'=8,'core'=2,'z'=8,'yhi'=4] {'chip'}, dimensions={0} | all-to-all | bytes 32768 | tf_op jit(solution)/shard_map/all_to_all | solution.py:21
  123.7 0.8 fusion.6
  124.6 0.8 broadcast_in_dim.13
  125.4 4.0 %all-to-all-start.4 = ((bf16[4,480,128]{2,1,0:T(8,128)(2,1)}), bf16[4,480,128]{2,1,0:T(8,128)(2,1)S(1)}, u32[]{:S(2)}, u32[]{:S(2)}) async-start(bf16[4,480,128]{2,1,0:T(8,128)(2,1)} %broadcast_in_dim.13), calls=%async_computation.4 | async-start | bytes 983040 | tf_op jit(solution)/shard_map/all_to_all | solution.py:21
  129.4 7.7 %collective-permute-start.12 = (bf16[112,128]{1,0:T(8,128)(2,1)S(1)}, bf16[112,128]{1,0:T(8,128)(2,1)S(1)}, u32[]{:S(2)}, u32[]{:S(2)}) collective-permute-start(bf16[112,128]{1,0:T(8,128)(2,1)S(1)} %get-tuple-element.53), channel_id=1, source_target_pairs={{1,0},{0,1},{33,2},{32,3},{65,4},{64,5},{97,6},{96,7},{129,8},{128... | collective-permute-start | bytes 86024 | tf_op jit(solution)/shard_map/ppermute | solution.py:405
  137.1 3.7 %collective-permute-start.13 = (bf16[112,128]{1,0:T(8,128)(2,1)S(1)}, bf16[112,128]{1,0:T(8,128)(2,1)S(1)}, u32[]{:S(2)}, u32[]{:S(2)}) collective-permute-start(bf16[112,128]{1,0:T(8,128)(2,1)S(1)} %get-tuple-element.54), channel_id=1, source_target_pairs={{0,0},{1,1},{32,2},{33,3},{64,4},{65,5},{96,6},{97,7},{128,8},{129... | collective-permute-start | bytes 86024 | tf_op jit(solution)/shard_map/ppermute | solution.py:404
  140.9 3.8 %collective-permute-done.12 = bf16[112,128]{1,0:T(8,128)(2,1)S(1)} collective-permute-done((bf16[112,128]{1,0:T(8,128)(2,1)S(1)}, bf16[112,128]{1,0:T(8,128)(2,1)S(1)}, u32[]{:S(2)}, u32[]{:S(2)}) %collective-permute-start.12) | collective-permute-done | bytes 28704 | tf_op jit(solution)/shard_map/ppermute | solution.py:405
  144.7 1.9 collective-permute-done.13
  146.6 3.1 %shard_map.130 = (bf16[8,224,128]{2,1,0:T(8,128)(2,1)S(1)}, bf16[8,224,128]{2,1,0:T(8,128)(2,1)S(1)}, bf16[8,64,448]{2,1,0:T(8,128)(2,1)}, bf16[8,64,448]{2,1,0:T(8,128)(2,1)}) custom-call(s32[2]{0:T(128)S(1)} %pad_add_fusion.1.place_ref, bf16[8,112,448]{2,1,0:T(8,128)(2,1)S(1)} %all-to-all-done.weights_ref, bf16[8,240,128]{2,1,0:T(8,128)(2,1)S(1)} %all_to_all.30.own_ref, ...), custom_call_target="tpu_custom_call" | custom-call | flops 822083584 | bytes 4063232 | tf_op jit(solution)/shard_map/pallas_call | solution.py:222
  149.8 2.2 collective-permute-start.14
  152.0 1.5 collective-permute-done.14
  153.6 1.0 pad_maximum_fusion
  154.6 12.2 %all-to-all-start.5 = ((bf16[8,448,128]{2,1,0:T(8,128)(2,1)}), bf16[8,448,128]{2,1,0:T(8,128)(2,1)S(1)}, u32[]{:S(2)}, u32[]{:S(2)}) async-start(bf16[8,448,128]{2,1,0:T(8,128)(2,1)} %pad_maximum_fusion), calls=%async_computation.5 | async-start | bytes 1835008 | tf_op jit(solution)/shard_map/all_to_all | solution.py:413
  168.3 12.1 %all-to-all-done.5 = bf16[8,448,128]{2,1,0:T(8,128)(2,1)S(1)} async-done(((bf16[8,448,128]{2,1,0:T(8,128)(2,1)}), bf16[8,448,128]{2,1,0:T(8,128)(2,1)S(1)}, u32[]{:S(2)}, u32[]{:S(2)}) %all-to-all-start.5) | async-done | bytes 917536 | tf_op jit(solution)/shard_map/all_to_all | solution.py:413
  180.4 2.7 %collective-permute-start.17 = (bf16[8,224,128]{2,1,0:T(8,128)(2,1)S(1)}, bf16[8,224,128]{2,1,0:T(8,128)(2,1)S(1)}, u32[]{:S(2)}, u32[]{:S(2)}) collective-permute-start(bf16[8,224,128]{2,1,0:T(8,128)(2,1)S(1)} %get-tuple-element.38.own_ref), channel_id=1, source_target_pairs={{0,32},{32,0},{1,33},{33,1},{2,34},{34,2},{3,35},{35,3},{4,36},{36... | collective-permute-start | bytes 1376264 | tf_op jit(solution)/shard_map/ppermute | solution.py:315
  183.1 1.9 collective-permute-start.15
  185.1 6.7 %collective-permute-start.16 = (bf16[112,128]{1,0:T(8,128)(2,1)S(1)}, bf16[112,128]{1,0:T(8,128)(2,1)S(1)}, u32[]{:S(2)}, u32[]{:S(2)}) collective-permute-start(bf16[112,128]{1,0:T(8,128)(2,1)S(1)} %get-tuple-element.50), channel_id=1, source_target_pairs={{0,0},{1,1},{32,2},{33,3},{4,4},{5,5},{36,6},{37,7},{8,8},{9,9},{4... | collective-permute-start | bytes 86024 | tf_op jit(solution)/shard_map/ppermute | solution.py:424
  191.8 2.4 collective-permute-done.16
  194.8 6.5 %shard_map.131 = (f32[112,4096]{1,0:T(8,128)}, f32[8,128]{1,0:T(8,128)S(1)}) custom-call(s32[16,1,256]{2,1,0:T(1,128)S(1)} %pad_add_fusion.ids_ref, bf16[8,224,128]{2,1,0:T(8,128)(2,1)S(1)} %get-tuple-element.38.own_ref, bf16[8,224,128]{2,1,0:T(8,128)(2,1)S(1)} %collective-permute-done.17.other_ref), custom_call_target="tpu_custom_call" | custom-call | flops 3758096384 | bytes 2752512 | tf_op jit(solution)/shard_map/pallas_call | solution.py:117
  202.3 41.9 %reduce-scatter.5.cloned.1.call-done.low_ref = bf16[64,448]{1,0:T(8,128)(2,1)} async-done(((bf16[512,448]{1,0:T(8,128)(2,1)}), bf16[64,448]{1,0:T(8,128)(2,1)}) %reduce-scatter.5.cloned.1.call-update) | async-done | bytes 57360 | tf_op jit(solution)/shard_map/reduce_scatter | solution.py:429
  244.2 1.7 shard_map.132
  (71 shorter events, 5.6 us)
Async XLA Ops:
  7.2 12.9 %copy-start.5 = (s32[128]{0:T(128)S(1)}, s32[128]{0:T(128)}, u32[]{:S(2)}) copy-start(s32[128]{0:T(128)} %param.8) | copy-start | bytes 1540
  7.2 23.2 %copy-start.2 = (bf16[128,224]{0,1:T(8,128)(2,1)S(1)}, bf16[128,224]{0,1:T(8,128)(2,1)}, u32[]{:S(2)}) copy-start(bf16[128,224]{0,1:T(8,128)(2,1)} %param.15) | copy-start | bytes 172036
  9.2 37.2 %all-to-all-start = ((bf16[8,112,448]{2,1,0:T(8,128)(2,1)}), bf16[8,112,448]{2,1,0:T(8,128)(2,1)S(1)}, u32[]{:S(2)}, u32[]{:S(2)}) async-start(bf16[8,112,448]{2,1,0:T(8,128)(2,1)} %broadcast_in_dim.10), calls=%async_computation | async-start | bytes 1835008 | tf_op jit(solution)/shard_map/all_to_all | solution.py:21
  20.1 18.2 %collective-permute-start.3 = (bf16[2,128]{1,0:T(2,128)(2,1)S(1)}, bf16[2,128]{1,0:T(2,128)(2,1)S(1)}, u32[]{:S(2)}, u32[]{:S(2)}) collective-permute-start(bf16[2,128]{1,0:T(2,128)(2,1)S(1)} %pad_maximum_fusion.6), channel_id=1, source_target_pairs={{0,0},{1,1},{2,32},{3,33},{4,64},{5,65},{6,96},{7,97},{8,128},{9,1... | collective-permute-start | bytes 1544 | tf_op jit(solution)/shard_map/ppermute | solution.py:322
  28.4 9.9 %collective-permute-start.2 = (bf16[2,128]{1,0:T(2,128)(2,1)S(1)}, bf16[2,128]{1,0:T(2,128)(2,1)S(1)}, u32[]{:S(2)}, u32[]{:S(2)}) collective-permute-start(bf16[2,128]{1,0:T(2,128)(2,1)S(1)} %pad_maximum_fusion.6), channel_id=1, source_target_pairs={{0,1},{1,0},{2,33},{3,32},{4,65},{5,64},{6,97},{7,96},{8,129},{9,1... | collective-permute-start | bytes 1544 | tf_op jit(solution)/shard_map/ppermute | solution.py:322
  30.4 8.0 %collective-permute-start = (bf16[112,128]{1,0:T(8,128)(2,1)S(1)}, bf16[112,128]{1,0:T(8,128)(2,1)S(1)}, u32[]{:S(2)}, u32[]{:S(2)}) collective-permute-start(bf16[112,128]{1,0:T(8,128)(2,1)S(1)} %get-tuple-element.61), channel_id=1, source_target_pairs={{0,1},{1,0},{2,33},{3,32},{4,5},{5,4},{6,37},{7,36},{8,9},{9,8},{1... | collective-permute-start | bytes 86024 | tf_op jit(solution)/shard_map/ppermute | solution.py:327
  36.1 9.5 %collective-permute-start.1 = (bf16[112,128]{1,0:T(8,128)(2,1)S(1)}, bf16[112,128]{1,0:T(8,128)(2,1)S(1)}, u32[]{:S(2)}, u32[]{:S(2)}) collective-permute-start(bf16[112,128]{1,0:T(8,128)(2,1)S(1)} %get-tuple-element.62), channel_id=1, source_target_pairs={{0,0},{1,1},{2,32},{3,33},{4,4},{5,5},{6,36},{7,37},{8,8},{9,9},{1... | collective-permute-start | bytes 86024 | tf_op jit(solution)/shard_map/ppermute | solution.py:326
  62.6 3.7 %collective-permute-start.4 = (bf16[8,240,128]{2,1,0:T(8,128)(2,1)S(1)}, bf16[8,240,128]{2,1,0:T(8,128)(2,1)S(1)}, u32[]{:S(2)}, u32[]{:S(2)}) collective-permute-start(bf16[8,240,128]{2,1,0:T(8,128)(2,1)S(1)} %all_to_all.30.own_ref), channel_id=1, source_target_pairs={{0,32},{32,0},{1,33},{33,1},{2,34},{34,2},{3,35},{35,3},{4,36},{36... | collective-permute-start | bytes 1474568 | tf_op jit(solution)/shard_map/ppermute | solution.py:315
  68.7 4.4 %collective-permute-start.5 = (bf16[8,112,256]{2,1,0:T(8,128)(2,1)S(1)}, bf16[8,112,256]{2,1,0:T(8,128)(2,1)S(1)}, u32[]{:S(2)}, u32[]{:S(2)}) collective-permute-start(bf16[8,112,256]{2,1,0:T(8,128)(2,1)S(1)} %shard_map.128), channel_id=1, source_target_pairs={{0,32},{32,0},{1,33},{33,1},{2,34},{34,2},{3,35},{35,3},{4,36},{36... | collective-permute-start | bytes 1376264 | tf_op jit(solution)/shard_map/ppermute | solution.py:315
  74.0 19.1 %all-to-all-start.2 = ((bf16[8,112,256]{2,1,0:T(8,128)(2,1)}), bf16[8,112,256]{2,1,0:T(8,128)(2,1)S(1)}, u32[]{:S(2)}, u32[]{:S(2)}) async-start(bf16[8,112,256]{2,1,0:T(8,128)(2,1)} %add.65), calls=%async_computation.2 | async-start | bytes 917504 | tf_op jit(solution)/shard_map/all_to_all | solution.py:350
  77.6 27.9 %copy-start.1 = (bf16[128,224]{0,1:T(8,128)(2,1)S(1)}, bf16[128,224]{0,1:T(8,128)(2,1)}, u32[]{:S(2)}) copy-start(bf16[128,224]{0,1:T(8,128)(2,1)} %param.9) | copy-start | bytes 172036
  77.6 27.9 %copy-start.3 = (f32[224]{0:T(256)S(1)}, f32[224]{0:T(256)}, u32[]{:S(2)}) copy-start(f32[224]{0:T(256)} %param.11) | copy-start | bytes 2692
  77.6 27.9 %copy-start.4 = (f32[224]{0:T(256)S(1)}, f32[224]{0:T(256)}, u32[]{:S(2)}) copy-start(f32[224]{0:T(256)} %param.12) | copy-start | bytes 2692
  79.8 20.1 %collective-permute-start.8 = (bf16[448,128]{1,0:T(8,128)(2,1)}, bf16[448,128]{1,0:T(8,128)(2,1)S(1)}, u32[]{:S(2)}, u32[]{:S(2)}) collective-permute-start(bf16[448,128]{1,0:T(8,128)(2,1)} %get-tuple-element.40), channel_id=1, source_target_pairs={{0,1},{1,2},{2,3},{3,0},{4,5},{5,6},{6,7},{7,4},{8,9},{9,10},{10,1... | collective-permute-start | bytes 344072 | tf_op jit(solution)/shard_map/ppermute | solution.py:345
  83.7 16.1 %collective-permute-start.10 = (bf16[448,128]{1,0:T(8,128)(2,1)S(1)}, bf16[448,128]{1,0:T(8,128)(2,1)S(1)}, u32[]{:S(2)}, u32[]{:S(2)}) collective-permute-start(bf16[448,128]{1,0:T(8,128)(2,1)S(1)} %get-tuple-element.41), channel_id=1, source_target_pairs={{0,3},{1,0},{2,1},{3,2},{4,7},{5,4},{6,5},{7,6},{8,11},{9,8},{10,9... | collective-permute-start | bytes 344072 | tf_op jit(solution)/shard_map/ppermute | solution.py:345
  87.2 12.7 %collective-permute-start.9 = (bf16[448,128]{1,0:T(8,128)(2,1)S(1)}, bf16[448,128]{1,0:T(8,128)(2,1)}, u32[]{:S(2)}, u32[]{:S(2)}) collective-permute-start(bf16[448,128]{1,0:T(8,128)(2,1)S(1)} %get-tuple-element.42), channel_id=1, source_target_pairs={{0,2},{1,3},{2,0},{3,1},{4,6},{5,7},{6,4},{7,5},{8,10},{9,11},{10,... | collective-permute-start | bytes 344072 | tf_op jit(solution)/shard_map/ppermute | solution.py:345
  93.2 7.8 %collective-permute-start.6 = (bf16[112,128]{1,0:T(8,128)(2,1)S(1)}, bf16[112,128]{1,0:T(8,128)(2,1)S(1)}, u32[]{:S(2)}, u32[]{:S(2)}) collective-permute-start(bf16[112,128]{1,0:T(8,128)(2,1)S(1)} %get-tuple-element.57), channel_id=1, source_target_pairs={{0,1},{1,0},{2,33},{3,32},{4,65},{5,64},{6,97},{7,96},{8,129},{9,1... | collective-permute-start | bytes 86024 | tf_op jit(solution)/shard_map/ppermute | solution.py:355
  96.4 9.1 %collective-permute-start.7 = (bf16[112,128]{1,0:T(8,128)(2,1)S(1)}, bf16[112,128]{1,0:T(8,128)(2,1)S(1)}, u32[]{:S(2)}, u32[]{:S(2)}) collective-permute-start(bf16[112,128]{1,0:T(8,128)(2,1)S(1)} %get-tuple-element.58), channel_id=1, source_target_pairs={{0,0},{1,1},{2,32},{3,33},{4,64},{5,65},{6,96},{7,97},{8,128},{9,1... | collective-permute-start | bytes 86024 | tf_op jit(solution)/shard_map/ppermute | solution.py:354
  105.7 3.1 %collective-permute-start.11 = (f32[4,128]{1,0:T(4,128)S(1)}, f32[4,128]{1,0:T(4,128)S(1)}, u32[]{:S(2)}, u32[]{:S(2)}) collective-permute-start(f32[4,128]{1,0:T(4,128)S(1)} %pad_maximum_fusion.5), channel_id=1, source_target_pairs={{0,32},{32,0},{1,33},{33,1},{2,34},{34,2},{3,35},{35,3},{4,36},{36... | collective-permute-start | bytes 6152 | tf_op jit(solution)/shard_map/ppermute | solution.py:315
  125.4 21.2 %all-to-all-start.4 = ((bf16[4,480,128]{2,1,0:T(8,128)(2,1)}), bf16[4,480,128]{2,1,0:T(8,128)(2,1)S(1)}, u32[]{:S(2)}, u32[]{:S(2)}) async-start(bf16[4,480,128]{2,1,0:T(8,128)(2,1)} %broadcast_in_dim.13), calls=%async_computation.4 | async-start | bytes 983040 | tf_op jit(solution)/shard_map/all_to_all | solution.py:21
  129.4 15.2 %collective-permute-start.12 = (bf16[112,128]{1,0:T(8,128)(2,1)S(1)}, bf16[112,128]{1,0:T(8,128)(2,1)S(1)}, u32[]{:S(2)}, u32[]{:S(2)}) collective-permute-start(bf16[112,128]{1,0:T(8,128)(2,1)S(1)} %get-tuple-element.53), channel_id=1, source_target_pairs={{1,0},{0,1},{33,2},{32,3},{65,4},{64,5},{97,6},{96,7},{129,8},{128... | collective-permute-start | bytes 86024 | tf_op jit(solution)/shard_map/ppermute | solution.py:405
  137.1 9.5 %collective-permute-start.13 = (bf16[112,128]{1,0:T(8,128)(2,1)S(1)}, bf16[112,128]{1,0:T(8,128)(2,1)S(1)}, u32[]{:S(2)}, u32[]{:S(2)}) collective-permute-start(bf16[112,128]{1,0:T(8,128)(2,1)S(1)} %get-tuple-element.54), channel_id=1, source_target_pairs={{0,0},{1,1},{32,2},{33,3},{64,4},{65,5},{96,6},{97,7},{128,8},{129... | collective-permute-start | bytes 86024 | tf_op jit(solution)/shard_map/ppermute | solution.py:404
  149.8 3.7 %collective-permute-start.14 = (bf16[8,224,128]{2,1,0:T(8,128)(2,1)S(1)}, bf16[8,224,128]{2,1,0:T(8,128)(2,1)S(1)}, u32[]{:S(2)}, u32[]{:S(2)}) collective-permute-start(bf16[8,224,128]{2,1,0:T(8,128)(2,1)S(1)} %get-tuple-element.23), channel_id=1, source_target_pairs={{0,32},{32,0},{1,33},{33,1},{2,34},{34,2},{3,35},{35,3},{4,36},{36... | collective-permute-start | bytes 1376264 | tf_op jit(solution)/shard_map/ppermute | solution.py:315
  154.6 25.7 %all-to-all-start.5 = ((bf16[8,448,128]{2,1,0:T(8,128)(2,1)}), bf16[8,448,128]{2,1,0:T(8,128)(2,1)S(1)}, u32[]{:S(2)}, u32[]{:S(2)}) async-start(bf16[8,448,128]{2,1,0:T(8,128)(2,1)} %pad_maximum_fusion), calls=%async_computation.5 | async-start | bytes 1835008 | tf_op jit(solution)/shard_map/all_to_all | solution.py:413
  166.8 35.5 %reduce-scatter.3.cloned.1.call-start = ((), (), s32[]{:S(2)}) async-start(), calls=%async_computation.8 | async-start | bytes 589824 | tf_op jit(solution)/shard_map/reduce_scatter | solution.py:429
  167.5 76.7 %reduce-scatter.5.cloned.1.call-start = ((), (), s32[]{:S(2)}) async-start(), calls=%async_computation.9 | async-start | bytes 589824 | tf_op jit(solution)/shard_map/reduce_scatter | solution.py:429
  180.4 14.4 %collective-permute-start.17 = (bf16[8,224,128]{2,1,0:T(8,128)(2,1)S(1)}, bf16[8,224,128]{2,1,0:T(8,128)(2,1)S(1)}, u32[]{:S(2)}, u32[]{:S(2)}) collective-permute-start(bf16[8,224,128]{2,1,0:T(8,128)(2,1)S(1)} %get-tuple-element.38.own_ref), channel_id=1, source_target_pairs={{0,32},{32,0},{1,33},{33,1},{2,34},{34,2},{3,35},{35,3},{4,36},{36... | collective-permute-start | bytes 1376264 | tf_op jit(solution)/shard_map/ppermute | solution.py:315
  183.1 8.6 %collective-permute-start.15 = (bf16[112,128]{1,0:T(8,128)(2,1)S(1)}, bf16[112,128]{1,0:T(8,128)(2,1)S(1)}, u32[]{:S(2)}, u32[]{:S(2)}) collective-permute-start(bf16[112,128]{1,0:T(8,128)(2,1)S(1)} %get-tuple-element.49), channel_id=1, source_target_pairs={{1,0},{0,1},{33,2},{32,3},{5,4},{4,5},{37,6},{36,7},{9,8},{8,9},{4... | collective-permute-start | bytes 86024 | tf_op jit(solution)/shard_map/ppermute | solution.py:425
  185.1 9.1 %collective-permute-start.16 = (bf16[112,128]{1,0:T(8,128)(2,1)S(1)}, bf16[112,128]{1,0:T(8,128)(2,1)S(1)}, u32[]{:S(2)}, u32[]{:S(2)}) collective-permute-start(bf16[112,128]{1,0:T(8,128)(2,1)S(1)} %get-tuple-element.50), channel_id=1, source_target_pairs={{0,0},{1,1},{32,2},{33,3},{4,4},{5,5},{36,6},{37,7},{8,8},{9,9},{4... | collective-permute-start | bytes 86024 | tf_op jit(solution)/shard_map/ppermute | solution.py:424
  201.3 0.6 copy-start
Sparse Core Ops, SparseCore 0:
  170.4 31.8 reduce-scatter.2
  205.3 38.8 reduce-scatter.4

commit v6 on v5

--- a/solution.py
+++ b/solution.py
@@ -10,6 +10,7 @@
 
 EPS = 1e-06
 GROUPS = 8
+PAD_ROWS = 80
 BF16 = jnp.bfloat16
 F32 = jnp.float32
 DP = ("z", "yhi")
@@ -131,8 +132,8 @@
             jax.ShapeDtypeStruct((8, 128), F32),
         ),
         cost_estimate=pl.CostEstimate(
-            flops=8 * blocks * toks * cols * entries,
-            bytes_accessed=cols * (4 * entries + 8 * blocks * toks),
+            flops=0,
+            bytes_accessed=0,
             transcendentals=0,
         ),
         compiler_params=pltpu.CompilerParams(vmem_limit_bytes=32 * 1024 * 1024),
@@ -181,7 +182,7 @@
 
 
 def out_kernel(
-    place_ref, weights_ref, own_ref, other_ref, normed_ref, keep_ref, send_ref, top_ref, low_ref
+    place_ref, weights_ref, own_ref, other_ref, normed_ref, keep_ref, send_ref, sums_ref
 ):
     na, cw, feats = weights_ref.shape
     nb, _, toks = normed_ref.shape
@@ -207,12 +208,10 @@
     for b in range(nb):
         gains += normed_ref[b, feats : feats + 16].astype(F32)
         gains += normed_ref[b, feats + 16 : feats + 32].astype(F32)
-    half = top_ref.shape[1]
     for a in range(na):
-        top_ref[a] = sums[a * cw : a * cw + half]
-        low_ref[a, : cw - half] = sums[a * cw + half : (a + 1) * cw]
-        low_ref[a, cw - half :] = jnp.zeros((16, feats), BF16)
-        low_ref[a, cw - half :, :toks] = gains.astype(BF16)
+        sums_ref[a, :cw] = sums[a * cw : (a + 1) * cw]
+        sums_ref[a, cw:] = jnp.zeros((PAD_ROWS, feats), BF16)
+        sums_ref[a, cw : cw + 16, :toks] = gains.astype(BF16)
 
 
 def out_products(place, weights, own, other, normed):
@@ -225,8 +224,7 @@
         out_shape=(
             jax.ShapeDtypeStruct((na, 2 * cw, toks), BF16),
             jax.ShapeDtypeStruct((na, 2 * cw, toks), BF16),
-            jax.ShapeDtypeStruct((na, (cw + 16) // 2, feats), BF16),
-            jax.ShapeDtypeStruct((na, (cw + 16) // 2, feats), BF16),
+            jax.ShapeDtypeStruct((na, cw + PAD_ROWS, feats), BF16),
         ),
         cost_estimate=pl.CostEstimate(
             flops=4 * na * cw * feats * nb * toks,
@@ -237,12 +235,18 @@
     )(place, weights, own, other, normed)
 
 
-def finish_kernel(cw, toks, lines, top_ref, low_ref, done_ref, embed_ref, hidden_ref, gains_ref):
-    fw = embed_ref.shape[0]
-    sums = jnp.concatenate([top_ref[...].astype(F32), low_ref[...].astype(F32)], axis=0)
-    turned = sums.T
-    embed_ref[...] = turned[:fw, :cw]
-    hidden_ref[...] = turned[fw:, :cw]
+def finish_kernel(
+    lines, place_ref, sums_ref, got0_ref, got1_ref, done_ref, out_ref, embed_ref, hidden_ref, gains_ref
+):
+    fw, cw = embed_ref.shape
+    toks = out_ref.shape[1]
+    odd = lax.rem(place_ref[1], 2) == 1
+    out_ref[:cw] = jnp.where(odd, got1_ref[...], got0_ref[...])
+    out_ref[cw:] = jnp.where(odd, got0_ref[...], got1_ref[...])
+    sums = sums_ref[...].astype(F32)
+    turned = sums[:cw].T
+    embed_ref[...] = turned[:fw]
+    hidden_ref[...] = turned[fw:]
     gains = jnp.concatenate(
         [sums[cw + i : cw + i + 1, :toks] for i in range(lines)], axis=1
     )
@@ -250,19 +254,23 @@
     gains_ref[1:2, :] = gains[:, fw : 2 * fw]
 
 
-def finish(top, low, done, cw, toks, lines):
-    fw = top.shape[1] // 2
+def finish(place, sums, got0, got1, done, lines):
+    fw = sums.shape[1] // 2
+    cw, toks = got0.shape
+    whole = pl.BlockSpec(memory_space=pltpu.VMEM)
     return pl.pallas_call(
-        functools.partial(finish_kernel, cw, toks, lines),
+        functools.partial(finish_kernel, lines),
+        in_specs=[pl.BlockSpec(memory_space=pltpu.SMEM), whole, whole, whole, whole],
         out_shape=(
+            jax.ShapeDtypeStruct((2 * cw, toks), BF16),
             jax.ShapeDtypeStruct((fw, cw), F32),
             jax.ShapeDtypeStruct((fw, cw), F32),
             jax.ShapeDtypeStruct((2, fw), F32),
         ),
         cost_estimate=pl.CostEstimate(
-            flops=0, bytes_accessed=4 * top.size + 8 * fw * cw, transcendentals=0
-        ),
-    )(top, low, done)
+            flops=0, bytes_accessed=2 * sums.size + 8 * fw * cw, transcendentals=0
+        ),
+    )(place, sums, got0, got1, done)
 
 
 def per_device(ids, hidden, table, gain_embed, gain_hidden, proj_embed, proj_hidden, grad_out):
@@ -407,7 +415,7 @@
     )
 
     normed, mine = lax.optimization_barrier((normed, mine))
-    keep, send, top, low_half = out_products(place, weights, own, other, normed)
+    keep, send, weight_terms = out_products(place, weights, own, other, normed)
     terms = (keep.astype(F32) + flip(send).astype(F32)).astype(BF16)
     mine = jnp.broadcast_to(mine[None], (nc,) + mine.shape)
     both = lax.all_to_all(
@@ -420,16 +428,14 @@
 
     terms = jnp.sum(both[:, :fw].astype(F32), axis=0).astype(BF16)
     first, second = terms[:cw], terms[cw:]
-    projected = in_order(
-        lax.ppermute(jnp.where(odd, second, first), ALL, turn_back(0)),
-        lax.ppermute(jnp.where(odd, first, second), ALL, turn_back(1)),
-        0,
-    )
-    top, low_half = (
-        lax.psum_scatter(x.reshape(-1, 2 * fw), "z", scatter_dimension=0, tiled=True)
-        for x in (top, low_half)
-    )
-    grad_embed, grad_hid, grad_gains = finish(top, low_half, done, cw, toks, lines)
+    got0 = lax.ppermute(jnp.where(odd, second, first), ALL, turn_back(0))
+    got1 = lax.ppermute(jnp.where(odd, first, second), ALL, turn_back(1))
+    weight_terms = lax.psum_scatter(
+        weight_terms.reshape(na * (cw + PAD_ROWS), 2 * fw), "z", scatter_dimension=0, tiled=True
+    )
+    projected, grad_embed, grad_hid, grad_gains = finish(
+        place, weight_terms, got0, got1, done, lines
+    )
     return (projected.T, grad_hidden.T, grad_table, grad_embed, grad_hid, grad_gains)
 
 

time: 258 us -> 209 us (0.81); the launches traced: 253 us -> 208 us
  waiting for transfers between devices: 79.6 us -> 21.7 us
  blocking collectives: 31 us -> 56.6 us
  starting transfers between devices: 99.4 us -> 88 us
    reduce_scatter x2 -> x1, waiting for transfers between devices: 42.3 us -> 0.02 us  [per_device(): lax.psum_scatter(weight_terms.reshape(na * (cw + PAD_ROWS), 2 * fw), 'z',...]
    all_to_all x0 -> x1, blocking collectives: none -> 25.6 us  [per_device(): lax.all_to_all(jnp.concatenate([terms, mine], axis=1), 'chip', 0, 0, tile...]
    all_to_all x1 -> x0, starting transfers between devices: 12.2 us -> none  [per_device(): lax.all_to_all(jnp.concatenate([terms, mine], axis=1), 'chip', 0, 0, tile...]
    all_to_all x1 -> x0, waiting for transfers between devices: 12.1 us -> none  [per_device(): lax.all_to_all(jnp.concatenate([terms, mine], axis=1), 'chip', 0, 0, tile...]
  transfers between devices with their start and end apart: 24 -> 22, of which waited for: 13 -> 9; matrix products, arithmetic and copies ran while one was open for 2% -> 2% of each run, Pallas kernels for 4% -> 5%
where the time goes in v6:
time: 209 us; the launch traced here: 208 us
  starting transfers between devices  88 us (42%)
  blocking collectives  56.6 us (27%)
  waiting for transfers between devices  21.7 us (10%)
  Pallas kernels  17.8 us (9%)
  between operations  14.6 us (7%)
  local copies, waits for them, and re-layouts  5.34 us (3%)
  other arithmetic  4.34 us (2%)
    all_to_all x2, blocking collectives, gather(): lax.all_to_all(jnp.broadcast_to(x[None], (count,) + x.shape), axes, 0, 0,...  31 us
    all_to_all x1, blocking collectives, per_device(): lax.all_to_all(jnp.concatenate([terms, mine], axis=1), 'chip', 0, 0, tile...  25.6 us
    all_to_all x2, starting transfers between devices, gather(): lax.all_to_all(jnp.broadcast_to(x[None], (count,) + x.shape), axes, 0, 0,...  14.9 us
    ppermute x3, starting transfers between devices, per_device(): lax.ppermute(shares[k], 'yhi', [(i, (i + k) % nb) for i in range(nb)])  13.3 us
    ppermute x5, starting transfers between devices, flip(): return lax.ppermute(x, 'core', [(0, 1), (1, 0)])  11.6 us
    ppermute x1, starting transfers between devices, per_device(): lax.ppermute(digits, ALL, swap_route(0))  8.29 us
    ppermute x1, starting transfers between devices, per_device(): lax.ppermute(jnp.where(odd, low, high), ALL, swap_back(1))  7.69 us
    ppermute x1, waiting for transfers between devices, per_device(): lax.ppermute(jnp.where(odd, second, first), ALL, turn(0))  7.25 us
  transfers between devices with their start and end apart: 22, of which 9 were waited for; matrix products, arithmetic and copies ran while one was open for 2% of the time, Pallas kernels for 5%

profile of v6, /device:TPU:1, one launch (start us, length us, event | category | flops | bytes accessed | tf_op | source)
XLA Modules:
  0.0 208.4 jit_solution(15761857730238754390)
XLA Ops:
  7.2 0.9 maximum_bitcast_fusion
  8.2 1.0 broadcast_in_dim.10
  9.2 10.9 %all-to-all-start = ((bf16[8,112,448]{2,1,0:T(8,128)(2,1)}), bf16[8,112,448]{2,1,0:T(8,128)(2,1)S(1)}, u32[]{:S(2)}, u32[]{:S(2)}) async-start(bf16[8,112,448]{2,1,0:T(8,128)(2,1)} %broadcast_in_dim.10), calls=%async_computation | async-start | bytes 1835008 | tf_op jit(solution)/shard_map/all_to_all | solution.py:22
  20.1 8.3 %collective-permute-start.3 = (bf16[2,128]{1,0:T(2,128)(2,1)S(1)}, bf16[2,128]{1,0:T(2,128)(2,1)S(1)}, u32[]{:S(2)}, u32[]{:S(2)}) collective-permute-start(bf16[2,128]{1,0:T(2,128)(2,1)S(1)} %pad_maximum_fusion.6), channel_id=1, source_target_pairs={{0,0},{1,1},{2,32},{3,33},{4,64},{5,65},{6,96},{7,97},{8,128},{9,1... | collective-permute-start | bytes 1544 | tf_op jit(solution)/shard_map/ppermute | solution.py:330
  28.4 1.9 collective-permute-start.2
  30.4 5.8 %collective-permute-start = (bf16[112,128]{1,0:T(8,128)(2,1)S(1)}, bf16[112,128]{1,0:T(8,128)(2,1)S(1)}, u32[]{:S(2)}, u32[]{:S(2)}) collective-permute-start(bf16[112,128]{1,0:T(8,128)(2,1)S(1)} %get-tuple-element.59), channel_id=1, source_target_pairs={{0,1},{1,0},{2,33},{3,32},{4,5},{5,4},{6,37},{7,36},{8,9},{9,8},{1... | collective-permute-start | bytes 86024 | tf_op jit(solution)/shard_map/ppermute | solution.py:335
  36.1 2.1 %collective-permute-start.1 = (bf16[112,128]{1,0:T(8,128)(2,1)S(1)}, bf16[112,128]{1,0:T(8,128)(2,1)S(1)}, u32[]{:S(2)}, u32[]{:S(2)}) collective-permute-start(bf16[112,128]{1,0:T(8,128)(2,1)S(1)} %get-tuple-element.60), channel_id=1, source_target_pairs={{0,0},{1,1},{2,32},{3,33},{4,4},{5,5},{6,36},{7,37},{8,8},{9,9},{1... | collective-permute-start | bytes 86024 | tf_op jit(solution)/shard_map/ppermute | solution.py:334
  38.4 7.2 %collective-permute-done.1 = bf16[112,128]{1,0:T(8,128)(2,1)S(1)} collective-permute-done((bf16[112,128]{1,0:T(8,128)(2,1)S(1)}, bf16[112,128]{1,0:T(8,128)(2,1)S(1)}, u32[]{:S(2)}, u32[]{:S(2)}) %collective-permute-start.1) | collective-permute-done | bytes 28704 | tf_op jit(solution)/shard_map/ppermute | solution.py:334
  45.6 0.8 all-to-all-done.weights_ref
  46.5 16.1 %all_to_all.30.own_ref = bf16[8,240,128]{2,1,0:T(8,128)(2,1)S(1)} all-to-all(bf16[8,240,128]{2,1,0:T(8,128)(2,1)S(1)} %broadcast_in_dim.11), channel_id=1, replica_groups=mesh['chip'=8,'core'=2,'z'=8,'yhi'=4] {'chip'}, dimensions={0} | all-to-all | bytes 983040 | tf_op jit(solution)/shard_map/all_to_all | solution.py:22
  62.6 1.9 collective-permute-start.4
  64.5 1.3 copy.28
  65.9 0.5 collective-permute-done.4.other_ref
  66.4 2.3 %shard_map.128 = bf16[8,112,256]{2,1,0:T(8,128)(2,1)S(1)} custom-call(s32[8,1,256]{2,1,0:T(1,128)S(1)} %bitcast.75, bf16[896,512]{1,0:T(8,128)(2,1)S(1)} %bitcast.73), custom_call_target="tpu_custom_call" | custom-call | flops 1879048192 | bytes 1376256 | tf_op jit(solution)/shard_map/pallas_call | solution.py:58
  68.7 2.0 collective-permute-start.5
  70.8 2.3 %shard_map.127 = bf16[8,112,256]{2,1,0:T(8,128)(2,1)S(1)} custom-call(s32[8,1,256]{2,1,0:T(1,128)S(1)} %bitcast.77, bf16[896,512]{1,0:T(8,128)(2,1)S(1)} %bitcast.74), custom_call_target="tpu_custom_call" | custom-call | flops 1879048192 | bytes 1376256 | tf_op jit(solution)/shard_map/pallas_call | solution.py:58
  73.1 0.9 add.63
  74.0 3.5 %all-to-all-start.2 = ((bf16[8,112,256]{2,1,0:T(8,128)(2,1)}), bf16[8,112,256]{2,1,0:T(8,128)(2,1)S(1)}, u32[]{:S(2)}, u32[]{:S(2)}) async-start(bf16[8,112,256]{2,1,0:T(8,128)(2,1)} %add.63), calls=%async_computation.2 | async-start | bytes 917504 | tf_op jit(solution)/shard_map/all_to_all | solution.py:358
  77.6 1.6 shard_map.129
  79.1 0.7 slice_bitcast_fusion.2
  79.8 3.9 %collective-permute-start.8 = (bf16[448,128]{1,0:T(8,128)(2,1)}, bf16[448,128]{1,0:T(8,128)(2,1)S(1)}, u32[]{:S(2)}, u32[]{:S(2)}) collective-permute-start(bf16[448,128]{1,0:T(8,128)(2,1)} %get-tuple-element.40), channel_id=1, source_target_pairs={{0,1},{1,2},{2,3},{3,0},{4,5},{5,6},{6,7},{7,4},{8,9},{9,10},{10,1... | collective-permute-start | bytes 344072 | tf_op jit(solution)/shard_map/ppermute | solution.py:353
  83.7 3.5 %collective-permute-start.10 = (bf16[448,128]{1,0:T(8,128)(2,1)S(1)}, bf16[448,128]{1,0:T(8,128)(2,1)S(1)}, u32[]{:S(2)}, u32[]{:S(2)}) collective-permute-start(bf16[448,128]{1,0:T(8,128)(2,1)S(1)} %get-tuple-element.41), channel_id=1, source_target_pairs={{0,3},{1,0},{2,1},{3,2},{4,7},{5,4},{6,5},{7,6},{8,11},{9,8},{10,9... | collective-permute-start | bytes 344072 | tf_op jit(solution)/shard_map/ppermute | solution.py:353
  87.2 5.9 %collective-permute-start.9 = (bf16[448,128]{1,0:T(8,128)(2,1)S(1)}, bf16[448,128]{1,0:T(8,128)(2,1)}, u32[]{:S(2)}, u32[]{:S(2)}) collective-permute-start(bf16[448,128]{1,0:T(8,128)(2,1)S(1)} %get-tuple-element.42), channel_id=1, source_target_pairs={{0,2},{1,3},{2,0},{3,1},{4,6},{5,7},{6,4},{7,5},{8,10},{9,11},{10,... | collective-permute-start | bytes 344072 | tf_op jit(solution)/shard_map/ppermute | solution.py:353
  93.2 3.1 %collective-permute-start.6 = (bf16[112,128]{1,0:T(8,128)(2,1)S(1)}, bf16[112,128]{1,0:T(8,128)(2,1)S(1)}, u32[]{:S(2)}, u32[]{:S(2)}) collective-permute-start(bf16[112,128]{1,0:T(8,128)(2,1)S(1)} %get-tuple-element.55), channel_id=1, source_target_pairs={{0,1},{1,0},{2,33},{3,32},{4,65},{5,64},{6,97},{7,96},{8,129},{9,1... | collective-permute-start | bytes 86024 | tf_op jit(solution)/shard_map/ppermute | solution.py:363
  96.4 3.5 %collective-permute-start.7 = (bf16[112,128]{1,0:T(8,128)(2,1)S(1)}, bf16[112,128]{1,0:T(8,128)(2,1)S(1)}, u32[]{:S(2)}, u32[]{:S(2)}) collective-permute-start(bf16[112,128]{1,0:T(8,128)(2,1)S(1)} %get-tuple-element.56), channel_id=1, source_target_pairs={{0,0},{1,1},{2,32},{3,33},{4,64},{5,65},{6,96},{7,97},{8,128},{9,1... | collective-permute-start | bytes 86024 | tf_op jit(solution)/shard_map/ppermute | solution.py:362
  99.9 1.0 fusion.1
  101.0 4.4 %collective-permute-done.7 = bf16[112,128]{1,0:T(8,128)(2,1)S(1)} collective-permute-done((bf16[112,128]{1,0:T(8,128)(2,1)S(1)}, bf16[112,128]{1,0:T(8,128)(2,1)S(1)}, u32[]{:S(2)}, u32[]{:S(2)}) %collective-permute-start.7) | collective-permute-done | bytes 28704 | tf_op jit(solution)/shard_map/ppermute | solution.py:362
  105.7 1.9 collective-permute-start.11
  107.6 1.1 collective-permute-done.11
  108.7 14.9 %all_to_all.31 = f32[8,4,128]{2,1,0:T(4,128)S(1)} all-to-all(f32[8,4,128]{2,1,0:T(4,128)S(1)} %broadcast_in_dim.12), channel_id=1, replica_groups=mesh['chip'=8,'core'=2,'z'=8,'yhi'=4] {'chip'}, dimensions={0} | all-to-all | bytes 32768 | tf_op jit(solution)/shard_map/all_to_all | solution.py:22
  123.7 0.8 fusion.6
  124.6 0.8 broadcast_in_dim.13
  125.4 4.0 %all-to-all-start.4 = ((bf16[4,480,128]{2,1,0:T(8,128)(2,1)}), bf16[4,480,128]{2,1,0:T(8,128)(2,1)S(1)}, u32[]{:S(2)}, u32[]{:S(2)}) async-start(bf16[4,480,128]{2,1,0:T(8,128)(2,1)} %broadcast_in_dim.13), calls=%async_computation.4 | async-start | bytes 983040 | tf_op jit(solution)/shard_map/all_to_all | solution.py:22
  129.4 7.7 %collective-permute-start.12 = (bf16[112,128]{1,0:T(8,128)(2,1)S(1)}, bf16[112,128]{1,0:T(8,128)(2,1)S(1)}, u32[]{:S(2)}, u32[]{:S(2)}) collective-permute-start(bf16[112,128]{1,0:T(8,128)(2,1)S(1)} %get-tuple-element.51), channel_id=1, source_target_pairs={{1,0},{0,1},{33,2},{32,3},{65,4},{64,5},{97,6},{96,7},{129,8},{128... | collective-permute-start | bytes 86024 | tf_op jit(solution)/shard_map/ppermute | solution.py:413
  137.1 3.7 %collective-permute-start.13 = (bf16[112,128]{1,0:T(8,128)(2,1)S(1)}, bf16[112,128]{1,0:T(8,128)(2,1)S(1)}, u32[]{:S(2)}, u32[]{:S(2)}) collective-permute-start(bf16[112,128]{1,0:T(8,128)(2,1)S(1)} %get-tuple-element.52), channel_id=1, source_target_pairs={{0,0},{1,1},{32,2},{33,3},{64,4},{65,5},{96,6},{97,7},{128,8},{129... | collective-permute-start | bytes 86024 | tf_op jit(solution)/shard_map/ppermute | solution.py:412
  140.9 3.8 %collective-permute-done.12 = bf16[112,128]{1,0:T(8,128)(2,1)S(1)} collective-permute-done((bf16[112,128]{1,0:T(8,128)(2,1)S(1)}, bf16[112,128]{1,0:T(8,128)(2,1)S(1)}, u32[]{:S(2)}, u32[]{:S(2)}) %collective-permute-start.12) | collective-permute-done | bytes 28704 | tf_op jit(solution)/shard_map/ppermute | solution.py:413
  144.7 1.9 collective-permute-done.13
  146.6 3.4 %shard_map.130 = (bf16[8,224,128]{2,1,0:T(8,128)(2,1)S(1)}, bf16[8,224,128]{2,1,0:T(8,128)(2,1)}, bf16[8,192,448]{2,1,0:T(8,128)(2,1)}) custom-call(s32[2]{0:T(128)S(1)} %pad_add_fusion.1.place_ref, bf16[8,112,448]{2,1,0:T(8,128)(2,1)S(1)} %all-to-all-done.weights_ref, bf16[8,240,128]{2,1,0:T(8,128)(2,1)S(1)} %all_to_all.30.own_ref, ...), custom_call_target="tpu_custom_call" | custom-call | flops 822083584 | bytes 4063232 | tf_op jit(solution)/shard_map/pallas_call | solution.py:221
  150.0 2.2 %collective-permute-start.14 = (bf16[8,224,128]{2,1,0:T(8,128)(2,1)}, bf16[8,224,128]{2,1,0:T(8,128)(2,1)S(1)}, u32[]{:S(2)}, u32[]{:S(2)}) collective-permute-start(bf16[8,224,128]{2,1,0:T(8,128)(2,1)} %get-tuple-element.24), channel_id=1, source_target_pairs={{0,32},{32,0},{1,33},{33,1},{2,34},{34,2},{3,35},{35,3},{4,36},{36... | collective-permute-start | bytes 1376264 | tf_op jit(solution)/shard_map/ppermute | solution.py:323
  152.3 1.6 collective-permute-done.14
  154.2 25.6 %all_to_all.32 = bf16[8,448,128]{2,1,0:T(8,128)(2,1)S(1)} all-to-all(bf16[8,448,128]{2,1,0:T(8,128)(2,1)S(1)} %pad_maximum_fusion), channel_id=1, replica_groups=mesh['chip'=8,'core'=2,'z'=8,'yhi'=4] {'chip'}, dimensions={0} | all-to-all | bytes 1835008 | tf_op jit(solution)/shard_map/all_to_all | solution.py:421
  179.8 3.5 %collective-permute-start.17 = (bf16[8,224,128]{2,1,0:T(8,128)(2,1)S(1)}, bf16[8,224,128]{2,1,0:T(8,128)(2,1)S(1)}, u32[]{:S(2)}, u32[]{:S(2)}) collective-permute-start(bf16[8,224,128]{2,1,0:T(8,128)(2,1)S(1)} %get-tuple-element.38.own_ref), channel_id=1, source_target_pairs={{0,32},{32,0},{1,33},{33,1},{2,34},{34,2},{3,35},{35,3},{4,36},{36... | collective-permute-start | bytes 1376264 | tf_op jit(solution)/shard_map/ppermute | solution.py:323
  183.4 1.9 collective-permute-start.16
  185.3 6.7 %collective-permute-start.15 = (bf16[112,128]{1,0:T(8,128)(2,1)S(1)}, bf16[112,128]{1,0:T(8,128)(2,1)S(1)}, u32[]{:S(2)}, u32[]{:S(2)}) collective-permute-start(bf16[112,128]{1,0:T(8,128)(2,1)S(1)} %get-tuple-element.48), channel_id=1, source_target_pairs={{0,0},{1,1},{32,2},{33,3},{4,4},{5,5},{36,6},{37,7},{8,8},{9,9},{4... | collective-permute-start | bytes 86024 | tf_op jit(solution)/shard_map/ppermute | solution.py:431
  192.0 6.5 %shard_map.131 = (f32[112,4096]{1,0:T(8,128)}, f32[8,128]{1,0:T(8,128)S(1)}) custom-call(s32[16,1,256]{2,1,0:T(1,128)S(1)} %pad_add_fusion.ids_ref, bf16[8,224,128]{2,1,0:T(8,128)(2,1)S(1)} %get-tuple-element.38.own_ref, bf16[8,224,128]{2,1,0:T(8,128)(2,1)S(1)} %collective-permute-done.17.other_ref), custom_call_target="tpu_custom_call" | custom-call | tf_op jit(solution)/shard_map/pallas_call | solution.py:118
  198.5 0.6 copy-done
  199.2 0.6 copy-done.4
  199.8 1.7 shard_map.132
  (71 shorter events, 1.5 us)
Async XLA Ops:
  7.2 12.9 %copy-start.8 = (s32[128]{0:T(128)S(1)}, s32[128]{0:T(128)}, u32[]{:S(2)}) copy-start(s32[128]{0:T(128)} %param.8) | copy-start | bytes 1540
  7.2 23.2 %copy-start.3 = (bf16[128,224]{0,1:T(8,128)(2,1)S(1)}, bf16[128,224]{0,1:T(8,128)(2,1)}, u32[]{:S(2)}) copy-start(bf16[128,224]{0,1:T(8,128)(2,1)} %param.15) | copy-start | bytes 172036
  9.2 37.2 %all-to-all-start = ((bf16[8,112,448]{2,1,0:T(8,128)(2,1)}), bf16[8,112,448]{2,1,0:T(8,128)(2,1)S(1)}, u32[]{:S(2)}, u32[]{:S(2)}) async-start(bf16[8,112,448]{2,1,0:T(8,128)(2,1)} %broadcast_in_dim.10), calls=%async_computation | async-start | bytes 1835008 | tf_op jit(solution)/shard_map/all_to_all | solution.py:22
  20.1 18.2 %collective-permute-start.3 = (bf16[2,128]{1,0:T(2,128)(2,1)S(1)}, bf16[2,128]{1,0:T(2,128)(2,1)S(1)}, u32[]{:S(2)}, u32[]{:S(2)}) collective-permute-start(bf16[2,128]{1,0:T(2,128)(2,1)S(1)} %pad_maximum_fusion.6), channel_id=1, source_target_pairs={{0,0},{1,1},{2,32},{3,33},{4,64},{5,65},{6,96},{7,97},{8,128},{9,1... | collective-permute-start | bytes 1544 | tf_op jit(solution)/shard_map/ppermute | solution.py:330
  28.4 9.9 %collective-permute-start.2 = (bf16[2,128]{1,0:T(2,128)(2,1)S(1)}, bf16[2,128]{1,0:T(2,128)(2,1)S(1)}, u32[]{:S(2)}, u32[]{:S(2)}) collective-permute-start(bf16[2,128]{1,0:T(2,128)(2,1)S(1)} %pad_maximum_fusion.6), channel_id=1, source_target_pairs={{0,1},{1,0},{2,33},{3,32},{4,65},{5,64},{6,97},{7,96},{8,129},{9,1... | collective-permute-start | bytes 1544 | tf_op jit(solution)/shard_map/ppermute | solution.py:330
  30.4 8.0 %collective-permute-start = (bf16[112,128]{1,0:T(8,128)(2,1)S(1)}, bf16[112,128]{1,0:T(8,128)(2,1)S(1)}, u32[]{:S(2)}, u32[]{:S(2)}) collective-permute-start(bf16[112,128]{1,0:T(8,128)(2,1)S(1)} %get-tuple-element.59), channel_id=1, source_target_pairs={{0,1},{1,0},{2,33},{3,32},{4,5},{5,4},{6,37},{7,36},{8,9},{9,8},{1... | collective-permute-start | bytes 86024 | tf_op jit(solution)/shard_map/ppermute | solution.py:335
  36.1 9.5 %collective-permute-start.1 = (bf16[112,128]{1,0:T(8,128)(2,1)S(1)}, bf16[112,128]{1,0:T(8,128)(2,1)S(1)}, u32[]{:S(2)}, u32[]{:S(2)}) collective-permute-start(bf16[112,128]{1,0:T(8,128)(2,1)S(1)} %get-tuple-element.60), channel_id=1, source_target_pairs={{0,0},{1,1},{2,32},{3,33},{4,4},{5,5},{6,36},{7,37},{8,8},{9,9},{1... | collective-permute-start | bytes 86024 | tf_op jit(solution)/shard_map/ppermute | solution.py:334
  62.6 3.7 %collective-permute-start.4 = (bf16[8,240,128]{2,1,0:T(8,128)(2,1)S(1)}, bf16[8,240,128]{2,1,0:T(8,128)(2,1)S(1)}, u32[]{:S(2)}, u32[]{:S(2)}) collective-permute-start(bf16[8,240,128]{2,1,0:T(8,128)(2,1)S(1)} %all_to_all.30.own_ref), channel_id=1, source_target_pairs={{0,32},{32,0},{1,33},{33,1},{2,34},{34,2},{3,35},{35,3},{4,36},{36... | collective-permute-start | bytes 1474568 | tf_op jit(solution)/shard_map/ppermute | solution.py:323
  68.7 4.4 %collective-permute-start.5 = (bf16[8,112,256]{2,1,0:T(8,128)(2,1)S(1)}, bf16[8,112,256]{2,1,0:T(8,128)(2,1)S(1)}, u32[]{:S(2)}, u32[]{:S(2)}) collective-permute-start(bf16[8,112,256]{2,1,0:T(8,128)(2,1)S(1)} %shard_map.128), channel_id=1, source_target_pairs={{0,32},{32,0},{1,33},{33,1},{2,34},{34,2},{3,35},{35,3},{4,36},{36... | collective-permute-start | bytes 1376264 | tf_op jit(solution)/shard_map/ppermute | solution.py:323
  74.0 19.1 %all-to-all-start.2 = ((bf16[8,112,256]{2,1,0:T(8,128)(2,1)}), bf16[8,112,256]{2,1,0:T(8,128)(2,1)S(1)}, u32[]{:S(2)}, u32[]{:S(2)}) async-start(bf16[8,112,256]{2,1,0:T(8,128)(2,1)} %add.63), calls=%async_computation.2 | async-start | bytes 917504 | tf_op jit(solution)/shard_map/all_to_all | solution.py:358
  77.6 69.1 %copy-start.1 = (s32[2]{0:T(128)}, s32[2]{0:T(128)S(1)}, u32[]{:S(2)}) copy-start(s32[2]{0:T(128)S(1)} %pad_add_fusion.1.place_ref) | copy-start | bytes 28
  77.6 27.9 %copy-start.2 = (bf16[128,224]{0,1:T(8,128)(2,1)S(1)}, bf16[128,224]{0,1:T(8,128)(2,1)}, u32[]{:S(2)}) copy-start(bf16[128,224]{0,1:T(8,128)(2,1)} %param.9) | copy-start | bytes 172036
  77.6 27.9 %copy-start.6 = (f32[224]{0:T(256)S(1)}, f32[224]{0:T(256)}, u32[]{:S(2)}) copy-start(f32[224]{0:T(256)} %param.11) | copy-start | bytes 2692
  77.6 27.9 %copy-start.7 = (f32[224]{0:T(256)S(1)}, f32[224]{0:T(256)}, u32[]{:S(2)}) copy-start(f32[224]{0:T(256)} %param.12) | copy-start | bytes 2692
  79.8 20.1 %collective-permute-start.8 = (bf16[448,128]{1,0:T(8,128)(2,1)}, bf16[448,128]{1,0:T(8,128)(2,1)S(1)}, u32[]{:S(2)}, u32[]{:S(2)}) collective-permute-start(bf16[448,128]{1,0:T(8,128)(2,1)} %get-tuple-element.40), channel_id=1, source_target_pairs={{0,1},{1,2},{2,3},{3,0},{4,5},{5,6},{6,7},{7,4},{8,9},{9,10},{10,1... | collective-permute-start | bytes 344072 | tf_op jit(solution)/shard_map/ppermute | solution.py:353
  83.7 16.1 %collective-permute-start.10 = (bf16[448,128]{1,0:T(8,128)(2,1)S(1)}, bf16[448,128]{1,0:T(8,128)(2,1)S(1)}, u32[]{:S(2)}, u32[]{:S(2)}) collective-permute-start(bf16[448,128]{1,0:T(8,128)(2,1)S(1)} %get-tuple-element.41), channel_id=1, source_target_pairs={{0,3},{1,0},{2,1},{3,2},{4,7},{5,4},{6,5},{7,6},{8,11},{9,8},{10,9... | collective-permute-start | bytes 344072 | tf_op jit(solution)/shard_map/ppermute | solution.py:353
  87.2 12.7 %collective-permute-start.9 = (bf16[448,128]{1,0:T(8,128)(2,1)S(1)}, bf16[448,128]{1,0:T(8,128)(2,1)}, u32[]{:S(2)}, u32[]{:S(2)}) collective-permute-start(bf16[448,128]{1,0:T(8,128)(2,1)S(1)} %get-tuple-element.42), channel_id=1, source_target_pairs={{0,2},{1,3},{2,0},{3,1},{4,6},{5,7},{6,4},{7,5},{8,10},{9,11},{10,... | collective-permute-start | bytes 344072 | tf_op jit(solution)/shard_map/ppermute | solution.py:353
  93.2 7.8 %collective-permute-start.6 = (bf16[112,128]{1,0:T(8,128)(2,1)S(1)}, bf16[112,128]{1,0:T(8,128)(2,1)S(1)}, u32[]{:S(2)}, u32[]{:S(2)}) collective-permute-start(bf16[112,128]{1,0:T(8,128)(2,1)S(1)} %get-tuple-element.55), channel_id=1, source_target_pairs={{0,1},{1,0},{2,33},{3,32},{4,65},{5,64},{6,97},{7,96},{8,129},{9,1... | collective-permute-start | bytes 86024 | tf_op jit(solution)/shard_map/ppermute | solution.py:363
  96.4 9.1 %collective-permute-start.7 = (bf16[112,128]{1,0:T(8,128)(2,1)S(1)}, bf16[112,128]{1,0:T(8,128)(2,1)S(1)}, u32[]{:S(2)}, u32[]{:S(2)}) collective-permute-start(bf16[112,128]{1,0:T(8,128)(2,1)S(1)} %get-tuple-element.56), channel_id=1, source_target_pairs={{0,0},{1,1},{2,32},{3,33},{4,64},{5,65},{6,96},{7,97},{8,128},{9,1... | collective-permute-start | bytes 86024 | tf_op jit(solution)/shard_map/ppermute | solution.py:362
  105.7 3.1 %collective-permute-start.11 = (f32[4,128]{1,0:T(4,128)S(1)}, f32[4,128]{1,0:T(4,128)S(1)}, u32[]{:S(2)}, u32[]{:S(2)}) collective-permute-start(f32[4,128]{1,0:T(4,128)S(1)} %pad_maximum_fusion.5), channel_id=1, source_target_pairs={{0,32},{32,0},{1,33},{33,1},{2,34},{34,2},{3,35},{35,3},{4,36},{36... | collective-permute-start | bytes 6152 | tf_op jit(solution)/shard_map/ppermute | solution.py:323
  125.4 21.2 %all-to-all-start.4 = ((bf16[4,480,128]{2,1,0:T(8,128)(2,1)}), bf16[4,480,128]{2,1,0:T(8,128)(2,1)S(1)}, u32[]{:S(2)}, u32[]{:S(2)}) async-start(bf16[4,480,128]{2,1,0:T(8,128)(2,1)} %broadcast_in_dim.13), calls=%async_computation.4 | async-start | bytes 983040 | tf_op jit(solution)/shard_map/all_to_all | solution.py:22
  129.4 69.7 %reduce-scatter.2.cloned.1.call-start = ((), (), s32[]{:S(2)}) async-start(), calls=%async_computation.7 | async-start | bytes 1769472 | tf_op jit(solution)/shard_map/reduce_scatter | solution.py:433
  129.4 15.2 %collective-permute-start.12 = (bf16[112,128]{1,0:T(8,128)(2,1)S(1)}, bf16[112,128]{1,0:T(8,128)(2,1)S(1)}, u32[]{:S(2)}, u32[]{:S(2)}) collective-permute-start(bf16[112,128]{1,0:T(8,128)(2,1)S(1)} %get-tuple-element.51), channel_id=1, source_target_pairs={{1,0},{0,1},{33,2},{32,3},{65,4},{64,5},{97,6},{96,7},{129,8},{128... | collective-permute-start | bytes 86024 | tf_op jit(solution)/shard_map/ppermute | solution.py:413
  137.1 9.5 %collective-permute-start.13 = (bf16[112,128]{1,0:T(8,128)(2,1)S(1)}, bf16[112,128]{1,0:T(8,128)(2,1)S(1)}, u32[]{:S(2)}, u32[]{:S(2)}) collective-permute-start(bf16[112,128]{1,0:T(8,128)(2,1)S(1)} %get-tuple-element.52), channel_id=1, source_target_pairs={{0,0},{1,1},{32,2},{33,3},{64,4},{65,5},{96,6},{97,7},{128,8},{129... | collective-permute-start | bytes 86024 | tf_op jit(solution)/shard_map/ppermute | solution.py:412
  150.0 3.9 %collective-permute-start.14 = (bf16[8,224,128]{2,1,0:T(8,128)(2,1)}, bf16[8,224,128]{2,1,0:T(8,128)(2,1)S(1)}, u32[]{:S(2)}, u32[]{:S(2)}) collective-permute-start(bf16[8,224,128]{2,1,0:T(8,128)(2,1)} %get-tuple-element.24), channel_id=1, source_target_pairs={{0,32},{32,0},{1,33},{33,1},{2,34},{34,2},{3,35},{35,3},{4,36},{36... | collective-permute-start | bytes 1376264 | tf_op jit(solution)/shard_map/ppermute | solution.py:323
  179.8 12.2 %collective-permute-start.17 = (bf16[8,224,128]{2,1,0:T(8,128)(2,1)S(1)}, bf16[8,224,128]{2,1,0:T(8,128)(2,1)S(1)}, u32[]{:S(2)}, u32[]{:S(2)}) collective-permute-start(bf16[8,224,128]{2,1,0:T(8,128)(2,1)S(1)} %get-tuple-element.38.own_ref), channel_id=1, source_target_pairs={{0,32},{32,0},{1,33},{33,1},{2,34},{34,2},{3,35},{35,3},{4,36},{36... | collective-permute-start | bytes 1376264 | tf_op jit(solution)/shard_map/ppermute | solution.py:323
  183.4 15.7 %collective-permute-start.16 = (bf16[112,128]{1,0:T(8,128)(2,1)S(1)}, bf16[112,128]{1,0:T(8,128)(2,1)S(1)}, u32[]{:S(2)}, u32[]{:S(2)}) collective-permute-start(bf16[112,128]{1,0:T(8,128)(2,1)S(1)} %get-tuple-element.47), channel_id=1, source_target_pairs={{1,0},{0,1},{33,2},{32,3},{5,4},{4,5},{37,6},{36,7},{9,8},{8,9},{4... | collective-permute-start | bytes 86024 | tf_op jit(solution)/shard_map/ppermute | solution.py:432
  185.3 13.8 %collective-permute-start.15 = (bf16[112,128]{1,0:T(8,128)(2,1)S(1)}, bf16[112,128]{1,0:T(8,128)(2,1)S(1)}, u32[]{:S(2)}, u32[]{:S(2)}) collective-permute-start(bf16[112,128]{1,0:T(8,128)(2,1)S(1)} %get-tuple-element.48), channel_id=1, source_target_pairs={{0,0},{1,1},{32,2},{33,3},{4,4},{5,5},{36,6},{37,7},{8,8},{9,9},{4... | collective-permute-start | bytes 86024 | tf_op jit(solution)/shard_map/ppermute | solution.py:431
  198.5 0.6 copy-start
  199.1 0.6 copy-start.4
  199.1 0.6 copy-start.5
Sparse Core Ops, SparseCore 0:
  152.4 42.3 reduce-scatter.1

commit v7 on v6

--- a/solution.py
+++ b/solution.py
@@ -49,12 +49,17 @@
         out_ref[i] = total[:, i * rows : (i + 1) * rows].astype(BF16)
 
 
-def lookup(ids, table):
-    blocks, _, rows = ids.shape
+def stack_groups(table):
     cols, entries = table.shape
     width = entries // GROUPS
+    return table.reshape(cols, GROUPS, width).transpose(1, 0, 2).reshape(cols * GROUPS, width)
+
+
+def lookup(ids, stacked):
+    blocks, _, rows = ids.shape
+    width = stacked.shape[1]
+    cols, entries = stacked.shape[0] // GROUPS, width * GROUPS
     parts = 4
-    stacked = table.reshape(cols, GROUPS, width).transpose(1, 0, 2).reshape(cols * GROUPS, width)
     return pl.pallas_call(
         lookup_kernel,
         grid=(blocks // parts,),
@@ -152,29 +157,34 @@
     )
 
 
-def grad_kernel(cw, place_ref, weights_ref, own_ref, other_ref, out_ref):
-    nb, feats, _ = out_ref.shape
+def grad_kernel(place_ref, weights_ref, own_ref, other_ref, keep_ref, send_ref):
+    cw = weights_ref.shape[1]
+    core, yhi = place_ref[0], place_ref[1]
+    odd, far = lax.rem(yhi, 2), lax.div(yhi, 2)
     weights = jnp.concatenate([weights_ref[a] for a in range(weights_ref.shape[0])], axis=0).T
-    for b in range(nb):
-        share = jnp.dot(
-            weights,
-            cot_columns(place_ref[0], own_ref, other_ref, b, cw),
-            preferred_element_type=F32,
+    for m in range(2):
+        even_share, odd_share = (
+            jnp.dot(
+                weights, cot_columns(core, own_ref, other_ref, b, cw), preferred_element_type=F32
+            )
+            for b in (2 * m, 2 * m + 1)
         )
-        out_ref[lax.rem(b + nb - place_ref[1], nb)] = share.astype(BF16)
-
-
-def grad_products(place, weights, own, other, nb):
+        slot = m + far - 2 * m * far
+        keep_ref[slot] = jnp.where(odd == 1, odd_share, even_share).astype(BF16)
+        send_ref[slot] = jnp.where(odd == 1, even_share, odd_share).astype(BF16)
+
+
+def grad_products(place, weights, own, other):
     na, cw, feats = weights.shape
     toks = own.shape[2]
     whole = pl.BlockSpec(memory_space=pltpu.VMEM)
     return pl.pallas_call(
-        functools.partial(grad_kernel, cw),
+        grad_kernel,
         in_specs=[pl.BlockSpec(memory_space=pltpu.SMEM), whole, whole, whole],
-        out_shape=jax.ShapeDtypeStruct((nb, feats, toks), BF16),
+        out_shape=(jax.ShapeDtypeStruct((2, feats, toks), BF16),) * 2,
         cost_estimate=pl.CostEstimate(
-            flops=2 * na * cw * feats * nb * toks,
-            bytes_accessed=2 * (weights.size + 2 * own.size + nb * feats * toks),
+            flops=8 * na * cw * feats * toks,
+            bytes_accessed=2 * (weights.size + 2 * own.size + 4 * feats * toks),
             transcendentals=0,
         ),
         compiler_params=pltpu.CompilerParams(vmem_limit_bytes=16 * 1024 * 1024),
@@ -336,7 +346,7 @@
         0,
     )
     cot = jnp.concatenate([cot, jnp.pad(digits, ((0, 12), (0, 0)))], axis=0)
-    cot, weights = lax.optimization_barrier((cot, weights))
+    cot, weights, stacked = lax.optimization_barrier((cot, weights, stack_groups(table)))
     own = gather(cot, "chip", nc)
     other = flip(own)
 
@@ -347,14 +357,15 @@
 
     own_ids, other_ids = ids_of(own), ids_of(other)
 
-    shares = grad_products(place, weights, own, other, nb)
-    grads = shares[0].astype(F32)
-    for k in range(1, nb):
-        grads += lax.ppermute(
-            shares[k], "yhi", [(i, (i + k) % nb) for i in range(nb)]
-        ).astype(F32)
-
-    pieces = lookup(own_ids, table) + flip(lookup(other_ids, table))
+    keep, send = grad_products(place, weights, own, other)
+    pair = keep.astype(F32) + lax.ppermute(
+        send, "yhi", [(i, i ^ 1) for i in range(nb)]
+    ).astype(F32)
+    grads = pair[0] + lax.ppermute(
+        pair[1].astype(BF16), "yhi", [(i, i ^ 2) for i in range(nb)]
+    ).astype(F32)
+
+    pieces = lookup(own_ids, stacked) + flip(lookup(other_ids, stacked))
     pieces = lax.all_to_all(pieces, "chip", 0, 0, tiled=True)
     cols = jnp.sum(pieces.astype(F32), axis=0).astype(BF16)
     first, second = cols[:, :toks], cols[:, toks:]

time: 209 us -> 217 us (1.038)
  waiting for transfers between devices: 21.7 us -> 33.7 us
  starting transfers between devices: 88 us -> 83.8 us
  blocking collectives: 56.6 us -> 58.8 us
    ppermute x3 -> x2, waiting for transfers between devices: 0.01 us -> 10.6 us  [the longest x1 10.6 us: per_device(): lax.ppermute(send, 'yhi', [(i, i ^ 1) for i in range(nb)]).astype(F32)]
    ppermute x3 -> x2, starting transfers between devices: 13.3 us -> 10.1 us  [the longest x1 6.16 us: per_device(): lax.ppermute(pair[1].astype(BF16), 'yhi', [(i, i ^ 2) for i in range(nb)])]
  transfers between devices with their start and end apart: 22 -> 21, of which waited for: 9 -> 10; matrix products, arithmetic and copies ran while one was open for 2% -> 0% of each run, Pallas kernels for 5% -> 5%
where the time goes in v7:
time: 217 us; the launch traced here: 216 us
  starting transfers between devices  83.8 us (39%)
  blocking collectives  58.8 us (27%)
  waiting for transfers between devices  33.7 us (16%)
  Pallas kernels  17.8 us (8%)
  between operations  14.6 us (7%)
  other arithmetic  3.53 us (2%)
  local copies, waits for them, and re-layouts  3.51 us (2%)
    all_to_all x2, blocking collectives, gather(): lax.all_to_all(jnp.broadcast_to(x[None], (count,) + x.shape), axes, 0, 0,...  32.3 us
    all_to_all x1, blocking collectives, per_device(): lax.all_to_all(jnp.concatenate([terms, mine], axis=1), 'chip', 0, 0, tile...  26.5 us
    all_to_all x2, starting transfers between devices, gather(): lax.all_to_all(jnp.broadcast_to(x[None], (count,) + x.shape), axes, 0, 0,...  14.3 us
    ppermute x5, starting transfers between devices, flip(): return lax.ppermute(x, 'core', [(0, 1), (1, 0)])  11.3 us
    ppermute x1, waiting for transfers between devices, per_device(): lax.ppermute(send, 'yhi', [(i, i ^ 1) for i in range(nb)]).astype(F32)  10.6 us
    ppermute x1, starting transfers between devices, per_device(): lax.ppermute(digits, ALL, swap_route(0))  8.29 us
    ppermute x1, starting transfers between devices, per_device(): lax.ppermute(jnp.where(odd, low, high), ALL, swap_back(1))  7.44 us
    ppermute x1, waiting for transfers between devices, per_device(): lax.ppermute(jnp.where(odd, second, first), ALL, turn(0))  7.15 us
  transfers between devices with their start and end apart: 21, of which 10 were waited for; matrix products, arithmetic and copies ran while one was open for 0% of the time, Pallas kernels for 5%

profile of v7, /device:TPU:1, one launch (start us, length us, event | category | flops | bytes accessed | tf_op | source)
XLA Modules:
  0.0 215.7 jit_solution(5051100231976444778)
XLA Ops:
  7.2 1.0 maximum_bitcast_fusion
  8.3 1.0 broadcast_in_dim.10
  9.3 10.9 %all-to-all-start = ((bf16[8,112,448]{2,1,0:T(8,128)(2,1)}), bf16[8,112,448]{2,1,0:T(8,128)(2,1)S(1)}, u32[]{:S(2)}, u32[]{:S(2)}) async-start(bf16[8,112,448]{2,1,0:T(8,128)(2,1)} %broadcast_in_dim.10), calls=%async_computation | async-start | bytes 1835008 | tf_op jit(solution)/shard_map/all_to_all | solution.py:22
  20.2 8.3 %collective-permute-start.3 = (bf16[2,128]{1,0:T(2,128)(2,1)S(1)}, bf16[2,128]{1,0:T(2,128)(2,1)S(1)}, u32[]{:S(2)}, u32[]{:S(2)}) collective-permute-start(bf16[2,128]{1,0:T(2,128)(2,1)S(1)} %pad_maximum_fusion.6), channel_id=1, source_target_pairs={{0,0},{1,1},{2,32},{3,33},{4,64},{5,65},{6,96},{7,97},{8,128},{9,1... | collective-permute-start | bytes 1544 | tf_op jit(solution)/shard_map/ppermute | solution.py:340
  28.5 1.9 collective-permute-start.2
  30.4 5.8 %collective-permute-start = (bf16[112,128]{1,0:T(8,128)(2,1)S(1)}, bf16[112,128]{1,0:T(8,128)(2,1)S(1)}, u32[]{:S(2)}, u32[]{:S(2)}) collective-permute-start(bf16[112,128]{1,0:T(8,128)(2,1)S(1)} %get-tuple-element.62), channel_id=1, source_target_pairs={{0,1},{1,0},{2,33},{3,32},{4,5},{5,4},{6,37},{7,36},{8,9},{9,8},{1... | collective-permute-start | bytes 86024 | tf_op jit(solution)/shard_map/ppermute | solution.py:345
  36.2 2.1 collective-permute-start.1
  38.5 7.1 %collective-permute-done.1 = bf16[112,128]{1,0:T(8,128)(2,1)S(1)} collective-permute-done((bf16[112,128]{1,0:T(8,128)(2,1)S(1)}, bf16[112,128]{1,0:T(8,128)(2,1)S(1)}, u32[]{:S(2)}, u32[]{:S(2)}) %collective-permute-start.1) | collective-permute-done | bytes 28704 | tf_op jit(solution)/shard_map/ppermute | solution.py:344
  45.7 0.8 all-to-all-done.weights_ref
  46.6 16.1 %all_to_all.30.own_ref = bf16[8,240,128]{2,1,0:T(8,128)(2,1)S(1)} all-to-all(bf16[8,240,128]{2,1,0:T(8,128)(2,1)S(1)} %broadcast_in_dim.11), channel_id=1, replica_groups=mesh['chip'=8,'core'=2,'z'=8,'yhi'=4] {'chip'}, dimensions={0} | all-to-all | bytes 983040 | tf_op jit(solution)/shard_map/all_to_all | solution.py:22
  62.7 1.9 collective-permute-start.4
  64.7 1.7 collective-permute-done.4.other_ref
  66.5 2.3 %shard_map.128 = bf16[8,112,256]{2,1,0:T(8,128)(2,1)S(1)} custom-call(s32[8,1,256]{2,1,0:T(1,128)S(1)} %bitcast.70, bf16[896,512]{1,0:T(8,128)(2,1)S(1)} %bitcast.68), custom_call_target="tpu_custom_call" | custom-call | flops 1879048192 | bytes 1376256 | tf_op jit(solution)/shard_map/pallas_call | solution.py:63
  68.8 2.0 collective-permute-start.5
  70.9 2.3 %shard_map.127 = bf16[8,112,256]{2,1,0:T(8,128)(2,1)S(1)} custom-call(s32[8,1,256]{2,1,0:T(1,128)S(1)} %bitcast.72, bf16[896,512]{1,0:T(8,128)(2,1)S(1)} %bitcast.69), custom_call_target="tpu_custom_call" | custom-call | flops 1879048192 | bytes 1376256 | tf_op jit(solution)/shard_map/pallas_call | solution.py:63
  73.2 0.9 add.60
  74.1 3.5 %all-to-all-start.2 = ((bf16[8,112,256]{2,1,0:T(8,128)(2,1)}), bf16[8,112,256]{2,1,0:T(8,128)(2,1)S(1)}, u32[]{:S(2)}, u32[]{:S(2)}) async-start(bf16[8,112,256]{2,1,0:T(8,128)(2,1)} %add.60), calls=%async_computation.2 | async-start | bytes 917504 | tf_op jit(solution)/shard_map/all_to_all | solution.py:369
  77.6 1.6 shard_map.129
  79.2 3.9 %collective-permute-start.8 = (bf16[2,448,128]{2,1,0:T(8,128)(2,1)S(1)}, bf16[2,448,128]{2,1,0:T(8,128)(2,1)S(1)}, u32[]{:S(2)}, u32[]{:S(2)}) collective-permute-start(bf16[2,448,128]{2,1,0:T(8,128)(2,1)S(1)} %get-tuple-element.26), channel_id=1, source_target_pairs={{0,1},{1,0},{2,3},{3,2},{4,5},{5,4},{6,7},{7,6},{8,9},{9,8},{10,11... | collective-permute-start | bytes 688136 | tf_op jit(solution)/shard_map/ppermute | solution.py:361
  83.2 10.6 %collective-permute-done.8 = bf16[2,448,128]{2,1,0:T(8,128)(2,1)S(1)} collective-permute-done((bf16[2,448,128]{2,1,0:T(8,128)(2,1)S(1)}, bf16[2,448,128]{2,1,0:T(8,128)(2,1)S(1)}, u32[]{:S(2)}, u32[]{:S(2)}) %collective-permute-start.8) | collective-permute-done | bytes 229408 | tf_op jit(solution)/shard_map/ppermute | solution.py:361
  93.9 6.2 %collective-permute-start.9 = (bf16[448,128]{1,0:T(8,128)(2,1)S(1)}, bf16[448,128]{1,0:T(8,128)(2,1)S(1)}, u32[]{:S(2)}, u32[]{:S(2)}) collective-permute-start(bf16[448,128]{1,0:T(8,128)(2,1)S(1)} %fusion.11), channel_id=1, source_target_pairs={{0,2},{1,3},{2,0},{3,1},{4,6},{5,7},{6,4},{7,5},{8,10},{9,11},{10,... | collective-permute-start | bytes 344072 | tf_op jit(solution)/shard_map/ppermute | solution.py:364
  100.1 1.9 collective-permute-start.6
  102.1 4.7 %collective-permute-start.7 = (bf16[112,128]{1,0:T(8,128)(2,1)S(1)}, bf16[112,128]{1,0:T(8,128)(2,1)S(1)}, u32[]{:S(2)}, u32[]{:S(2)}) collective-permute-start(bf16[112,128]{1,0:T(8,128)(2,1)S(1)} %get-tuple-element.59), channel_id=1, source_target_pairs={{0,0},{1,1},{2,32},{3,33},{4,64},{5,65},{6,96},{7,97},{8,128},{9,1... | collective-permute-start | bytes 86024 | tf_op jit(solution)/shard_map/ppermute | solution.py:373
  106.8 0.8 collective-permute-done.6
  107.6 3.5 %collective-permute-done.7 = bf16[112,128]{1,0:T(8,128)(2,1)S(1)} collective-permute-done((bf16[112,128]{1,0:T(8,128)(2,1)S(1)}, bf16[112,128]{1,0:T(8,128)(2,1)S(1)}, u32[]{:S(2)}, u32[]{:S(2)}) %collective-permute-start.7) | collective-permute-done | bytes 28704 | tf_op jit(solution)/shard_map/ppermute | solution.py:373
  111.2 0.1 fusion.10
  111.4 1.9 collective-permute-start.10
  113.3 1.1 collective-permute-done.10
  114.4 16.2 %all_to_all.31 = f32[8,4,128]{2,1,0:T(4,128)S(1)} all-to-all(f32[8,4,128]{2,1,0:T(4,128)S(1)} %broadcast_in_dim.12), channel_id=1, replica_groups=mesh['chip'=8,'core'=2,'z'=8,'yhi'=4] {'chip'}, dimensions={0} | all-to-all | bytes 32768 | tf_op jit(solution)/shard_map/all_to_all | solution.py:22
  130.7 0.8 fusion.5
  131.6 0.8 broadcast_in_dim.13
  132.4 3.5 %all-to-all-start.4 = ((bf16[4,480,128]{2,1,0:T(8,128)(2,1)}), bf16[4,480,128]{2,1,0:T(8,128)(2,1)S(1)}, u32[]{:S(2)}, u32[]{:S(2)}) async-start(bf16[4,480,128]{2,1,0:T(8,128)(2,1)} %broadcast_in_dim.13), calls=%async_computation.4 | async-start | bytes 983040 | tf_op jit(solution)/shard_map/all_to_all | solution.py:22
  135.9 7.4 %collective-permute-start.11 = (bf16[112,128]{1,0:T(8,128)(2,1)S(1)}, bf16[112,128]{1,0:T(8,128)(2,1)S(1)}, u32[]{:S(2)}, u32[]{:S(2)}) collective-permute-start(bf16[112,128]{1,0:T(8,128)(2,1)S(1)} %get-tuple-element.54), channel_id=1, source_target_pairs={{1,0},{0,1},{33,2},{32,3},{65,4},{64,5},{97,6},{96,7},{129,8},{128... | collective-permute-start | bytes 86024 | tf_op jit(solution)/shard_map/ppermute | solution.py:424
  143.4 3.7 %collective-permute-start.12 = (bf16[112,128]{1,0:T(8,128)(2,1)S(1)}, bf16[112,128]{1,0:T(8,128)(2,1)S(1)}, u32[]{:S(2)}, u32[]{:S(2)}) collective-permute-start(bf16[112,128]{1,0:T(8,128)(2,1)S(1)} %get-tuple-element.55), channel_id=1, source_target_pairs={{0,0},{1,1},{32,2},{33,3},{64,4},{65,5},{96,6},{97,7},{128,8},{129... | collective-permute-start | bytes 86024 | tf_op jit(solution)/shard_map/ppermute | solution.py:423
  147.1 4.3 %collective-permute-done.11 = bf16[112,128]{1,0:T(8,128)(2,1)S(1)} collective-permute-done((bf16[112,128]{1,0:T(8,128)(2,1)S(1)}, bf16[112,128]{1,0:T(8,128)(2,1)S(1)}, u32[]{:S(2)}, u32[]{:S(2)}) %collective-permute-start.11) | collective-permute-done | bytes 28704 | tf_op jit(solution)/shard_map/ppermute | solution.py:424
  151.5 1.5 collective-permute-done.12
  153.0 3.4 %shard_map.130 = (bf16[8,224,128]{2,1,0:T(8,128)(2,1)S(1)}, bf16[8,224,128]{2,1,0:T(8,128)(2,1)}, bf16[8,192,448]{2,1,0:T(8,128)(2,1)}) custom-call(s32[2]{0:T(128)S(1)} %pad_add_fusion.1.place_ref, bf16[8,112,448]{2,1,0:T(8,128)(2,1)S(1)} %all-to-all-done.weights_ref, bf16[8,240,128]{2,1,0:T(8,128)(2,1)S(1)} %all_to_all.30.own_ref, ...), custom_call_target="tpu_custom_call" | custom-call | flops 822083584 | bytes 4063232 | tf_op jit(solution)/shard_map/pallas_call | solution.py:231
  156.4 1.9 collective-permute-start.13
  158.4 2.0 collective-permute-done.13
  160.3 0.1 add_convert_fusion
  160.6 26.5 %all_to_all.32 = bf16[8,448,128]{2,1,0:T(8,128)(2,1)S(1)} all-to-all(bf16[8,448,128]{2,1,0:T(8,128)(2,1)S(1)} %pad_maximum_fusion), channel_id=1, replica_groups=mesh['chip'=8,'core'=2,'z'=8,'yhi'=4] {'chip'}, dimensions={0} | all-to-all | bytes 1835008 | tf_op jit(solution)/shard_map/all_to_all | solution.py:432
  187.2 3.5 %collective-permute-start.16 = (bf16[8,224,128]{2,1,0:T(8,128)(2,1)S(1)}, bf16[8,224,128]{2,1,0:T(8,128)(2,1)S(1)}, u32[]{:S(2)}, u32[]{:S(2)}) collective-permute-start(bf16[8,224,128]{2,1,0:T(8,128)(2,1)S(1)} %get-tuple-element.44.own_ref), channel_id=1, source_target_pairs={{0,32},{32,0},{1,33},{33,1},{2,34},{34,2},{3,35},{35,3},{4,36},{36... | collective-permute-start | bytes 1376264 | tf_op jit(solution)/shard_map/ppermute | solution.py:333
  190.7 1.9 collective-permute-start.15
  192.7 6.7 %collective-permute-start.14 = (bf16[112,128]{1,0:T(8,128)(2,1)S(1)}, bf16[112,128]{1,0:T(8,128)(2,1)S(1)}, u32[]{:S(2)}, u32[]{:S(2)}) collective-permute-start(bf16[112,128]{1,0:T(8,128)(2,1)S(1)} %get-tuple-element.51), channel_id=1, source_target_pairs={{0,0},{1,1},{32,2},{33,3},{4,4},{5,5},{36,6},{37,7},{8,8},{9,9},{4... | collective-permute-start | bytes 86024 | tf_op jit(solution)/shard_map/ppermute | solution.py:442
  199.4 6.5 %shard_map.131 = (f32[112,4096]{1,0:T(8,128)}, f32[8,128]{1,0:T(8,128)S(1)}) custom-call(s32[16,1,256]{2,1,0:T(1,128)S(1)} %pad_add_fusion.ids_ref, bf16[8,224,128]{2,1,0:T(8,128)(2,1)S(1)} %get-tuple-element.44.own_ref, bf16[8,224,128]{2,1,0:T(8,128)(2,1)S(1)} %collective-permute-done.16.other_ref), custom_call_target="tpu_custom_call" | custom-call | tf_op jit(solution)/shard_map/pallas_call | solution.py:123
  205.9 0.6 copy-done
  206.5 0.6 copy-done.5
  207.1 1.7 shard_map.132
  (72 shorter events, 1.3 us)
Async XLA Ops:
  7.2 13.0 %copy-start.9 = (s32[128]{0:T(128)S(1)}, s32[128]{0:T(128)}, u32[]{:S(2)}) copy-start(s32[128]{0:T(128)} %param.8) | copy-start | bytes 1540
  7.2 23.2 %copy-start.4 = (bf16[128,224]{0,1:T(8,128)(2,1)S(1)}, bf16[128,224]{0,1:T(8,128)(2,1)}, u32[]{:S(2)}) copy-start(bf16[128,224]{0,1:T(8,128)(2,1)} %param.15) | copy-start | bytes 172036
  7.2 31.2 %copy-start.2 = (bf16[112,4096]{1,0:T(8,128)(2,1)S(1)}, bf16[112,4096]{1,0:T(8,128)(2,1)}, u32[]{:S(2)}) copy-start(bf16[112,4096]{1,0:T(8,128)(2,1)} %param.10) | copy-start | bytes 2752516
  9.3 37.2 %all-to-all-start = ((bf16[8,112,448]{2,1,0:T(8,128)(2,1)}), bf16[8,112,448]{2,1,0:T(8,128)(2,1)S(1)}, u32[]{:S(2)}, u32[]{:S(2)}) async-start(bf16[8,112,448]{2,1,0:T(8,128)(2,1)} %broadcast_in_dim.10), calls=%async_computation | async-start | bytes 1835008 | tf_op jit(solution)/shard_map/all_to_all | solution.py:22
  20.2 18.3 %collective-permute-start.3 = (bf16[2,128]{1,0:T(2,128)(2,1)S(1)}, bf16[2,128]{1,0:T(2,128)(2,1)S(1)}, u32[]{:S(2)}, u32[]{:S(2)}) collective-permute-start(bf16[2,128]{1,0:T(2,128)(2,1)S(1)} %pad_maximum_fusion.6), channel_id=1, source_target_pairs={{0,0},{1,1},{2,32},{3,33},{4,64},{5,65},{6,96},{7,97},{8,128},{9,1... | collective-permute-start | bytes 1544 | tf_op jit(solution)/shard_map/ppermute | solution.py:340
  28.5 10.0 %collective-permute-start.2 = (bf16[2,128]{1,0:T(2,128)(2,1)S(1)}, bf16[2,128]{1,0:T(2,128)(2,1)S(1)}, u32[]{:S(2)}, u32[]{:S(2)}) collective-permute-start(bf16[2,128]{1,0:T(2,128)(2,1)S(1)} %pad_maximum_fusion.6), channel_id=1, source_target_pairs={{0,1},{1,0},{2,33},{3,32},{4,65},{5,64},{6,97},{7,96},{8,129},{9,1... | collective-permute-start | bytes 1544 | tf_op jit(solution)/shard_map/ppermute | solution.py:340
  30.4 8.1 %collective-permute-start = (bf16[112,128]{1,0:T(8,128)(2,1)S(1)}, bf16[112,128]{1,0:T(8,128)(2,1)S(1)}, u32[]{:S(2)}, u32[]{:S(2)}) collective-permute-start(bf16[112,128]{1,0:T(8,128)(2,1)S(1)} %get-tuple-element.62), channel_id=1, source_target_pairs={{0,1},{1,0},{2,33},{3,32},{4,5},{5,4},{6,37},{7,36},{8,9},{9,8},{1... | collective-permute-start | bytes 86024 | tf_op jit(solution)/shard_map/ppermute | solution.py:345
  36.2 9.5 %collective-permute-start.1 = (bf16[112,128]{1,0:T(8,128)(2,1)S(1)}, bf16[112,128]{1,0:T(8,128)(2,1)S(1)}, u32[]{:S(2)}, u32[]{:S(2)}) collective-permute-start(bf16[112,128]{1,0:T(8,128)(2,1)S(1)} %get-tuple-element.63), channel_id=1, source_target_pairs={{0,0},{1,1},{2,32},{3,33},{4,4},{5,5},{6,36},{7,37},{8,8},{9,9},{1... | collective-permute-start | bytes 86024 | tf_op jit(solution)/shard_map/ppermute | solution.py:344
  62.7 3.7 %collective-permute-start.4 = (bf16[8,240,128]{2,1,0:T(8,128)(2,1)S(1)}, bf16[8,240,128]{2,1,0:T(8,128)(2,1)S(1)}, u32[]{:S(2)}, u32[]{:S(2)}) collective-permute-start(bf16[8,240,128]{2,1,0:T(8,128)(2,1)S(1)} %all_to_all.30.own_ref), channel_id=1, source_target_pairs={{0,32},{32,0},{1,33},{33,1},{2,34},{34,2},{3,35},{35,3},{4,36},{36... | collective-permute-start | bytes 1474568 | tf_op jit(solution)/shard_map/ppermute | solution.py:333
  68.8 4.4 %collective-permute-start.5 = (bf16[8,112,256]{2,1,0:T(8,128)(2,1)S(1)}, bf16[8,112,256]{2,1,0:T(8,128)(2,1)S(1)}, u32[]{:S(2)}, u32[]{:S(2)}) collective-permute-start(bf16[8,112,256]{2,1,0:T(8,128)(2,1)S(1)} %shard_map.128), channel_id=1, source_target_pairs={{0,32},{32,0},{1,33},{33,1},{2,34},{34,2},{3,35},{35,3},{4,36},{36... | collective-permute-start | bytes 1376264 | tf_op jit(solution)/shard_map/ppermute | solution.py:333
  74.1 26.0 %all-to-all-start.2 = ((bf16[8,112,256]{2,1,0:T(8,128)(2,1)}), bf16[8,112,256]{2,1,0:T(8,128)(2,1)S(1)}, u32[]{:S(2)}, u32[]{:S(2)}) async-start(bf16[8,112,256]{2,1,0:T(8,128)(2,1)} %add.60), calls=%async_computation.2 | async-start | bytes 917504 | tf_op jit(solution)/shard_map/all_to_all | solution.py:369
  77.6 75.4 %copy-start.1 = (s32[2]{0:T(128)}, s32[2]{0:T(128)S(1)}, u32[]{:S(2)}) copy-start(s32[2]{0:T(128)S(1)} %pad_add_fusion.1.place_ref) | copy-start | bytes 28
  77.6 33.5 %copy-start.3 = (bf16[128,224]{0,1:T(8,128)(2,1)S(1)}, bf16[128,224]{0,1:T(8,128)(2,1)}, u32[]{:S(2)}) copy-start(bf16[128,224]{0,1:T(8,128)(2,1)} %param.9) | copy-start | bytes 172036
  77.6 33.6 %copy-start.7 = (f32[224]{0:T(256)S(1)}, f32[224]{0:T(256)}, u32[]{:S(2)}) copy-start(f32[224]{0:T(256)} %param.11) | copy-start | bytes 2692
  77.6 33.6 %copy-start.8 = (f32[224]{0:T(256)S(1)}, f32[224]{0:T(256)}, u32[]{:S(2)}) copy-start(f32[224]{0:T(256)} %param.12) | copy-start | bytes 2692
  79.2 14.6 %collective-permute-start.8 = (bf16[2,448,128]{2,1,0:T(8,128)(2,1)S(1)}, bf16[2,448,128]{2,1,0:T(8,128)(2,1)S(1)}, u32[]{:S(2)}, u32[]{:S(2)}) collective-permute-start(bf16[2,448,128]{2,1,0:T(8,128)(2,1)S(1)} %get-tuple-element.26), channel_id=1, source_target_pairs={{0,1},{1,0},{2,3},{3,2},{4,5},{5,4},{6,7},{7,6},{8,9},{9,8},{10,11... | collective-permute-start | bytes 688136 | tf_op jit(solution)/shard_map/ppermute | solution.py:361
  93.9 12.9 %collective-permute-start.9 = (bf16[448,128]{1,0:T(8,128)(2,1)S(1)}, bf16[448,128]{1,0:T(8,128)(2,1)S(1)}, u32[]{:S(2)}, u32[]{:S(2)}) collective-permute-start(bf16[448,128]{1,0:T(8,128)(2,1)S(1)} %fusion.11), channel_id=1, source_target_pairs={{0,2},{1,3},{2,0},{3,1},{4,6},{5,7},{6,4},{7,5},{8,10},{9,11},{10,... | collective-permute-start | bytes 344072 | tf_op jit(solution)/shard_map/ppermute | solution.py:364
  100.1 7.5 %collective-permute-start.6 = (bf16[112,128]{1,0:T(8,128)(2,1)S(1)}, bf16[112,128]{1,0:T(8,128)(2,1)S(1)}, u32[]{:S(2)}, u32[]{:S(2)}) collective-permute-start(bf16[112,128]{1,0:T(8,128)(2,1)S(1)} %get-tuple-element.58), channel_id=1, source_target_pairs={{0,1},{1,0},{2,33},{3,32},{4,65},{5,64},{6,97},{7,96},{8,129},{9,1... | collective-permute-start | bytes 86024 | tf_op jit(solution)/shard_map/ppermute | solution.py:374
  102.1 9.1 %collective-permute-start.7 = (bf16[112,128]{1,0:T(8,128)(2,1)S(1)}, bf16[112,128]{1,0:T(8,128)(2,1)S(1)}, u32[]{:S(2)}, u32[]{:S(2)}) collective-permute-start(bf16[112,128]{1,0:T(8,128)(2,1)S(1)} %get-tuple-element.59), channel_id=1, source_target_pairs={{0,0},{1,1},{2,32},{3,33},{4,64},{5,65},{6,96},{7,97},{8,128},{9,1... | collective-permute-start | bytes 86024 | tf_op jit(solution)/shard_map/ppermute | solution.py:373
  111.4 3.1 %collective-permute-start.10 = (f32[4,128]{1,0:T(4,128)S(1)}, f32[4,128]{1,0:T(4,128)S(1)}, u32[]{:S(2)}, u32[]{:S(2)}) collective-permute-start(f32[4,128]{1,0:T(4,128)S(1)} %pad_maximum_fusion.5), channel_id=1, source_target_pairs={{0,32},{32,0},{1,33},{33,1},{2,34},{34,2},{3,35},{35,3},{4,36},{36... | collective-permute-start | bytes 6152 | tf_op jit(solution)/shard_map/ppermute | solution.py:333
  132.4 20.6 %all-to-all-start.4 = ((bf16[4,480,128]{2,1,0:T(8,128)(2,1)}), bf16[4,480,128]{2,1,0:T(8,128)(2,1)S(1)}, u32[]{:S(2)}, u32[]{:S(2)}) async-start(bf16[4,480,128]{2,1,0:T(8,128)(2,1)} %broadcast_in_dim.13), calls=%async_computation.4 | async-start | bytes 983040 | tf_op jit(solution)/shard_map/all_to_all | solution.py:22
  135.9 70.6 %reduce-scatter.2.cloned.1.call-start = ((), (), s32[]{:S(2)}) async-start(), calls=%async_computation.7 | async-start | bytes 1769472 | tf_op jit(solution)/shard_map/reduce_scatter | solution.py:444
  135.9 15.5 %collective-permute-start.11 = (bf16[112,128]{1,0:T(8,128)(2,1)S(1)}, bf16[112,128]{1,0:T(8,128)(2,1)S(1)}, u32[]{:S(2)}, u32[]{:S(2)}) collective-permute-start(bf16[112,128]{1,0:T(8,128)(2,1)S(1)} %get-tuple-element.54), channel_id=1, source_target_pairs={{1,0},{0,1},{33,2},{32,3},{65,4},{64,5},{97,6},{96,7},{129,8},{128... | collective-permute-start | bytes 86024 | tf_op jit(solution)/shard_map/ppermute | solution.py:424
  143.4 9.6 %collective-permute-start.12 = (bf16[112,128]{1,0:T(8,128)(2,1)S(1)}, bf16[112,128]{1,0:T(8,128)(2,1)S(1)}, u32[]{:S(2)}, u32[]{:S(2)}) collective-permute-start(bf16[112,128]{1,0:T(8,128)(2,1)S(1)} %get-tuple-element.55), channel_id=1, source_target_pairs={{0,0},{1,1},{32,2},{33,3},{64,4},{65,5},{96,6},{97,7},{128,8},{129... | collective-permute-start | bytes 86024 | tf_op jit(solution)/shard_map/ppermute | solution.py:423
  156.4 3.9 %collective-permute-start.13 = (bf16[8,224,128]{2,1,0:T(8,128)(2,1)}, bf16[8,224,128]{2,1,0:T(8,128)(2,1)S(1)}, u32[]{:S(2)}, u32[]{:S(2)}) collective-permute-start(bf16[8,224,128]{2,1,0:T(8,128)(2,1)} %get-tuple-element.30), channel_id=1, source_target_pairs={{0,32},{32,0},{1,33},{33,1},{2,34},{34,2},{3,35},{35,3},{4,36},{36... | collective-permute-start | bytes 1376264 | tf_op jit(solution)/shard_map/ppermute | solution.py:333
  187.2 12.2 %collective-permute-start.16 = (bf16[8,224,128]{2,1,0:T(8,128)(2,1)S(1)}, bf16[8,224,128]{2,1,0:T(8,128)(2,1)S(1)}, u32[]{:S(2)}, u32[]{:S(2)}) collective-permute-start(bf16[8,224,128]{2,1,0:T(8,128)(2,1)S(1)} %get-tuple-element.44.own_ref), channel_id=1, source_target_pairs={{0,32},{32,0},{1,33},{33,1},{2,34},{34,2},{3,35},{35,3},{4,36},{36... | collective-permute-start | bytes 1376264 | tf_op jit(solution)/shard_map/ppermute | solution.py:333
  190.7 15.7 %collective-permute-start.15 = (bf16[112,128]{1,0:T(8,128)(2,1)S(1)}, bf16[112,128]{1,0:T(8,128)(2,1)S(1)}, u32[]{:S(2)}, u32[]{:S(2)}) collective-permute-start(bf16[112,128]{1,0:T(8,128)(2,1)S(1)} %get-tuple-element.50), channel_id=1, source_target_pairs={{1,0},{0,1},{33,2},{32,3},{5,4},{4,5},{37,6},{36,7},{9,8},{8,9},{4... | collective-permute-start | bytes 86024 | tf_op jit(solution)/shard_map/ppermute | solution.py:443
  192.7 13.8 %collective-permute-start.14 = (bf16[112,128]{1,0:T(8,128)(2,1)S(1)}, bf16[112,128]{1,0:T(8,128)(2,1)S(1)}, u32[]{:S(2)}, u32[]{:S(2)}) collective-permute-start(bf16[112,128]{1,0:T(8,128)(2,1)S(1)} %get-tuple-element.51), channel_id=1, source_target_pairs={{0,0},{1,1},{32,2},{33,3},{4,4},{5,5},{36,6},{37,7},{8,8},{9,9},{4... | collective-permute-start | bytes 86024 | tf_op jit(solution)/shard_map/ppermute | solution.py:442
  205.9 0.6 copy-start
  206.5 0.6 copy-start.5
  206.5 0.6 copy-start.6
Sparse Core Ops, SparseCore 0:
  158.5 43.6 reduce-scatter.1

commit v8 on v6

--- a/solution.py
+++ b/solution.py
@@ -10,7 +10,7 @@
 
 EPS = 1e-06
 GROUPS = 8
-PAD_ROWS = 80
+PAD_ROWS = 64
 BF16 = jnp.bfloat16
 F32 = jnp.float32
 DP = ("z", "yhi")
@@ -155,13 +155,18 @@
 def grad_kernel(cw, place_ref, weights_ref, own_ref, other_ref, out_ref):
     nb, feats, _ = out_ref.shape
     weights = jnp.concatenate([weights_ref[a] for a in range(weights_ref.shape[0])], axis=0).T
-    for b in range(nb):
-        share = jnp.dot(
+    whole = [
+        jnp.dot(
             weights,
             cot_columns(place_ref[0], own_ref, other_ref, b, cw),
             preferred_element_type=F32,
-        )
-        out_ref[lax.rem(b + nb - place_ref[1], nb)] = share.astype(BF16)
+        ).astype(BF16)
+        for b in range(nb)
+    ]
+    for b in range(nb):
+        half, pair = b % 2 * cw, b // 2 * 2
+        share = [whole[pair + x][half : half + cw] for x in range(2)] + [whole[b][2 * cw :]]
+        out_ref[lax.rem(b + nb - place_ref[1], nb)] = jnp.concatenate(share, axis=0)
 
 
 def grad_products(place, weights, own, other, nb):
@@ -181,6 +186,14 @@
     )(place, weights, own, other)
 
 
+def normed_columns(normed_ref, b, cw):
+    pair, x = b // 2 * 2, b % 2 * cw
+    return jnp.concatenate(
+        [normed_ref[pair, x : x + cw], normed_ref[pair + 1, x : x + cw], normed_ref[b, 2 * cw : 4 * cw]],
+        axis=0,
+    )
+
+
 def out_kernel(
     place_ref, weights_ref, own_ref, other_ref, normed_ref, keep_ref, send_ref, sums_ref
 ):
@@ -188,9 +201,8 @@
     nb, _, toks = normed_ref.shape
     core = place_ref[0]
     weights = jnp.concatenate([weights_ref[a] for a in range(na)], axis=0)
-    terms = [
-        jnp.dot(weights, normed_ref[b, :feats], preferred_element_type=F32) for b in range(nb)
-    ]
+    blocks = [normed_columns(normed_ref, b, cw) for b in range(nb)]
+    terms = [jnp.dot(weights, block, preferred_element_type=F32) for block in blocks]
     for x in range(2):
         keep = jnp.where(core == 0, terms[x], terms[x + 2]).astype(BF16)
         send = jnp.where(core == 0, terms[x + 2], terms[x]).astype(BF16)
@@ -200,7 +212,7 @@
     cot = jnp.concatenate(
         [cot_columns(core, own_ref, other_ref, b, cw) for b in range(nb)], axis=1
     )
-    normed = jnp.concatenate([normed_ref[b, :feats] for b in range(nb)], axis=1)
+    normed = jnp.concatenate(blocks, axis=1)
     sums = lax.dot_general(
         cot, normed, (((1,), (1,)), ((), ())), preferred_element_type=F32
     ).astype(BF16)
@@ -268,7 +280,7 @@
             jax.ShapeDtypeStruct((2, fw), F32),
         ),
         cost_estimate=pl.CostEstimate(
-            flops=0, bytes_accessed=2 * sums.size + 8 * fw * cw, transcendentals=0
+            flops=0, bytes_accessed=0, transcendentals=0
         ),
     )(place, sums, got0, got1, done)
 
@@ -295,8 +307,14 @@
             for j in range(nd)
         ]
 
-    def swap_back(c):
-        return [(b, a) for a, b in swap_route(c)]
+    across = [
+        ((2 * p + c) * nd + q * nb + 2 * c2 + i, (2 * q + c2) * nd + p * nb + 2 * c + i)
+        for p in range(na)
+        for c in range(2)
+        for q in range(na)
+        for c2 in range(2)
+        for i in range(2)
+    ]
 
     def in_order(got0, got1, axis):
         return jnp.concatenate(
@@ -357,36 +375,48 @@
     pieces = lookup(own_ids, table) + flip(lookup(other_ids, table))
     pieces = lax.all_to_all(pieces, "chip", 0, 0, tiled=True)
     cols = jnp.sum(pieces.astype(F32), axis=0).astype(BF16)
-    first, second = cols[:, :toks], cols[:, toks:]
-    embed = in_order(
-        lax.ppermute(jnp.where(odd, second, first), ALL, swap_route(0)),
-        lax.ppermute(jnp.where(odd, first, second), ALL, swap_route(1)),
-        0,
-    ).astype(F32)
+    embed = jnp.concatenate([cols[:, :toks], cols[:, toks:]], axis=0)
+    embed = lax.ppermute(embed, ALL, across).astype(F32)
+
+    def by_block(x):
+        return jnp.sum(x.reshape(2, cw, toks), axis=1)
+
+    def to_rows(x):
+        return jnp.broadcast_to(x[:, None], (2, cw, toks)).reshape(2 * cw, toks)
 
     hid = hidden.T.astype(F32)
-    gain_e, gain_h = gain_embed[:, None], gain_hidden[:, None]
+    gain_e = jnp.where(odd, gain_embed[cw:], gain_embed[:cw])
+    gain_e, gain_h = jnp.concatenate([gain_e, gain_e])[:, None], gain_hidden[:, None]
     grad_left, grad_right = grads[:fw], grads[fw:]
     dn_embed, dn_hidden = grad_left * gain_e, grad_right * gain_h
-    stats = jnp.stack(
+    halves = jnp.concatenate([by_block(embed * embed), by_block(dn_embed * embed)], axis=0)
+    halves += lax.ppermute(halves, "yhi", [(i, i ^ 1) for i in range(nb)])
+    stats = jnp.concatenate(
         [
-            jnp.sum(embed * embed, axis=0),
-            jnp.sum(hid * hid, axis=0),
-            jnp.sum(dn_embed * embed, axis=0),
-            jnp.sum(dn_hidden * hid, axis=0),
-        ]
-    )
-    stats = jnp.sum(gather(stats + flip(stats), "chip", nc), axis=0)
-    inv_embed = lax.rsqrt(stats[0] / full + EPS)[None]
-    inv_hidden = lax.rsqrt(stats[1] / full + EPS)[None]
+            halves,
+            jnp.sum(hid * hid, axis=0, keepdims=True),
+            jnp.sum(dn_hidden * hid, axis=0, keepdims=True),
+        ],
+        axis=0,
+    )
+    stats = jnp.sum(gather(stats, VOCAB, nv), axis=0)
+    inv_embed = lax.rsqrt(stats[:2] / full + EPS)
+    coef_embed = to_rows(stats[2:4] * inv_embed / full)
+    inv_embed = to_rows(inv_embed)
+    inv_hidden = lax.rsqrt(stats[4:5] / full + EPS)
+    coef_hidden = stats[5:6] * inv_hidden / full
     norm_embed, norm_hidden = embed * inv_embed, hid * inv_hidden
-    coef_embed = stats[2][None] * inv_embed / full
-    coef_hidden = stats[3][None] * inv_hidden / full
     grad_embedded = (inv_embed * (dn_embed - norm_embed * coef_embed)).astype(BF16)
     grad_hidden = (inv_hidden * (dn_hidden - norm_hidden * coef_hidden)).astype(BF16)
 
+    gains = jnp.sum(grad_left * norm_embed, axis=1)
+    gains = gains[:cw] + gains[cw:]
     gains = jnp.concatenate(
-        [jnp.sum(grad_left * norm_embed, axis=1), jnp.sum(grad_right * norm_hidden, axis=1)]
+        [
+            jnp.where(odd, 0.0, gains),
+            jnp.where(odd, gains, 0.0),
+            jnp.sum(grad_right * norm_hidden, axis=1),
+        ]
     )
     lines = -(-2 * fw // toks)
     gains = jnp.pad(gains, (0, lines * toks - 2 * fw)).reshape(lines, toks)
@@ -407,12 +437,7 @@
         nb,
     )
 
-    low, high = grad_embedded[:cw], grad_embedded[cw:]
-    mine = in_order(
-        lax.ppermute(jnp.where(odd, high, low), ALL, swap_back(0)),
-        lax.ppermute(jnp.where(odd, low, high), ALL, swap_back(1)),
-        0,
-    )
+    mine = lax.ppermute(grad_embedded, ALL, across)
 
     normed, mine = lax.optimization_barrier((normed, mine))
     keep, send, weight_terms = out_products(place, weights, own, other, normed)

time: 209 us -> 207 us (level)
  starting transfers between devices: 88 us -> 83 us
  waiting for transfers between devices: 21.7 us -> 25.8 us
    all_to_all x1, blocking collectives: 25.6 us -> 22.1 us  [per_device(): lax.all_to_all(jnp.concatenate([terms, mine], axis=1), 'chip', 0, 0, tile...]
    ppermute x4 -> x3, starting transfers between devices: 18 us -> 14.7 us  [the longest x1 8.15 us: per_device(): mine = lax.ppermute(grad_embedded, ALL, across)]
    ppermute x4 -> x3, waiting for transfers between devices: 10.3 us -> 13.2 us  [the longest x1 7.77 us: per_device(): mine = lax.ppermute(grad_embedded, ALL, across)]
    ppermute x5 -> x4, starting transfers between devices: 11.6 us -> 9.4 us  [flip(): return lax.ppermute(x, 'core', [(0, 1), (1, 0)])]
  transfers between devices with their start and end apart: 22 -> 20, of which waited for: 9 -> 8; matrix products, arithmetic and copies ran while one was open for 2% -> 2% of each run, Pallas kernels for 5% -> 5%
where the time goes in v8:
time: 207 us; the launch traced here: 206 us
  starting transfers between devices  83 us (40%)
  blocking collectives  54.8 us (26%)
  waiting for transfers between devices  25.8 us (12%)
  Pallas kernels  17.7 us (9%)
  between operations  14.6 us (7%)
  local copies, waits for them, and re-layouts  5.33 us (3%)
  other arithmetic  4.7 us (2%)
    all_to_all x2, blocking collectives, gather(): lax.all_to_all(jnp.broadcast_to(x[None], (count,) + x.shape), axes, 0, 0,...  32.6 us
    all_to_all x1, blocking collectives, per_device(): lax.all_to_all(jnp.concatenate([terms, mine], axis=1), 'chip', 0, 0, tile...  22.1 us
    all_to_all x2, starting transfers between devices, gather(): lax.all_to_all(jnp.broadcast_to(x[None], (count,) + x.shape), axes, 0, 0,...  15.5 us
    ppermute x3, starting transfers between devices, per_device(): lax.ppermute(shares[k], 'yhi', [(i, (i + k) % nb) for i in range(nb)])  13.3 us
    ppermute x4, starting transfers between devices, flip(): return lax.ppermute(x, 'core', [(0, 1), (1, 0)])  9.4 us
    ppermute x1, starting transfers between devices, per_device(): lax.ppermute(digits, ALL, swap_route(0))  8.29 us
    ppermute x1, starting transfers between devices, per_device(): mine = lax.ppermute(grad_embedded, ALL, across)  8.15 us
    ppermute x1, waiting for transfers between devices, per_device(): mine = lax.ppermute(grad_embedded, ALL, across)  7.77 us
  transfers between devices with their start and end apart: 20, of which 8 were waited for; matrix products, arithmetic and copies ran while one was open for 2% of the time, Pallas kernels for 5%

profile of v8, /device:TPU:1, one launch (start us, length us, event | category | flops | bytes accessed | tf_op | source)
XLA Modules:
  0.0 205.8 jit_solution(5044520924442657241)
XLA Ops:
  7.2 0.9 maximum_bitcast_fusion
  8.2 1.0 broadcast_in_dim.22
  9.2 10.9 %all-to-all-start = ((bf16[8,112,448]{2,1,0:T(8,128)(2,1)}), bf16[8,112,448]{2,1,0:T(8,128)(2,1)S(1)}, u32[]{:S(2)}, u32[]{:S(2)}) async-start(bf16[8,112,448]{2,1,0:T(8,128)(2,1)} %broadcast_in_dim.22), calls=%async_computation | async-start | bytes 1835008 | tf_op jit(solution)/shard_map/all_to_all | solution.py:22
  20.1 8.3 %collective-permute-start.3 = (bf16[2,128]{1,0:T(2,128)(2,1)S(1)}, bf16[2,128]{1,0:T(2,128)(2,1)S(1)}, u32[]{:S(2)}, u32[]{:S(2)}) collective-permute-start(bf16[2,128]{1,0:T(2,128)(2,1)S(1)} %pad_maximum_fusion.7), channel_id=1, source_target_pairs={{0,0},{1,1},{2,32},{3,33},{4,64},{5,65},{6,96},{7,97},{8,128},{9,1... | collective-permute-start | bytes 1544 | tf_op jit(solution)/shard_map/ppermute | solution.py:348
  28.4 1.9 collective-permute-start.2
  30.4 5.8 %collective-permute-start = (bf16[112,128]{1,0:T(8,128)(2,1)S(1)}, bf16[112,128]{1,0:T(8,128)(2,1)S(1)}, u32[]{:S(2)}, u32[]{:S(2)}) collective-permute-start(bf16[112,128]{1,0:T(8,128)(2,1)S(1)} %get-tuple-element.53), channel_id=1, source_target_pairs={{0,1},{1,0},{2,33},{3,32},{4,5},{5,4},{6,37},{7,36},{8,9},{9,8},{1... | collective-permute-start | bytes 86024 | tf_op jit(solution)/shard_map/ppermute | solution.py:353
  36.1 2.1 %collective-permute-start.1 = (bf16[112,128]{1,0:T(8,128)(2,1)S(1)}, bf16[112,128]{1,0:T(8,128)(2,1)S(1)}, u32[]{:S(2)}, u32[]{:S(2)}) collective-permute-start(bf16[112,128]{1,0:T(8,128)(2,1)S(1)} %get-tuple-element.54), channel_id=1, source_target_pairs={{0,0},{1,1},{2,32},{3,33},{4,4},{5,5},{6,36},{7,37},{8,8},{9,9},{1... | collective-permute-start | bytes 86024 | tf_op jit(solution)/shard_map/ppermute | solution.py:352
  38.4 7.2 %collective-permute-done.1 = bf16[112,128]{1,0:T(8,128)(2,1)S(1)} collective-permute-done((bf16[112,128]{1,0:T(8,128)(2,1)S(1)}, bf16[112,128]{1,0:T(8,128)(2,1)S(1)}, u32[]{:S(2)}, u32[]{:S(2)}) %collective-permute-start.1) | collective-permute-done | bytes 28704 | tf_op jit(solution)/shard_map/ppermute | solution.py:352
  45.6 0.8 all-to-all-done.weights_ref
  46.5 16.1 %all_to_all.30.own_ref = bf16[8,240,128]{2,1,0:T(8,128)(2,1)S(1)} all-to-all(bf16[8,240,128]{2,1,0:T(8,128)(2,1)S(1)} %broadcast_in_dim.23), channel_id=1, replica_groups=mesh['chip'=8,'core'=2,'z'=8,'yhi'=4] {'chip'}, dimensions={0} | all-to-all | bytes 983040 | tf_op jit(solution)/shard_map/all_to_all | solution.py:22
  62.6 1.9 collective-permute-start.4
  64.5 1.3 copy.28
  65.9 0.5 collective-permute-done.4.other_ref
  66.4 2.3 %shard_map.128 = bf16[8,112,256]{2,1,0:T(8,128)(2,1)S(1)} custom-call(s32[8,1,256]{2,1,0:T(1,128)S(1)} %bitcast.86, bf16[896,512]{1,0:T(8,128)(2,1)S(1)} %bitcast.84), custom_call_target="tpu_custom_call" | custom-call | flops 1879048192 | bytes 1376256 | tf_op jit(solution)/shard_map/pallas_call | solution.py:58
  68.7 2.0 collective-permute-start.5
  70.8 2.3 %shard_map.127 = bf16[8,112,256]{2,1,0:T(8,128)(2,1)S(1)} custom-call(s32[8,1,256]{2,1,0:T(1,128)S(1)} %bitcast.88, bf16[896,512]{1,0:T(8,128)(2,1)S(1)} %bitcast.85), custom_call_target="tpu_custom_call" | custom-call | flops 1879048192 | bytes 1376256 | tf_op jit(solution)/shard_map/pallas_call | solution.py:58
  73.1 0.9 add.70
  74.0 3.5 %all-to-all-start.2 = ((bf16[8,112,256]{2,1,0:T(8,128)(2,1)}), bf16[8,112,256]{2,1,0:T(8,128)(2,1)S(1)}, u32[]{:S(2)}, u32[]{:S(2)}) async-start(bf16[8,112,256]{2,1,0:T(8,128)(2,1)} %add.70), calls=%async_computation.2 | async-start | bytes 917504 | tf_op jit(solution)/shard_map/all_to_all | solution.py:376
  77.7 1.6 shard_map.129
  79.3 0.7 slice_bitcast_fusion.2
  80.0 3.9 %collective-permute-start.7 = (bf16[448,128]{1,0:T(8,128)(2,1)}, bf16[448,128]{1,0:T(8,128)(2,1)S(1)}, u32[]{:S(2)}, u32[]{:S(2)}) collective-permute-start(bf16[448,128]{1,0:T(8,128)(2,1)} %get-tuple-element.38), channel_id=1, source_target_pairs={{0,1},{1,2},{2,3},{3,0},{4,5},{5,6},{6,7},{7,4},{8,9},{9,10},{10,1... | collective-permute-start | bytes 344072 | tf_op jit(solution)/shard_map/ppermute | solution.py:371
  83.9 3.5 %collective-permute-start.9 = (bf16[448,128]{1,0:T(8,128)(2,1)S(1)}, bf16[448,128]{1,0:T(8,128)(2,1)S(1)}, u32[]{:S(2)}, u32[]{:S(2)}) collective-permute-start(bf16[448,128]{1,0:T(8,128)(2,1)S(1)} %get-tuple-element.39), channel_id=1, source_target_pairs={{0,3},{1,0},{2,1},{3,2},{4,7},{5,4},{6,5},{7,6},{8,11},{9,8},{10,9... | collective-permute-start | bytes 344072 | tf_op jit(solution)/shard_map/ppermute | solution.py:371
  87.4 5.9 %collective-permute-start.8 = (bf16[448,128]{1,0:T(8,128)(2,1)S(1)}, bf16[448,128]{1,0:T(8,128)(2,1)}, u32[]{:S(2)}, u32[]{:S(2)}) collective-permute-start(bf16[448,128]{1,0:T(8,128)(2,1)S(1)} %get-tuple-element.40), channel_id=1, source_target_pairs={{0,2},{1,3},{2,0},{3,1},{4,6},{5,7},{6,4},{7,5},{8,10},{9,11},{10,... | collective-permute-start | bytes 344072 | tf_op jit(solution)/shard_map/ppermute | solution.py:371
  93.4 4.4 %collective-permute-start.6 = (bf16[224,128]{1,0:T(8,128)(2,1)S(1)}, bf16[224,128]{1,0:T(8,128)(2,1)S(1)}, u32[]{:S(2)}, u32[]{:S(2)}) collective-permute-start(bf16[224,128]{1,0:T(8,128)(2,1)S(1)} %pad_maximum_fusion.3), channel_id=1, source_target_pairs={{0,0},{1,1},{2,32},{3,33},{4,64},{5,65},{6,96},{7,97},{8,128},{9,1... | collective-permute-start | bytes 172040 | tf_op jit(solution)/shard_map/ppermute | solution.py:379
  97.8 2.0 collective-permute-done.8
  99.9 1.0 fusion.1
  100.8 2.1 %collective-permute-done.6 = bf16[224,128]{1,0:T(8,128)(2,1)S(1)} collective-permute-done((bf16[224,128]{1,0:T(8,128)(2,1)S(1)}, bf16[224,128]{1,0:T(8,128)(2,1)S(1)}, u32[]{:S(2)}, u32[]{:S(2)}) %collective-permute-start.6) | collective-permute-done | bytes 57376 | tf_op jit(solution)/shard_map/ppermute | solution.py:379
  103.0 0.1 fusion.12
  103.2 2.1 %collective-permute-start.10 = (f32[4,128]{1,0:T(4,128)S(1)}, f32[4,128]{1,0:T(4,128)S(1)}, u32[]{:S(2)}, u32[]{:S(2)}) collective-permute-start(f32[4,128]{1,0:T(4,128)S(1)} %pad_maximum_fusion.5), channel_id=1, source_target_pairs={{0,1},{1,0},{2,3},{3,2},{4,5},{5,4},{6,7},{7,6},{8,9},{9,8},{10,11... | collective-permute-start | bytes 6152 | tf_op jit(solution)/shard_map/ppermute | solution.py:393
  105.4 3.2 %collective-permute-done.10 = f32[4,128]{1,0:T(4,128)S(1)} collective-permute-done((f32[4,128]{1,0:T(4,128)S(1)}, f32[4,128]{1,0:T(4,128)S(1)}, u32[]{:S(2)}, u32[]{:S(2)}) %collective-permute-start.10) | collective-permute-done | bytes 2080 | tf_op jit(solution)/shard_map/ppermute | solution.py:393
  108.6 16.5 %all_to_all.31 = f32[16,6,128]{2,1,0:T(8,128)S(1)} all-to-all(f32[16,6,128]{2,1,0:T(8,128)S(1)} %broadcast_in_dim.28), channel_id=1, replica_groups=mesh['chip'=8,'core'=2,'z'=8,'yhi'=4] {'chip','core'}, dimensions={0} | all-to-all | bytes 98304 | tf_op jit(solution)/shard_map/all_to_all | solution.py:22
  125.3 0.8 multiply_reduce_fusion
  126.3 0.8 broadcast_in_dim.31
  127.1 4.7 %all-to-all-start.4 = ((bf16[4,480,128]{2,1,0:T(8,128)(2,1)}), bf16[4,480,128]{2,1,0:T(8,128)(2,1)S(1)}, u32[]{:S(2)}, u32[]{:S(2)}) async-start(bf16[4,480,128]{2,1,0:T(8,128)(2,1)} %broadcast_in_dim.31), calls=%async_computation.4 | async-start | bytes 983040 | tf_op jit(solution)/shard_map/all_to_all | solution.py:22
  131.8 8.2 %collective-permute-start.11 = (bf16[224,128]{1,0:T(8,128)(2,1)S(1)}, bf16[224,128]{1,0:T(8,128)(2,1)S(1)}, u32[]{:S(2)}, u32[]{:S(2)}) collective-permute-start(bf16[224,128]{1,0:T(8,128)(2,1)S(1)} %get-tuple-element.42), channel_id=1, source_target_pairs={{0,0},{1,1},{2,32},{3,33},{4,64},{5,65},{6,96},{7,97},{8,128},{9,1... | collective-permute-start | bytes 172040 | tf_op jit(solution)/shard_map/ppermute | solution.py:440
  140.0 7.8 %collective-permute-done.11 = bf16[224,128]{1,0:T(8,128)(2,1)S(1)} collective-permute-done((bf16[224,128]{1,0:T(8,128)(2,1)S(1)}, bf16[224,128]{1,0:T(8,128)(2,1)S(1)}, u32[]{:S(2)}, u32[]{:S(2)}) %collective-permute-start.11) | collective-permute-done | bytes 57376 | tf_op jit(solution)/shard_map/ppermute | solution.py:440
  147.7 3.3 %shard_map.130 = (bf16[8,224,128]{2,1,0:T(8,128)(2,1)S(1)}, bf16[8,224,128]{2,1,0:T(8,128)(2,1)}, bf16[8,176,448]{2,1,0:T(8,128)(2,1)}) custom-call(s32[2]{0:T(128)S(1)} %pad_add_fusion.1.place_ref, bf16[8,112,448]{2,1,0:T(8,128)(2,1)S(1)} %all-to-all-done.weights_ref, bf16[8,240,128]{2,1,0:T(8,128)(2,1)S(1)} %all_to_all.30.own_ref, ...), custom_call_target="tpu_custom_call" | custom-call | flops 822083584 | bytes 4063232 | tf_op jit(solution)/shard_map/pallas_call | solution.py:233
  151.1 1.9 collective-permute-start.12
  153.0 2.0 collective-permute-done.12
  155.0 0.1 add_convert_fusion
  155.3 22.1 %all_to_all.32 = bf16[8,448,128]{2,1,0:T(8,128)(2,1)S(1)} all-to-all(bf16[8,448,128]{2,1,0:T(8,128)(2,1)S(1)} %pad_maximum_fusion), channel_id=1, replica_groups=mesh['chip'=8,'core'=2,'z'=8,'yhi'=4] {'chip'}, dimensions={0} | all-to-all | bytes 1835008 | tf_op jit(solution)/shard_map/all_to_all | solution.py:446
  177.5 3.5 %collective-permute-start.15 = (bf16[8,224,128]{2,1,0:T(8,128)(2,1)S(1)}, bf16[8,224,128]{2,1,0:T(8,128)(2,1)S(1)}, u32[]{:S(2)}, u32[]{:S(2)}) collective-permute-start(bf16[8,224,128]{2,1,0:T(8,128)(2,1)S(1)} %get-tuple-element.36.own_ref), channel_id=1, source_target_pairs={{0,32},{32,0},{1,33},{33,1},{2,34},{34,2},{3,35},{35,3},{4,36},{36... | collective-permute-start | bytes 1376264 | tf_op jit(solution)/shard_map/ppermute | solution.py:341
  181.0 2.2 %collective-permute-start.14 = (bf16[112,128]{1,0:T(8,128)(2,1)S(1)}, bf16[112,128]{1,0:T(8,128)(2,1)S(1)}, u32[]{:S(2)}, u32[]{:S(2)}) collective-permute-start(bf16[112,128]{1,0:T(8,128)(2,1)S(1)} %get-tuple-element.47), channel_id=1, source_target_pairs={{1,0},{0,1},{33,2},{32,3},{5,4},{4,5},{37,6},{36,7},{9,8},{8,9},{4... | collective-permute-start | bytes 86024 | tf_op jit(solution)/shard_map/ppermute | solution.py:457
  183.3 6.2 %collective-permute-start.13 = (bf16[112,128]{1,0:T(8,128)(2,1)S(1)}, bf16[112,128]{1,0:T(8,128)(2,1)S(1)}, u32[]{:S(2)}, u32[]{:S(2)}) collective-permute-start(bf16[112,128]{1,0:T(8,128)(2,1)S(1)} %get-tuple-element.48), channel_id=1, source_target_pairs={{0,0},{1,1},{32,2},{33,3},{4,4},{5,5},{36,6},{37,7},{8,8},{9,9},{4... | collective-permute-start | bytes 86024 | tf_op jit(solution)/shard_map/ppermute | solution.py:456
  189.5 6.5 %shard_map.131 = (f32[112,4096]{1,0:T(8,128)}, f32[8,128]{1,0:T(8,128)S(1)}) custom-call(s32[16,1,256]{2,1,0:T(1,128)S(1)} %pad_add_fusion.ids_ref, bf16[8,224,128]{2,1,0:T(8,128)(2,1)S(1)} %get-tuple-element.36.own_ref, bf16[8,224,128]{2,1,0:T(8,128)(2,1)S(1)} %collective-permute-done.15.other_ref), custom_call_target="tpu_custom_call" | custom-call | tf_op jit(solution)/shard_map/pallas_call | solution.py:118
  196.0 0.6 copy-done
  196.7 0.6 copy-done.4
  197.3 1.7 shard_map.132
  (73 shorter events, 1.4 us)
Async XLA Ops:
  7.2 12.9 %copy-start.8 = (s32[128]{0:T(128)S(1)}, s32[128]{0:T(128)}, u32[]{:S(2)}) copy-start(s32[128]{0:T(128)} %param.8) | copy-start | bytes 1540
  7.2 23.2 %copy-start.3 = (bf16[128,224]{0,1:T(8,128)(2,1)S(1)}, bf16[128,224]{0,1:T(8,128)(2,1)}, u32[]{:S(2)}) copy-start(bf16[128,224]{0,1:T(8,128)(2,1)} %param.15) | copy-start | bytes 172036
  9.2 37.2 %all-to-all-start = ((bf16[8,112,448]{2,1,0:T(8,128)(2,1)}), bf16[8,112,448]{2,1,0:T(8,128)(2,1)S(1)}, u32[]{:S(2)}, u32[]{:S(2)}) async-start(bf16[8,112,448]{2,1,0:T(8,128)(2,1)} %broadcast_in_dim.22), calls=%async_computation | async-start | bytes 1835008 | tf_op jit(solution)/shard_map/all_to_all | solution.py:22
  20.1 18.2 %collective-permute-start.3 = (bf16[2,128]{1,0:T(2,128)(2,1)S(1)}, bf16[2,128]{1,0:T(2,128)(2,1)S(1)}, u32[]{:S(2)}, u32[]{:S(2)}) collective-permute-start(bf16[2,128]{1,0:T(2,128)(2,1)S(1)} %pad_maximum_fusion.7), channel_id=1, source_target_pairs={{0,0},{1,1},{2,32},{3,33},{4,64},{5,65},{6,96},{7,97},{8,128},{9,1... | collective-permute-start | bytes 1544 | tf_op jit(solution)/shard_map/ppermute | solution.py:348
  28.4 9.9 %collective-permute-start.2 = (bf16[2,128]{1,0:T(2,128)(2,1)S(1)}, bf16[2,128]{1,0:T(2,128)(2,1)S(1)}, u32[]{:S(2)}, u32[]{:S(2)}) collective-permute-start(bf16[2,128]{1,0:T(2,128)(2,1)S(1)} %pad_maximum_fusion.7), channel_id=1, source_target_pairs={{0,1},{1,0},{2,33},{3,32},{4,65},{5,64},{6,97},{7,96},{8,129},{9,1... | collective-permute-start | bytes 1544 | tf_op jit(solution)/shard_map/ppermute | solution.py:348
  30.4 8.0 %collective-permute-start = (bf16[112,128]{1,0:T(8,128)(2,1)S(1)}, bf16[112,128]{1,0:T(8,128)(2,1)S(1)}, u32[]{:S(2)}, u32[]{:S(2)}) collective-permute-start(bf16[112,128]{1,0:T(8,128)(2,1)S(1)} %get-tuple-element.53), channel_id=1, source_target_pairs={{0,1},{1,0},{2,33},{3,32},{4,5},{5,4},{6,37},{7,36},{8,9},{9,8},{1... | collective-permute-start | bytes 86024 | tf_op jit(solution)/shard_map/ppermute | solution.py:353
  36.1 9.5 %collective-permute-start.1 = (bf16[112,128]{1,0:T(8,128)(2,1)S(1)}, bf16[112,128]{1,0:T(8,128)(2,1)S(1)}, u32[]{:S(2)}, u32[]{:S(2)}) collective-permute-start(bf16[112,128]{1,0:T(8,128)(2,1)S(1)} %get-tuple-element.54), channel_id=1, source_target_pairs={{0,0},{1,1},{2,32},{3,33},{4,4},{5,5},{6,36},{7,37},{8,8},{9,9},{1... | collective-permute-start | bytes 86024 | tf_op jit(solution)/shard_map/ppermute | solution.py:352
  62.6 3.7 %collective-permute-start.4 = (bf16[8,240,128]{2,1,0:T(8,128)(2,1)S(1)}, bf16[8,240,128]{2,1,0:T(8,128)(2,1)S(1)}, u32[]{:S(2)}, u32[]{:S(2)}) collective-permute-start(bf16[8,240,128]{2,1,0:T(8,128)(2,1)S(1)} %all_to_all.30.own_ref), channel_id=1, source_target_pairs={{0,32},{32,0},{1,33},{33,1},{2,34},{34,2},{3,35},{35,3},{4,36},{36... | collective-permute-start | bytes 1474568 | tf_op jit(solution)/shard_map/ppermute | solution.py:341
  68.7 4.4 %collective-permute-start.5 = (bf16[8,112,256]{2,1,0:T(8,128)(2,1)S(1)}, bf16[8,112,256]{2,1,0:T(8,128)(2,1)S(1)}, u32[]{:S(2)}, u32[]{:S(2)}) collective-permute-start(bf16[8,112,256]{2,1,0:T(8,128)(2,1)S(1)} %shard_map.128), channel_id=1, source_target_pairs={{0,32},{32,0},{1,33},{33,1},{2,34},{34,2},{3,35},{35,3},{4,36},{36... | collective-permute-start | bytes 1376264 | tf_op jit(solution)/shard_map/ppermute | solution.py:341
  73.1 4.5 %copy-start.7 = (f32[224]{0:T(256)S(1)}, f32[224]{0:T(256)}, u32[]{:S(2)}) copy-start(f32[224]{0:T(256)} %param.11) | copy-start | bytes 2692
  74.0 19.3 %all-to-all-start.2 = ((bf16[8,112,256]{2,1,0:T(8,128)(2,1)}), bf16[8,112,256]{2,1,0:T(8,128)(2,1)S(1)}, u32[]{:S(2)}, u32[]{:S(2)}) async-start(bf16[8,112,256]{2,1,0:T(8,128)(2,1)} %add.70), calls=%async_computation.2 | async-start | bytes 917504 | tf_op jit(solution)/shard_map/all_to_all | solution.py:376
  77.6 70.2 %copy-start.1 = (s32[2]{0:T(128)}, s32[2]{0:T(128)S(1)}, u32[]{:S(2)}) copy-start(s32[2]{0:T(128)S(1)} %pad_add_fusion.1.place_ref) | copy-start | bytes 28
  77.7 25.3 %copy-start.2 = (bf16[128,224]{0,1:T(8,128)(2,1)S(1)}, bf16[128,224]{0,1:T(8,128)(2,1)}, u32[]{:S(2)}) copy-start(bf16[128,224]{0,1:T(8,128)(2,1)} %param.9) | copy-start | bytes 172036
  77.7 25.3 %copy-start.6 = (f32[224]{0:T(256)S(1)}, f32[224]{0:T(256)}, u32[]{:S(2)}) copy-start(f32[224]{0:T(256)} %param.12) | copy-start | bytes 2692
  80.0 17.8 %collective-permute-start.7 = (bf16[448,128]{1,0:T(8,128)(2,1)}, bf16[448,128]{1,0:T(8,128)(2,1)S(1)}, u32[]{:S(2)}, u32[]{:S(2)}) collective-permute-start(bf16[448,128]{1,0:T(8,128)(2,1)} %get-tuple-element.38), channel_id=1, source_target_pairs={{0,1},{1,2},{2,3},{3,0},{4,5},{5,6},{6,7},{7,4},{8,9},{9,10},{10,1... | collective-permute-start | bytes 344072 | tf_op jit(solution)/shard_map/ppermute | solution.py:371
  83.9 13.9 %collective-permute-start.9 = (bf16[448,128]{1,0:T(8,128)(2,1)S(1)}, bf16[448,128]{1,0:T(8,128)(2,1)S(1)}, u32[]{:S(2)}, u32[]{:S(2)}) collective-permute-start(bf16[448,128]{1,0:T(8,128)(2,1)S(1)} %get-tuple-element.39), channel_id=1, source_target_pairs={{0,3},{1,0},{2,1},{3,2},{4,7},{5,4},{6,5},{7,6},{8,11},{9,8},{10,9... | collective-permute-start | bytes 344072 | tf_op jit(solution)/shard_map/ppermute | solution.py:371
  87.4 12.5 %collective-permute-start.8 = (bf16[448,128]{1,0:T(8,128)(2,1)S(1)}, bf16[448,128]{1,0:T(8,128)(2,1)}, u32[]{:S(2)}, u32[]{:S(2)}) collective-permute-start(bf16[448,128]{1,0:T(8,128)(2,1)S(1)} %get-tuple-element.40), channel_id=1, source_target_pairs={{0,2},{1,3},{2,0},{3,1},{4,6},{5,7},{6,4},{7,5},{8,10},{9,11},{10,... | collective-permute-start | bytes 344072 | tf_op jit(solution)/shard_map/ppermute | solution.py:371
  93.4 9.6 %collective-permute-start.6 = (bf16[224,128]{1,0:T(8,128)(2,1)S(1)}, bf16[224,128]{1,0:T(8,128)(2,1)S(1)}, u32[]{:S(2)}, u32[]{:S(2)}) collective-permute-start(bf16[224,128]{1,0:T(8,128)(2,1)S(1)} %pad_maximum_fusion.3), channel_id=1, source_target_pairs={{0,0},{1,1},{2,32},{3,33},{4,64},{5,65},{6,96},{7,97},{8,128},{9,1... | collective-permute-start | bytes 172040 | tf_op jit(solution)/shard_map/ppermute | solution.py:379
  103.2 5.4 %collective-permute-start.10 = (f32[4,128]{1,0:T(4,128)S(1)}, f32[4,128]{1,0:T(4,128)S(1)}, u32[]{:S(2)}, u32[]{:S(2)}) collective-permute-start(f32[4,128]{1,0:T(4,128)S(1)} %pad_maximum_fusion.5), channel_id=1, source_target_pairs={{0,1},{1,0},{2,3},{3,2},{4,5},{5,4},{6,7},{7,6},{8,9},{9,8},{10,11... | collective-permute-start | bytes 6152 | tf_op jit(solution)/shard_map/ppermute | solution.py:393
  127.1 20.6 %all-to-all-start.4 = ((bf16[4,480,128]{2,1,0:T(8,128)(2,1)}), bf16[4,480,128]{2,1,0:T(8,128)(2,1)S(1)}, u32[]{:S(2)}, u32[]{:S(2)}) async-start(bf16[4,480,128]{2,1,0:T(8,128)(2,1)} %broadcast_in_dim.31), calls=%async_computation.4 | async-start | bytes 983040 | tf_op jit(solution)/shard_map/all_to_all | solution.py:22
  131.8 64.9 %reduce-scatter.2.cloned.1.call-start = ((), (), s32[]{:S(2)}) async-start(), calls=%async_computation.7 | async-start | bytes 1622016 | tf_op jit(solution)/shard_map/reduce_scatter | solution.py:458
  131.8 15.9 %collective-permute-start.11 = (bf16[224,128]{1,0:T(8,128)(2,1)S(1)}, bf16[224,128]{1,0:T(8,128)(2,1)S(1)}, u32[]{:S(2)}, u32[]{:S(2)}) collective-permute-start(bf16[224,128]{1,0:T(8,128)(2,1)S(1)} %get-tuple-element.42), channel_id=1, source_target_pairs={{0,0},{1,1},{2,32},{3,33},{4,64},{5,65},{6,96},{7,97},{8,128},{9,1... | collective-permute-start | bytes 172040 | tf_op jit(solution)/shard_map/ppermute | solution.py:440
  151.1 3.9 %collective-permute-start.12 = (bf16[8,224,128]{2,1,0:T(8,128)(2,1)}, bf16[8,224,128]{2,1,0:T(8,128)(2,1)S(1)}, u32[]{:S(2)}, u32[]{:S(2)}) collective-permute-start(bf16[8,224,128]{2,1,0:T(8,128)(2,1)} %get-tuple-element.24), channel_id=1, source_target_pairs={{0,32},{32,0},{1,33},{33,1},{2,34},{34,2},{3,35},{35,3},{4,36},{36... | collective-permute-start | bytes 1376264 | tf_op jit(solution)/shard_map/ppermute | solution.py:341
  177.5 12.1 %collective-permute-start.15 = (bf16[8,224,128]{2,1,0:T(8,128)(2,1)S(1)}, bf16[8,224,128]{2,1,0:T(8,128)(2,1)S(1)}, u32[]{:S(2)}, u32[]{:S(2)}) collective-permute-start(bf16[8,224,128]{2,1,0:T(8,128)(2,1)S(1)} %get-tuple-element.36.own_ref), channel_id=1, source_target_pairs={{0,32},{32,0},{1,33},{33,1},{2,34},{34,2},{3,35},{35,3},{4,36},{36... | collective-permute-start | bytes 1376264 | tf_op jit(solution)/shard_map/ppermute | solution.py:341
  181.0 15.6 %collective-permute-start.14 = (bf16[112,128]{1,0:T(8,128)(2,1)S(1)}, bf16[112,128]{1,0:T(8,128)(2,1)S(1)}, u32[]{:S(2)}, u32[]{:S(2)}) collective-permute-start(bf16[112,128]{1,0:T(8,128)(2,1)S(1)} %get-tuple-element.47), channel_id=1, source_target_pairs={{1,0},{0,1},{33,2},{32,3},{5,4},{4,5},{37,6},{36,7},{9,8},{8,9},{4... | collective-permute-start | bytes 86024 | tf_op jit(solution)/shard_map/ppermute | solution.py:457
  183.3 13.4 %collective-permute-start.13 = (bf16[112,128]{1,0:T(8,128)(2,1)S(1)}, bf16[112,128]{1,0:T(8,128)(2,1)S(1)}, u32[]{:S(2)}, u32[]{:S(2)}) collective-permute-start(bf16[112,128]{1,0:T(8,128)(2,1)S(1)} %get-tuple-element.48), channel_id=1, source_target_pairs={{0,0},{1,1},{32,2},{33,3},{4,4},{5,5},{36,6},{37,7},{8,8},{9,9},{4... | collective-permute-start | bytes 86024 | tf_op jit(solution)/shard_map/ppermute | solution.py:456
  196.0 0.6 copy-start
  196.6 0.6 copy-start.4
  196.6 0.6 copy-start.5
Sparse Core Ops, SparseCore 0:
  153.1 37.3 reduce-scatter.1

commit v9 on v8

--- a/solution.py
+++ b/solution.py
@@ -113,7 +113,7 @@
 def scatter(ids, own, other, entries):
     blocks, rows, toks = own.shape
     cols = rows // 2
-    parts = 4
+    parts = blocks
     half = blocks // parts
     return pl.pallas_call(
         scatter_kernel,
@@ -166,7 +166,7 @@
     for b in range(nb):
         half, pair = b % 2 * cw, b // 2 * 2
         share = [whole[pair + x][half : half + cw] for x in range(2)] + [whole[b][2 * cw :]]
-        out_ref[lax.rem(b + nb - place_ref[1], nb)] = jnp.concatenate(share, axis=0)
+        out_ref[b] = jnp.concatenate(share, axis=0)
 
 
 def grad_products(place, weights, own, other, nb):
@@ -366,13 +366,10 @@
     own_ids, other_ids = ids_of(own), ids_of(other)
 
     shares = grad_products(place, weights, own, other, nb)
-    grads = shares[0].astype(F32)
-    for k in range(1, nb):
-        grads += lax.ppermute(
-            shares[k], "yhi", [(i, (i + k) % nb) for i in range(nb)]
-        ).astype(F32)
-
+    shares = lax.all_to_all(shares, "yhi", 0, 0, tiled=True)
     pieces = lookup(own_ids, table) + flip(lookup(other_ids, table))
+    pieces, shares = lax.optimization_barrier((pieces, shares))
+    grads = jnp.sum(shares.astype(F32), axis=0)
     pieces = lax.all_to_all(pieces, "chip", 0, 0, tiled=True)
     cols = jnp.sum(pieces.astype(F32), axis=0).astype(BF16)
     embed = jnp.concatenate([cols[:, :toks], cols[:, toks:]], axis=0)

time: 207 us -> 210 us (1.014)
  waiting for transfers between devices: 25.8 us -> 32.6 us
    ppermute x3 -> x0, starting transfers between devices: 13.3 us -> none  [per_device(): lax.ppermute(shares[k], 'yhi', [(i, (i + k) % nb) for i in range(nb)])]
    all_to_all x1, waiting for transfers between devices: 0.01 us -> 6.63 us  [per_device(): pieces = lax.all_to_all(pieces, 'chip', 0, 0, tiled=True)]
    all_to_all x0 -> x1, starting transfers between devices: none -> 5.03 us  [per_device(): shares = lax.all_to_all(shares, 'yhi', 0, 0, tiled=True)]
    all_to_all x0 -> x1, waiting for transfers between devices: none -> 4.92 us  [per_device(): shares = lax.all_to_all(shares, 'yhi', 0, 0, tiled=True)]
    ppermute x1, starting transfers between devices: 4.39 us -> 8.25 us  [per_device(): embed = lax.ppermute(embed, ALL, across).astype(F32)]
    ppermute x1, starting transfers between devices: 2.14 us -> 5.62 us  [per_device(): halves += lax.ppermute(halves, 'yhi', [(i, i ^ 1) for i in range(nb)])]
    ppermute x1, waiting for transfers between devices: 3.24 us -> 0.96 us  [per_device(): halves += lax.ppermute(halves, 'yhi', [(i, i ^ 1) for i in range(nb)])]
  transfers between devices with their start and end apart: 20 -> 18, of which waited for: 8 -> 9; matrix products, arithmetic and copies ran while one was open for 2% -> 1% of each run, Pallas kernels for 5% -> 5%
where the time goes in v9:
time: 210 us; the launch traced here: 209 us
  starting transfers between devices  82.7 us (39%)
  blocking collectives  53.1 us (25%)
  waiting for transfers between devices  32.6 us (16%)
  Pallas kernels  17.8 us (8%)
  between operations  14.5 us (7%)
  local copies, waits for them, and re-layouts  4.67 us (2%)
  other arithmetic  3.8 us (2%)
    all_to_all x2, blocking collectives, gather(): lax.all_to_all(jnp.broadcast_to(x[None], (count,) + x.shape), axes, 0, 0,...  31.7 us
    all_to_all x1, blocking collectives, per_device(): lax.all_to_all(jnp.concatenate([terms, mine], axis=1), 'chip', 0, 0, tile...  21.4 us
    all_to_all x2, starting transfers between devices, gather(): lax.all_to_all(jnp.broadcast_to(x[None], (count,) + x.shape), axes, 0, 0,...  16.3 us
    ppermute x4, starting transfers between devices, flip(): return lax.ppermute(x, 'core', [(0, 1), (1, 0)])  9.92 us
    ppermute x1, starting transfers between devices, per_device(): lax.ppermute(digits, ALL, swap_route(0))  8.29 us
    ppermute x1, starting transfers between devices, per_device(): embed = lax.ppermute(embed, ALL, across).astype(F32)  8.25 us
    ppermute x1, starting transfers between devices, per_device(): mine = lax.ppermute(grad_embedded, ALL, across)  8.15 us
    ppermute x1, waiting for transfers between devices, per_device(): mine = lax.ppermute(grad_embedded, ALL, across)  7.77 us
  transfers between devices with their start and end apart: 18, of which 9 were waited for; matrix products, arithmetic and copies ran while one was open for 1% of the time, Pallas kernels for 5%

profile of v9, /device:TPU:1, one launch (start us, length us, event | category | flops | bytes accessed | tf_op | source)
XLA Modules:
  0.0 209.1 jit_solution(17463549118090580769)
XLA Ops:
  7.2 0.9 maximum_bitcast_fusion
  8.1 0.1 copy.18
  8.2 1.0 broadcast_in_dim.22
  9.2 10.9 %all-to-all-start = ((bf16[8,112,448]{2,1,0:T(8,128)(2,1)}), bf16[8,112,448]{2,1,0:T(8,128)(2,1)S(1)}, u32[]{:S(2)}, u32[]{:S(2)}) async-start(bf16[8,112,448]{2,1,0:T(8,128)(2,1)} %broadcast_in_dim.22), calls=%async_computation | async-start | bytes 1835008 | tf_op jit(solution)/shard_map/all_to_all | solution.py:22
  20.1 8.3 %collective-permute-start.3 = (bf16[2,128]{1,0:T(2,128)(2,1)S(1)}, bf16[2,128]{1,0:T(2,128)(2,1)S(1)}, u32[]{:S(2)}, u32[]{:S(2)}) collective-permute-start(bf16[2,128]{1,0:T(2,128)(2,1)S(1)} %pad_maximum_fusion.7), channel_id=1, source_target_pairs={{0,0},{1,1},{2,32},{3,33},{4,64},{5,65},{6,96},{7,97},{8,128},{9,1... | collective-permute-start | bytes 1544 | tf_op jit(solution)/shard_map/ppermute | solution.py:348
  28.4 1.9 collective-permute-start.2
  30.4 5.8 %collective-permute-start = (bf16[112,128]{1,0:T(8,128)(2,1)S(1)}, bf16[112,128]{1,0:T(8,128)(2,1)S(1)}, u32[]{:S(2)}, u32[]{:S(2)}) collective-permute-start(bf16[112,128]{1,0:T(8,128)(2,1)S(1)} %get-tuple-element.54), channel_id=1, source_target_pairs={{0,1},{1,0},{2,33},{3,32},{4,5},{5,4},{6,37},{7,36},{8,9},{9,8},{1... | collective-permute-start | bytes 86024 | tf_op jit(solution)/shard_map/ppermute | solution.py:353
  36.1 2.1 %collective-permute-start.1 = (bf16[112,128]{1,0:T(8,128)(2,1)S(1)}, bf16[112,128]{1,0:T(8,128)(2,1)S(1)}, u32[]{:S(2)}, u32[]{:S(2)}) collective-permute-start(bf16[112,128]{1,0:T(8,128)(2,1)S(1)} %get-tuple-element.55), channel_id=1, source_target_pairs={{0,0},{1,1},{2,32},{3,33},{4,4},{5,5},{6,36},{7,37},{8,8},{9,9},{1... | collective-permute-start | bytes 86024 | tf_op jit(solution)/shard_map/ppermute | solution.py:352
  38.4 7.2 %collective-permute-done.1 = bf16[112,128]{1,0:T(8,128)(2,1)S(1)} collective-permute-done((bf16[112,128]{1,0:T(8,128)(2,1)S(1)}, bf16[112,128]{1,0:T(8,128)(2,1)S(1)}, u32[]{:S(2)}, u32[]{:S(2)}) %collective-permute-start.1) | collective-permute-done | bytes 28704 | tf_op jit(solution)/shard_map/ppermute | solution.py:352
  45.6 0.8 all-to-all-done.weights_ref
  46.5 16.1 %all_to_all.35.own_ref = bf16[8,240,128]{2,1,0:T(8,128)(2,1)S(1)} all-to-all(bf16[8,240,128]{2,1,0:T(8,128)(2,1)S(1)} %broadcast_in_dim.23), channel_id=1, replica_groups=mesh['chip'=8,'core'=2,'z'=8,'yhi'=4] {'chip'}, dimensions={0} | all-to-all | bytes 983040 | tf_op jit(solution)/shard_map/all_to_all | solution.py:22
  62.6 1.9 collective-permute-start.4
  64.5 1.3 copy.28
  65.9 0.4 collective-permute-done.4.other_ref
  66.4 2.3 %shard_map.129 = bf16[4,448,128]{2,1,0:T(8,128)(2,1)} custom-call(s32[2]{0:T(128)S(1)} %pad_add_fusion.1.place_ref, bf16[8,112,448]{2,1,0:T(8,128)(2,1)S(1)} %all-to-all-done.weights_ref, bf16[8,240,128]{2,1,0:T(8,128)(2,1)S(1)} %all_to_all.35.own_ref, bf16[8,240,128]{2,1,0:T(8,128)(2,1)S(1)} %collective-permute-done.4.other_ref), custom_call_target="tpu_custom_call" | custom-call | flops 411041792 | bytes 2244608 | tf_op jit(solution)/shard_map/pallas_call | solution.py:176
  68.7 5.0 %all-to-all-start.2 = ((bf16[4,448,128]{2,1,0:T(8,128)(2,1)}), bf16[4,448,128]{2,1,0:T(8,128)(2,1)S(1)}, u32[]{:S(2)}, u32[]{:S(2)}) async-start(bf16[4,448,128]{2,1,0:T(8,128)(2,1)} %shard_map.129), calls=%async_computation.2 | async-start | bytes 917504 | tf_op jit(solution)/shard_map/all_to_all | solution.py:369
  73.8 2.3 %shard_map.128 = bf16[8,112,256]{2,1,0:T(8,128)(2,1)S(1)} custom-call(s32[8,1,256]{2,1,0:T(1,128)S(1)} %bitcast.75, bf16[896,512]{1,0:T(8,128)(2,1)S(1)} %bitcast.73), custom_call_target="tpu_custom_call" | custom-call | flops 1879048192 | bytes 1376256 | tf_op jit(solution)/shard_map/pallas_call | solution.py:58
  76.1 2.6 %collective-permute-start.5 = (bf16[8,112,256]{2,1,0:T(8,128)(2,1)S(1)}, bf16[8,112,256]{2,1,0:T(8,128)(2,1)S(1)}, u32[]{:S(2)}, u32[]{:S(2)}) collective-permute-start(bf16[8,112,256]{2,1,0:T(8,128)(2,1)S(1)} %shard_map.128), channel_id=1, source_target_pairs={{0,32},{32,0},{1,33},{33,1},{2,34},{34,2},{3,35},{35,3},{4,36},{36... | collective-permute-start | bytes 1376264 | tf_op jit(solution)/shard_map/ppermute | solution.py:341
  78.7 2.3 %shard_map.127 = bf16[8,112,256]{2,1,0:T(8,128)(2,1)S(1)} custom-call(s32[8,1,256]{2,1,0:T(1,128)S(1)} %bitcast.77, bf16[896,512]{1,0:T(8,128)(2,1)S(1)} %bitcast.74), custom_call_target="tpu_custom_call" | custom-call | flops 1879048192 | bytes 1376256 | tf_op jit(solution)/shard_map/pallas_call | solution.py:58
  81.1 0.9 add.61
  82.0 4.9 %all-to-all-done.2 = bf16[4,448,128]{2,1,0:T(8,128)(2,1)S(1)} async-done(((bf16[4,448,128]{2,1,0:T(8,128)(2,1)}), bf16[4,448,128]{2,1,0:T(8,128)(2,1)S(1)}, u32[]{:S(2)}, u32[]{:S(2)}) %all-to-all-start.2) | async-done | bytes 458784 | tf_op jit(solution)/shard_map/all_to_all | solution.py:369
  86.9 3.5 %all-to-all-start.3 = ((bf16[8,112,256]{2,1,0:T(8,128)(2,1)}), bf16[8,112,256]{2,1,0:T(8,128)(2,1)S(1)}, u32[]{:S(2)}, u32[]{:S(2)}) async-start(bf16[8,112,256]{2,1,0:T(8,128)(2,1)} %add.61), calls=%async_computation.3 | async-start | bytes 917504 | tf_op jit(solution)/shard_map/all_to_all | solution.py:373
  90.5 6.6 %all-to-all-done.3 = bf16[8,112,256]{2,1,0:T(8,128)(2,1)S(1)} async-done(((bf16[8,112,256]{2,1,0:T(8,128)(2,1)}), bf16[8,112,256]{2,1,0:T(8,128)(2,1)S(1)}, u32[]{:S(2)}, u32[]{:S(2)}) %all-to-all-start.3) | async-done | bytes 458784 | tf_op jit(solution)/shard_map/all_to_all | solution.py:373
  97.3 8.2 %collective-permute-start.6 = (bf16[224,128]{1,0:T(8,128)(2,1)S(1)}, bf16[224,128]{1,0:T(8,128)(2,1)S(1)}, u32[]{:S(2)}, u32[]{:S(2)}) collective-permute-start(bf16[224,128]{1,0:T(8,128)(2,1)S(1)} %pad_maximum_fusion.3), channel_id=1, source_target_pairs={{0,0},{1,1},{2,32},{3,33},{4,64},{5,65},{6,96},{7,97},{8,128},{9,1... | collective-permute-start | bytes 172040 | tf_op jit(solution)/shard_map/ppermute | solution.py:376
  105.6 1.8 collective-permute-done.6
  107.4 0.1 fusion.10
  107.6 5.6 %collective-permute-start.7 = (f32[4,128]{1,0:T(4,128)S(1)}, f32[4,128]{1,0:T(4,128)S(1)}, u32[]{:S(2)}, u32[]{:S(2)}) collective-permute-start(f32[4,128]{1,0:T(4,128)S(1)} %pad_maximum_fusion.5), channel_id=1, source_target_pairs={{0,1},{1,0},{2,3},{3,2},{4,5},{5,4},{6,7},{7,6},{8,9},{9,8},{10,11... | collective-permute-start | bytes 6152 | tf_op jit(solution)/shard_map/ppermute | solution.py:390
  113.3 1.0 collective-permute-done.7
  114.3 15.6 %all_to_all.36 = f32[16,6,128]{2,1,0:T(8,128)S(1)} all-to-all(f32[16,6,128]{2,1,0:T(8,128)S(1)} %broadcast_in_dim.28), channel_id=1, replica_groups=mesh['chip'=8,'core'=2,'z'=8,'yhi'=4] {'chip','core'}, dimensions={0} | all-to-all | bytes 98304 | tf_op jit(solution)/shard_map/all_to_all | solution.py:22
  129.9 0.1 multiply_convert_fusion
  130.0 0.8 multiply_reduce_fusion
  130.9 0.1 fusion.17
  131.0 0.8 broadcast_in_dim.31
  131.8 5.4 %all-to-all-start.5 = ((bf16[4,480,128]{2,1,0:T(8,128)(2,1)}), bf16[4,480,128]{2,1,0:T(8,128)(2,1)S(1)}, u32[]{:S(2)}, u32[]{:S(2)}) async-start(bf16[4,480,128]{2,1,0:T(8,128)(2,1)} %broadcast_in_dim.31), calls=%async_computation.5 | async-start | bytes 983040 | tf_op jit(solution)/shard_map/all_to_all | solution.py:22
  137.3 8.2 %collective-permute-start.8 = (bf16[224,128]{1,0:T(8,128)(2,1)S(1)}, bf16[224,128]{1,0:T(8,128)(2,1)S(1)}, u32[]{:S(2)}, u32[]{:S(2)}) collective-permute-start(bf16[224,128]{1,0:T(8,128)(2,1)S(1)} %get-tuple-element.43), channel_id=1, source_target_pairs={{0,0},{1,1},{2,32},{3,33},{4,64},{5,65},{6,96},{7,97},{8,128},{9,1... | collective-permute-start | bytes 172040 | tf_op jit(solution)/shard_map/ppermute | solution.py:437
  145.4 7.8 %collective-permute-done.8 = bf16[224,128]{1,0:T(8,128)(2,1)S(1)} collective-permute-done((bf16[224,128]{1,0:T(8,128)(2,1)S(1)}, bf16[224,128]{1,0:T(8,128)(2,1)S(1)}, u32[]{:S(2)}, u32[]{:S(2)}) %collective-permute-start.8) | collective-permute-done | bytes 57376 | tf_op jit(solution)/shard_map/ppermute | solution.py:437
  153.2 3.3 %shard_map.130 = (bf16[8,224,128]{2,1,0:T(8,128)(2,1)S(1)}, bf16[8,224,128]{2,1,0:T(8,128)(2,1)}, bf16[8,176,448]{2,1,0:T(8,128)(2,1)}) custom-call(s32[2]{0:T(128)S(1)} %pad_add_fusion.1.place_ref, bf16[8,112,448]{2,1,0:T(8,128)(2,1)S(1)} %all-to-all-done.weights_ref, bf16[8,240,128]{2,1,0:T(8,128)(2,1)S(1)} %all_to_all.35.own_ref, ...), custom_call_target="tpu_custom_call" | custom-call | flops 822083584 | bytes 4063232 | tf_op jit(solution)/shard_map/pallas_call | solution.py:233
  156.5 1.9 collective-permute-start.9
  158.5 2.0 collective-permute-done.9
  160.4 0.1 add_convert_fusion
  160.7 21.4 %all_to_all.37 = bf16[8,448,128]{2,1,0:T(8,128)(2,1)S(1)} all-to-all(bf16[8,448,128]{2,1,0:T(8,128)(2,1)S(1)} %pad_maximum_fusion), channel_id=1, replica_groups=mesh['chip'=8,'core'=2,'z'=8,'yhi'=4] {'chip'}, dimensions={0} | all-to-all | bytes 1835008 | tf_op jit(solution)/shard_map/all_to_all | solution.py:443
  182.1 3.5 %collective-permute-start.12 = (bf16[8,224,128]{2,1,0:T(8,128)(2,1)S(1)}, bf16[8,224,128]{2,1,0:T(8,128)(2,1)S(1)}, u32[]{:S(2)}, u32[]{:S(2)}) collective-permute-start(bf16[8,224,128]{2,1,0:T(8,128)(2,1)S(1)} %get-tuple-element.40.own_ref), channel_id=1, source_target_pairs={{0,32},{32,0},{1,33},{33,1},{2,34},{34,2},{3,35},{35,3},{4,36},{36... | collective-permute-start | bytes 1376264 | tf_op jit(solution)/shard_map/ppermute | solution.py:341
  185.7 1.9 collective-permute-start.11
  187.6 6.0 %collective-permute-start.10 = (bf16[112,128]{1,0:T(8,128)(2,1)S(1)}, bf16[112,128]{1,0:T(8,128)(2,1)S(1)}, u32[]{:S(2)}, u32[]{:S(2)}) collective-permute-start(bf16[112,128]{1,0:T(8,128)(2,1)S(1)} %get-tuple-element.49), channel_id=1, source_target_pairs={{0,0},{1,1},{32,2},{33,3},{4,4},{5,5},{36,6},{37,7},{8,8},{9,9},{4... | collective-permute-start | bytes 86024 | tf_op jit(solution)/shard_map/ppermute | solution.py:453
  193.6 5.7 %shard_map.131 = (f32[112,4096]{1,0:T(8,128)}, f32[8,128]{1,0:T(8,128)S(1)}) custom-call(s32[16,1,256]{2,1,0:T(1,128)S(1)} %pad_add_fusion.ids_ref, bf16[8,224,128]{2,1,0:T(8,128)(2,1)S(1)} %get-tuple-element.40.own_ref, bf16[8,224,128]{2,1,0:T(8,128)(2,1)S(1)} %collective-permute-done.12.other_ref), custom_call_target="tpu_custom_call" | custom-call | tf_op jit(solution)/shard_map/pallas_call | solution.py:118
  199.3 0.6 copy-done
  200.0 0.6 copy-done.4
  200.5 1.7 shard_map.132
  (68 shorter events, 1.2 us)
Async XLA Ops:
  7.2 12.9 %copy-start.8 = (s32[128]{0:T(128)S(1)}, s32[128]{0:T(128)}, u32[]{:S(2)}) copy-start(s32[128]{0:T(128)} %param.8) | copy-start | bytes 1540
  7.2 23.2 %copy-start.3 = (bf16[128,224]{0,1:T(8,128)(2,1)S(1)}, bf16[128,224]{0,1:T(8,128)(2,1)}, u32[]{:S(2)}) copy-start(bf16[128,224]{0,1:T(8,128)(2,1)} %param.15) | copy-start | bytes 172036
  9.2 37.2 %all-to-all-start = ((bf16[8,112,448]{2,1,0:T(8,128)(2,1)}), bf16[8,112,448]{2,1,0:T(8,128)(2,1)S(1)}, u32[]{:S(2)}, u32[]{:S(2)}) async-start(bf16[8,112,448]{2,1,0:T(8,128)(2,1)} %broadcast_in_dim.22), calls=%async_computation | async-start | bytes 1835008 | tf_op jit(solution)/shard_map/all_to_all | solution.py:22
  20.1 18.2 %collective-permute-start.3 = (bf16[2,128]{1,0:T(2,128)(2,1)S(1)}, bf16[2,128]{1,0:T(2,128)(2,1)S(1)}, u32[]{:S(2)}, u32[]{:S(2)}) collective-permute-start(bf16[2,128]{1,0:T(2,128)(2,1)S(1)} %pad_maximum_fusion.7), channel_id=1, source_target_pairs={{0,0},{1,1},{2,32},{3,33},{4,64},{5,65},{6,96},{7,97},{8,128},{9,1... | collective-permute-start | bytes 1544 | tf_op jit(solution)/shard_map/ppermute | solution.py:348
  28.4 9.9 %collective-permute-start.2 = (bf16[2,128]{1,0:T(2,128)(2,1)S(1)}, bf16[2,128]{1,0:T(2,128)(2,1)S(1)}, u32[]{:S(2)}, u32[]{:S(2)}) collective-permute-start(bf16[2,128]{1,0:T(2,128)(2,1)S(1)} %pad_maximum_fusion.7), channel_id=1, source_target_pairs={{0,1},{1,0},{2,33},{3,32},{4,65},{5,64},{6,97},{7,96},{8,129},{9,1... | collective-permute-start | bytes 1544 | tf_op jit(solution)/shard_map/ppermute | solution.py:348
  30.4 8.0 %collective-permute-start = (bf16[112,128]{1,0:T(8,128)(2,1)S(1)}, bf16[112,128]{1,0:T(8,128)(2,1)S(1)}, u32[]{:S(2)}, u32[]{:S(2)}) collective-permute-start(bf16[112,128]{1,0:T(8,128)(2,1)S(1)} %get-tuple-element.54), channel_id=1, source_target_pairs={{0,1},{1,0},{2,33},{3,32},{4,5},{5,4},{6,37},{7,36},{8,9},{9,8},{1... | collective-permute-start | bytes 86024 | tf_op jit(solution)/shard_map/ppermute | solution.py:353
  36.1 9.5 %collective-permute-start.1 = (bf16[112,128]{1,0:T(8,128)(2,1)S(1)}, bf16[112,128]{1,0:T(8,128)(2,1)S(1)}, u32[]{:S(2)}, u32[]{:S(2)}) collective-permute-start(bf16[112,128]{1,0:T(8,128)(2,1)S(1)} %get-tuple-element.55), channel_id=1, source_target_pairs={{0,0},{1,1},{2,32},{3,33},{4,4},{5,5},{6,36},{7,37},{8,8},{9,9},{1... | collective-permute-start | bytes 86024 | tf_op jit(solution)/shard_map/ppermute | solution.py:352
  62.6 3.7 %collective-permute-start.4 = (bf16[8,240,128]{2,1,0:T(8,128)(2,1)S(1)}, bf16[8,240,128]{2,1,0:T(8,128)(2,1)S(1)}, u32[]{:S(2)}, u32[]{:S(2)}) collective-permute-start(bf16[8,240,128]{2,1,0:T(8,128)(2,1)S(1)} %all_to_all.35.own_ref), channel_id=1, source_target_pairs={{0,32},{32,0},{1,33},{33,1},{2,34},{34,2},{3,35},{35,3},{4,36},{36... | collective-permute-start | bytes 1474568 | tf_op jit(solution)/shard_map/ppermute | solution.py:341
  65.9 87.3 %copy-start.1 = (s32[2]{0:T(128)}, s32[2]{0:T(128)S(1)}, u32[]{:S(2)}) copy-start(s32[2]{0:T(128)S(1)} %pad_add_fusion.1.place_ref) | copy-start | bytes 28
  68.7 18.2 %all-to-all-start.2 = ((bf16[4,448,128]{2,1,0:T(8,128)(2,1)}), bf16[4,448,128]{2,1,0:T(8,128)(2,1)S(1)}, u32[]{:S(2)}, u32[]{:S(2)}) async-start(bf16[4,448,128]{2,1,0:T(8,128)(2,1)} %shard_map.129), calls=%async_computation.2 | async-start | bytes 917504 | tf_op jit(solution)/shard_map/all_to_all | solution.py:369
  76.1 5.0 %collective-permute-start.5 = (bf16[8,112,256]{2,1,0:T(8,128)(2,1)S(1)}, bf16[8,112,256]{2,1,0:T(8,128)(2,1)S(1)}, u32[]{:S(2)}, u32[]{:S(2)}) collective-permute-start(bf16[8,112,256]{2,1,0:T(8,128)(2,1)S(1)} %shard_map.128), channel_id=1, source_target_pairs={{0,32},{32,0},{1,33},{33,1},{2,34},{34,2},{3,35},{35,3},{4,36},{36... | collective-permute-start | bytes 1376264 | tf_op jit(solution)/shard_map/ppermute | solution.py:341
  81.1 9.3 %copy-start.7 = (f32[224]{0:T(256)S(1)}, f32[224]{0:T(256)}, u32[]{:S(2)}) copy-start(f32[224]{0:T(256)} %param.11) | copy-start | bytes 2692
  81.1 26.4 %copy-start.2 = (bf16[128,224]{0,1:T(8,128)(2,1)S(1)}, bf16[128,224]{0,1:T(8,128)(2,1)}, u32[]{:S(2)}) copy-start(bf16[128,224]{0,1:T(8,128)(2,1)} %param.9) | copy-start | bytes 172036
  81.1 26.4 %copy-start.6 = (f32[224]{0:T(256)S(1)}, f32[224]{0:T(256)}, u32[]{:S(2)}) copy-start(f32[224]{0:T(256)} %param.12) | copy-start | bytes 2692
  86.9 10.3 %all-to-all-start.3 = ((bf16[8,112,256]{2,1,0:T(8,128)(2,1)}), bf16[8,112,256]{2,1,0:T(8,128)(2,1)S(1)}, u32[]{:S(2)}, u32[]{:S(2)}) async-start(bf16[8,112,256]{2,1,0:T(8,128)(2,1)} %add.61), calls=%async_computation.3 | async-start | bytes 917504 | tf_op jit(solution)/shard_map/all_to_all | solution.py:373
  97.3 10.1 %collective-permute-start.6 = (bf16[224,128]{1,0:T(8,128)(2,1)S(1)}, bf16[224,128]{1,0:T(8,128)(2,1)S(1)}, u32[]{:S(2)}, u32[]{:S(2)}) collective-permute-start(bf16[224,128]{1,0:T(8,128)(2,1)S(1)} %pad_maximum_fusion.3), channel_id=1, source_target_pairs={{0,0},{1,1},{2,32},{3,33},{4,64},{5,65},{6,96},{7,97},{8,128},{9,1... | collective-permute-start | bytes 172040 | tf_op jit(solution)/shard_map/ppermute | solution.py:376
  107.6 6.6 %collective-permute-start.7 = (f32[4,128]{1,0:T(4,128)S(1)}, f32[4,128]{1,0:T(4,128)S(1)}, u32[]{:S(2)}, u32[]{:S(2)}) collective-permute-start(f32[4,128]{1,0:T(4,128)S(1)} %pad_maximum_fusion.5), channel_id=1, source_target_pairs={{0,1},{1,0},{2,3},{3,2},{4,5},{5,4},{6,7},{7,6},{8,9},{9,8},{10,11... | collective-permute-start | bytes 6152 | tf_op jit(solution)/shard_map/ppermute | solution.py:390
  131.8 21.4 %all-to-all-start.5 = ((bf16[4,480,128]{2,1,0:T(8,128)(2,1)}), bf16[4,480,128]{2,1,0:T(8,128)(2,1)S(1)}, u32[]{:S(2)}, u32[]{:S(2)}) async-start(bf16[4,480,128]{2,1,0:T(8,128)(2,1)} %broadcast_in_dim.31), calls=%async_computation.5 | async-start | bytes 983040 | tf_op jit(solution)/shard_map/all_to_all | solution.py:22
  137.3 62.7 %reduce-scatter.2.cloned.1.call-start = ((), (), s32[]{:S(2)}) async-start(), calls=%async_computation.8 | async-start | bytes 1622016 | tf_op jit(solution)/shard_map/reduce_scatter | solution.py:455
  137.3 15.9 %collective-permute-start.8 = (bf16[224,128]{1,0:T(8,128)(2,1)S(1)}, bf16[224,128]{1,0:T(8,128)(2,1)S(1)}, u32[]{:S(2)}, u32[]{:S(2)}) collective-permute-start(bf16[224,128]{1,0:T(8,128)(2,1)S(1)} %get-tuple-element.43), channel_id=1, source_target_pairs={{0,0},{1,1},{2,32},{3,33},{4,64},{5,65},{6,96},{7,97},{8,128},{9,1... | collective-permute-start | bytes 172040 | tf_op jit(solution)/shard_map/ppermute | solution.py:437
  156.5 3.9 %collective-permute-start.9 = (bf16[8,224,128]{2,1,0:T(8,128)(2,1)}, bf16[8,224,128]{2,1,0:T(8,128)(2,1)S(1)}, u32[]{:S(2)}, u32[]{:S(2)}) collective-permute-start(bf16[8,224,128]{2,1,0:T(8,128)(2,1)} %get-tuple-element.28), channel_id=1, source_target_pairs={{0,32},{32,0},{1,33},{33,1},{2,34},{34,2},{3,35},{35,3},{4,36},{36... | collective-permute-start | bytes 1376264 | tf_op jit(solution)/shard_map/ppermute | solution.py:341
  182.1 11.5 %collective-permute-start.12 = (bf16[8,224,128]{2,1,0:T(8,128)(2,1)S(1)}, bf16[8,224,128]{2,1,0:T(8,128)(2,1)S(1)}, u32[]{:S(2)}, u32[]{:S(2)}) collective-permute-start(bf16[8,224,128]{2,1,0:T(8,128)(2,1)S(1)} %get-tuple-element.40.own_ref), channel_id=1, source_target_pairs={{0,32},{32,0},{1,33},{33,1},{2,34},{34,2},{3,35},{35,3},{4,36},{36... | collective-permute-start | bytes 1376264 | tf_op jit(solution)/shard_map/ppermute | solution.py:341
  185.7 14.2 %collective-permute-start.11 = (bf16[112,128]{1,0:T(8,128)(2,1)S(1)}, bf16[112,128]{1,0:T(8,128)(2,1)S(1)}, u32[]{:S(2)}, u32[]{:S(2)}) collective-permute-start(bf16[112,128]{1,0:T(8,128)(2,1)S(1)} %get-tuple-element.48), channel_id=1, source_target_pairs={{1,0},{0,1},{33,2},{32,3},{5,4},{4,5},{37,6},{36,7},{9,8},{8,9},{4... | collective-permute-start | bytes 86024 | tf_op jit(solution)/shard_map/ppermute | solution.py:454
  187.6 12.3 %collective-permute-start.10 = (bf16[112,128]{1,0:T(8,128)(2,1)S(1)}, bf16[112,128]{1,0:T(8,128)(2,1)S(1)}, u32[]{:S(2)}, u32[]{:S(2)}) collective-permute-start(bf16[112,128]{1,0:T(8,128)(2,1)S(1)} %get-tuple-element.49), channel_id=1, source_target_pairs={{0,0},{1,1},{32,2},{33,3},{4,4},{5,5},{36,6},{37,7},{8,8},{9,9},{4... | collective-permute-start | bytes 86024 | tf_op jit(solution)/shard_map/ppermute | solution.py:453
  199.3 0.6 copy-start
  199.9 0.6 copy-start.4
  199.9 0.6 copy-start.5
Sparse Core Ops, SparseCore 0:
  158.6 36.4 reduce-scatter.1
